TPU v7x, 128 devices: a whole 4x4x4 slice. The times are simulated.
128 devices in a mesh: pair: 32 (over z, x, y_hi), row: 4 (over y_lo, core).
Axes of the slice: x: 4, y: 4 (y_hi: 2, y_lo: 2; y = y_hi * 2 + y_lo), z: 4, core: 2. Of those that a mesh axis runs over, the one named last changes fastest.
Arguments:
- samples_slab: float32 [4, 8192, 8192], P('row', 'pair'), may hold values from -420 to 420
- block_order: int32 [128], replicated, may hold values from 0 to 127, each once
- rotations: float32 [3, 64, 128, 128], P(None, 'pair'), may hold values from -0.5 to 0.5
Outputs:
- rotated_slab: float32 [8192, 32768], P('pair', 'row')
- pair_grams: float32 [3, 64, 128, 128], P(None, 'pair')
Inputs may be any that keep to these rules, and one draw needn't show every extreme that they name: `block_order`: each block number appears once.
All inputs are finite; a program needn't handle non-finite values.
Results may differ from a plain program's by a relative error of at most 0.0003.
Values sent between devices are 32-bit elements; how exact they have to be, the bound alone decides.
No kernel may reach another device: no remote copies, remote signals or barrier semaphores. Data moves between devices by JAX's collectives and lax.ppermute only.
A program may use at most 192 MiB of HBM per device.

v0:
```python
import jax
import jax.numpy as jnp
from jax import lax
from jax.sharding import PartitionSpec as P

epsilon = 1e-06


def from_behind(value, axis, steps):
    count = lax.axis_size(axis)
    leading, last = (max(0, -steps), min(count, count - steps))
    return lax.ppermute(value, axis, [(source, source + steps) for source in range(leading, last)])


def sandwich(mixing, gram_sum):
    inner = jnp.einsum("kce,kef->kcf", gram_sum, mixing, precision=lax.Precision.HIGHEST)
    return jnp.einsum("kcd,kcf->kdf", mixing, inner, precision=lax.Precision.HIGHEST)


def assemble(
    upper_blocks, lower_blocks, upper_chain, incoming_upper, incoming_lower, at_start, at_end
):
    first_upper = jnp.where(at_start, upper_blocks[0], incoming_upper)
    new_upper = jnp.concatenate([first_upper[None], upper_chain[:-1]], 0)
    last_lower = jnp.where(at_end, upper_blocks[-1], incoming_lower)
    new_lower = jnp.concatenate([lower_blocks[1:], last_lower[None]], 0)
    return jnp.stack([new_upper, new_lower], 1)


def upper_sequence(upper_blocks, lower_blocks, at_start):
    head = jnp.where(at_start, lower_blocks[0], upper_blocks[0])
    return jnp.concatenate([head[None], upper_blocks[1:]], 0)


def advance(columns_held, at_start, at_end):
    upper_blocks = columns_held[:, 0]
    lower_blocks = columns_held[:, 1]
    upper_chain = upper_sequence(upper_blocks, lower_blocks, at_start)
    incoming_upper = from_behind(upper_chain[-1], "pair", 1)
    incoming_lower = from_behind(lower_blocks[0], "pair", -1)
    return assemble(
        upper_blocks, lower_blocks, upper_chain, incoming_upper, incoming_lower, at_start, at_end
    )


def transform(pair_cols, diagonal_sum, rotation, total_rows):
    inverse_norm = lax.rsqrt(diagonal_sum / total_rows + epsilon)
    mixing = rotation * inverse_norm[:, :, None]
    mixed_cols = jnp.einsum("kcd,kcr->kdr", mixing, pair_cols, precision=lax.Precision.HIGHEST)
    return (mixed_cols, mixing)


def body(samples_slab, block_order, rotations):
    rows_dev = samples_slab.shape[1]
    ncolumns = samples_slab.shape[2]
    block_count = block_order.shape[0]
    block_width = ncolumns // block_count
    step_count = rotations.shape[0]
    pairs_here = rotations.shape[1]
    pair_width = rotations.shape[2]
    transposed = samples_slab[0].T.reshape(block_count, block_width, rows_dev)
    arranged = jnp.take(transposed, block_order, axis=0)
    columns_held = lax.all_to_all(arranged, "pair", split_axis=0, concat_axis=2, tiled=True)
    sample_count = columns_held.shape[2]
    total_rows = sample_count * lax.axis_size("row")
    columns_held = columns_held.reshape(pairs_here, 2, block_width, sample_count)
    at_start = lax.axis_index("pair") == 0
    at_end = lax.axis_index("pair") == lax.axis_size("pair") - 1
    results = []
    for turn_index in range(step_count):
        pair_cols = columns_held.reshape(pairs_here, pair_width, sample_count)
        partial_value = jnp.einsum(
            "kcr,kdr->kcd", pair_cols, pair_cols, precision=lax.Precision.HIGHEST
        )
        gram_sum = lax.psum(partial_value, "row")
        diagonal_sum = jnp.diagonal(gram_sum, axis1=1, axis2=2)
        mixed_cols, mixing = transform(pair_cols, diagonal_sum, rotations[turn_index], total_rows)
        results.append(sandwich(mixing, gram_sum) / total_rows)
        columns_held = mixed_cols.reshape(pairs_here, 2, block_width, sample_count)
        if turn_index + 1 < step_count:
            columns_held = advance(columns_held, at_start, at_end)
    pair_grams = jnp.stack(results)
    rotated_slab = columns_held.reshape(2 * pairs_here * block_width, sample_count)
    return (rotated_slab, pair_grams)


def solution(mesh):
    in_specs = (P("row", "pair", None), P(), P(None, "pair", None, None))
    out_specs = (P("pair", "row"), P(None, "pair", None, None))
    return jax.shard_map(body, mesh=mesh, in_specs=in_specs, out_specs=out_specs, check_vma=False)
```

profile of v0, /device:TPU:2, one launch (start us, length us, event | category | flops | bytes accessed | tf_op | source)
XLA Modules:
  0.0 567.8 jit_solution(15163340502153301424)
XLA Ops:
  8.5 9.0 %copy.35 = f32[1,256,8192]{1,2,0:T(8,128)} copy(f32[1,256,8192]{2,1,0:T(8,128)} %param.3) | data formatting | bytes 16777216 | tf_op args[0]
  17.5 7.7 %gather_fusion = f32[128,64,256]{2,1,0:T(8,128)} fusion(f32[128,64,256]{2,1,0:T(8,128)} %bitcast.108, s32[1024]{0:T(1024)S(1)} %pad_clamp_fusion), kind=kCustom, calls=%fused_computation | custom fusion | bytes 16777728 | tf_op jit(solution)/shard_map/jit(_take)/gather | solution.py:62
  25.2 4.0 broadcast_select_fusion
  29.2 107.7 %all_to_all.15 = f32[128,64,256]{2,1,0:T(8,128)S(1)} all-to-all(f32[128,64,256]{2,1,0:T(8,128)S(1)} %broadcast_select_fusion), channel_id=1, replica_groups=mesh['pair'=32,'row'=4] {'pair'}, dimensions={0} | all-to-all | bytes 16777216 | tf_op jit(solution)/shard_map/all_to_all | solution.py:63
  136.9 8.3 %copy.36 = f32[4,64,32,256]{3,2,1,0:T(8,128)} copy(f32[4,64,32,256]{3,1,0,2:T(8,128)S(1)} %bitcast.109) | data formatting | bytes 16777216 | tf_op jit(solution)/shard_map/all_to_all | solution.py:63
  145.2 9.4 %reshape_reshape.6 = f32[2,128,8192]{2,1,0:T(8,128)} reshape(f32[4,64,32,256]{3,2,1,0:T(8,128)} %copy.36) | data formatting | bytes 16777216 | tf_op jit(solution)/shard_map/reshape;reshape | solution.py:71
  154.6 12.0 %fusion.20 = f32[2,128,128]{2,1,0:T(8,128)} fusion(f32[2,128,8192]{2,1,0:T(8,128)} %reshape_reshape.6), kind=kOutput, calls=%fused_computation.57 | convolution fusion | flops 3221225472 | bytes 8519680 | tf_op jit(solution)/shard_map/kcr,kdr->kcd/dot_general | solution.py:72
  166.9 32.1 %all-reduce.4.cloned.1.call-done = f32[2,128,128]{2,1,0:T(8,128)} async-done(((f32[2,128,128]{2,1,0:T(8,128)}), f32[2,128,128]{2,1,0:T(8,128)}) %all-reduce.4.cloned.1.call-update) | async-done | bytes 131088 | tf_op jit(solution)/shard_map/psum | solution.py:75
  199.0 5.5 copy.37
  206.4 10.4 %fusion.10 = f32[2,128,8192]{2,1,0:T(8,128)S(1)} fusion(f32[2,128,8192]{2,1,0:T(8,128)} %reshape_reshape.6, f32[3,2,128,128]{3,2,1,0:T(8,128)S(1)} %copy-done.4, f32[2,128]{1,0:T(2,128)S(1)} %bitcast.111), kind=kOutput, calls=%fused_computation.40 | convolution fusion | flops 3221258240 | bytes 16909312 | tf_op jit(solution)/shard_map/kcd,kcr->kdr/dot_general | solution.py:49
  222.1 4.6 collective-permute-start
  230.3 87.0 %collective-permute-done = f32[64,8192]{1,0:T(8,128)} collective-permute-done((f32[64,8192]{1,0:T(8,128)}, f32[64,8192]{1,0:T(8,128)}, u32[]{:S(2)}, u32[]{:S(2)}) %collective-permute-start) | collective-permute-done | bytes 2097184 | tf_op jit(solution)/shard_map/ppermute | solution.py:12
  319.5 3.9 fusion.1
  329.4 8.3 %fusion.21 = f32[2,128,128]{2,1,0:T(8,128)} fusion(f32[2,128,8192]{2,1,0:T(8,128)S(1)} %bitcast.102), kind=kOutput, calls=%fused_computation.58 | convolution fusion | flops 3221225472 | bytes 8519680 | tf_op jit(solution)/shard_map/kcr,kdr->kcd/dot_general | solution.py:72
  338.0 35.6 %all-reduce.6.cloned.1.call-done = f32[2,128,128]{2,1,0:T(8,128)} async-done(((f32[2,128,128]{2,1,0:T(8,128)}), f32[2,128,128]{2,1,0:T(8,128)}) %all-reduce.6.cloned.1.call-update) | async-done | bytes 131088 | tf_op jit(solution)/shard_map/psum | solution.py:75
  373.6 5.5 copy.41
  381.0 10.4 %fusion.8 = f32[2,128,8192]{2,1,0:T(8,128)S(1)} fusion(f32[2,128,8192]{2,1,0:T(8,128)} %bitcast.103, f32[3,2,128,128]{3,2,1,0:T(8,128)S(1)} %copy-done.4, f32[2,128]{1,0:T(2,128)S(1)} %bitcast.114), kind=kOutput, calls=%fused_computation.38 | convolution fusion | flops 3221258240 | bytes 16909312 | tf_op jit(solution)/shard_map/kcd,kcr->kdr/dot_general | solution.py:49
  392.3 4.6 collective-permute-start.2
  396.9 4.0 collective-permute-start.3
  401.8 85.5 %collective-permute-done.2 = f32[64,8192]{1,0:T(8,128)S(1)} collective-permute-done((f32[64,8192]{1,0:T(8,128)S(1)}, f32[64,8192]{1,0:T(8,128)S(1)}, u32[]{:S(2)}, u32[]{:S(2)}) %collective-permute-start.2) | collective-permute-done | bytes 2097184 | tf_op jit(solution)/shard_map/ppermute | solution.py:12
  495.8 8.3 %fusion.22 = f32[2,128,128]{2,1,0:T(8,128)} fusion(f32[2,128,8192]{2,1,0:T(8,128)S(1)} %bitcast.100), kind=kOutput, calls=%fused_computation.59 | convolution fusion | flops 3221225472 | bytes 8519680 | tf_op jit(solution)/shard_map/kcr,kdr->kcd/dot_general | solution.py:72
  505.0 35.0 %all-reduce.8.cloned.1.call-done = f32[2,128,128]{2,1,0:T(8,128)} async-done(((f32[2,128,128]{2,1,0:T(8,128)}), f32[2,128,128]{2,1,0:T(8,128)}) %all-reduce.8.cloned.1.call-update) | async-done | bytes 131088 | tf_op jit(solution)/shard_map/psum | solution.py:75
  540.0 5.6 copy.45
  547.6 11.9 %fusion.6 = f32[2,128,8192]{2,1,0:T(8,128)} fusion(f32[2,128,8192]{2,1,0:T(8,128)} %bitcast.101, f32[3,2,128,128]{3,2,1,0:T(8,128)S(1)} %copy-done.4, f32[2,128]{1,0:T(2,128)S(1)} %bitcast.117), kind=kOutput, calls=%fused_computation.36 | convolution fusion | flops 3221258240 | bytes 16909312 | tf_op jit(solution)/shard_map/kcd,kcr->kdr/dot_general | solution.py:49
  (55 shorter events, 37.2 us)
Async XLA Ops:
  7.2 191.8 %all-reduce.4.cloned.1.call-start = ((), (), s32[]{:S(2)}) async-start(), calls=%async_computation.1 | async-start | bytes 262144 | tf_op jit(solution)/shard_map/psum | solution.py:75
  166.6 207.0 %all-reduce.6.cloned.1.call-start = ((), (), s32[]{:S(2)}) async-start(), calls=%async_computation.2 | async-start | bytes 262144 | tf_op jit(solution)/shard_map/psum | solution.py:75
  166.8 39.6 %copy-start.4 = (f32[3,2,128,128]{3,2,1,0:T(8,128)S(1)}, f32[3,2,128,128]{3,2,1,0:T(8,128)}, u32[]{:S(2)}) copy-start(f32[3,2,128,128]{3,2,1,0:T(8,128)} %param.5) | copy-start | bytes 1179652
  216.8 5.3 copy-start.2
  222.1 95.2 %collective-permute-start = (f32[64,8192]{1,0:T(8,128)}, f32[64,8192]{1,0:T(8,128)}, u32[]{:S(2)}, u32[]{:S(2)}) collective-permute-start(f32[64,8192]{1,0:T(8,128)} %get-tuple-element.10), channel_id=1, source_target_pairs={{0,4},{4,8},{8,12},{12,16},{16,20},{20,24},{24,28},{28,32},{32,36}... | collective-permute-start | bytes 6291464 | tf_op jit(solution)/shard_map/ppermute | solution.py:12
  226.7 92.8 %collective-permute-start.1 = (f32[64,8192]{1,0:T(8,128)}, f32[64,8192]{1,0:T(8,128)}, u32[]{:S(2)}, u32[]{:S(2)}) collective-permute-start(f32[64,8192]{1,0:T(8,128)} %get-tuple-element.11), channel_id=1, source_target_pairs={{4,0},{8,4},{12,8},{16,12},{20,16},{24,20},{28,24},{32,28},{36,32}... | collective-permute-start | bytes 6291464 | tf_op jit(solution)/shard_map/ppermute | solution.py:12
  230.3 93.1 %copy-start.3 = (f32[1,64,8192]{2,1,0:T(8,128)S(1)}, f32[1,64,8192]{2,1,0:T(8,128)}, u32[]{:S(2)}) copy-start(f32[1,64,8192]{2,1,0:T(8,128)} %get-tuple-element.13) | copy-start | bytes 6291460
  326.0 3.4 copy-start.1
  337.8 202.2 %all-reduce.8.cloned.1.call-start = ((), (), s32[]{:S(2)}) async-start(), calls=%async_computation.3 | async-start | bytes 262144 | tf_op jit(solution)/shard_map/psum | solution.py:75
  391.4 9.6 %copy-start.5 = (f32[2,128,128]{2,1,0:T(8,128)S(1)}, f32[2,128,128]{2,1,0:T(8,128)}, u32[]{:S(2)}) copy-start(f32[2,128,128]{2,1,0:T(8,128)} %all-reduce.4.cloned.1.call-done) | copy-start | bytes 393220
  392.3 94.9 %collective-permute-start.2 = (f32[64,8192]{1,0:T(8,128)S(1)}, f32[64,8192]{1,0:T(8,128)S(1)}, u32[]{:S(2)}, u32[]{:S(2)}) collective-permute-start(f32[64,8192]{1,0:T(8,128)S(1)} %get-tuple-element.4), channel_id=1, source_target_pairs={{0,4},{4,8},{8,12},{12,16},{16,20},{20,24},{24,28},{28,32},{32,36}... | collective-permute-start | bytes 6291464 | tf_op jit(solution)/shard_map/ppermute | solution.py:12
  396.9 92.5 %collective-permute-start.3 = (f32[64,8192]{1,0:T(8,128)S(1)}, f32[64,8192]{1,0:T(8,128)S(1)}, u32[]{:S(2)}, u32[]{:S(2)}) collective-permute-start(f32[64,8192]{1,0:T(8,128)S(1)} %get-tuple-element.5), channel_id=1, source_target_pairs={{4,0},{8,4},{12,8},{16,12},{20,16},{24,20},{28,24},{32,28},{36,32}... | collective-permute-start | bytes 6291464 | tf_op jit(solution)/shard_map/ppermute | solution.py:12
  492.5 3.2 copy-start
  495.8 8.4 %copy-start.6 = (f32[2,128,128]{2,1,0:T(8,128)S(1)}, f32[2,128,128]{2,1,0:T(8,128)}, u32[]{:S(2)}) copy-start(f32[2,128,128]{2,1,0:T(8,128)} %all-reduce.6.cloned.1.call-done) | copy-start | bytes 393220
  547.6 11.9 %copy-start.7 = (f32[2,128,128]{2,1,0:T(8,128)S(1)}, f32[2,128,128]{2,1,0:T(8,128)}, u32[]{:S(2)}) copy-start(f32[2,128,128]{2,1,0:T(8,128)} %all-reduce.8.cloned.1.call-done) | copy-start | bytes 393220
Sparse Core Ops, SparseCore 0:
  166.7 32.2 all-reduce.3
  337.9 35.6 all-reduce.5
  504.3 35.6 all-reduce.7
where the time goes:
time: 578 us; the launch traced here: 568 us
  waiting for transfers between devices  280 us (48%)
  blocking collectives  108 us (19%)
  local copies, waits for them, and re-layouts  67.1 us (12%)
  matrix products  63.7 us (11%)
  other arithmetic  18.1 us (3%)
  starting transfers between devices  17.4 us (3%)
  between operations  14.2 us (2%)
    ppermute x4, waiting for transfers between devices, from_behind(): lax.ppermute(value, axis, [(source, source + steps) for source in range(l...  177 us
    all_to_all x1, blocking collectives, body(): lax.all_to_all(arranged, 'pair', split_axis=0, concat_axis=2, tiled=True)  108 us
    psum x3, waiting for transfers between devices, body(): gram_sum = lax.psum(partial_value, 'row')  103 us
    dot_general x3, matrix products, transform(): jnp.einsum('kcd,kcr->kdr', mixing, pair_cols, precision=lax.Precision.HIG...  32.6 us
    dot_general x3, matrix products, body(): jnp.einsum('kcr,kdr->kcd', pair_cols, pair_cols, precision=lax.Precision....  28.7 us
    unnamed x20, local copies, waits for them, and re-layouts  17.8 us
    ppermute x4, starting transfers between devices, from_behind(): lax.ppermute(value, axis, [(source, source + steps) for source in range(l...  16.9 us
    psum x3, local copies, waits for them, and re-layouts, body(): gram_sum = lax.psum(partial_value, 'row')  16.6 us
  transfers between devices with their start and end apart: 7, of which 7 were waited for; matrix products, arithmetic and copies ran while one was open for 0% of the time, Pallas kernels for 0%

commit v1 on v0

v1 whole, which is shorter than its diff:
```python
import functools
import itertools

import jax
import jax.numpy as jnp
from jax import lax
from jax.experimental import pallas as pl
from jax.experimental.pallas import tpu as pltpu
from jax.sharding import PartitionSpec as P


BOTH = ("pair", "row")
NZ, NX, NY, NC = 4, 4, 2, 2
NPAIR = 64
PAIRW = 128
HALF = 64
SAMP = 256
NDEV = 32
ROWS = 32768
EPS = 1e-06
QUARTER = 24
PAYROWS = 256 + QUARTER + 32
MIB = 1 << 20
F32, BF16 = jnp.float32, jnp.bfloat16


def flat(z, x, yh, yl, c):
    return (((z * NX + x) * 2 + yh) * 2 + yl) * 2 + c


def exchange(value, flip):
    pairs = []
    for here in itertools.product(range(NZ), range(NX), range(2), range(2), range(2)):
        there = tuple(a ^ b for a, b in zip(here, flip))
        pairs.append((flat(*here), flat(*there)))
    return lax.ppermute(value, BOTH, pairs)


def sum_all(value):
    for flip in (
        (0, 0, 0, 0, 1),
        (0, 0, 0, 1, 0),
        (0, 0, 1, 1, 0),
        (0, 1, 0, 0, 0),
        (0, 3, 0, 0, 0),
        (1, 0, 0, 0, 0),
        (3, 0, 0, 0, 0),
    ):
        value = value + exchange(value, flip)
    return value


def sum_row(value):
    for flip in ((0, 0, 0, 0, 1), (0, 0, 0, 1, 0)):
        value = value + exchange(value, flip)
    return value


def gather_pairs(own):
    def grow(held, offs, flip, bit):
        return jnp.concatenate([held, exchange(held, flip)], 0), offs + [o ^ bit for o in offs]

    x1, x3, z1, z3 = (0, 1, 0, 0, 0), (0, 3, 0, 0, 0), (1, 0, 0, 0, 0), (3, 0, 0, 0, 0)
    first, first_offs = own, [0]
    second, second_offs = exchange(own, (0, 0, 1, 1, 0)), [2]
    first, first_offs = grow(first, first_offs, x1, 4)
    second, second_offs = grow(second, second_offs, z1, 16)
    first, first_offs = grow(first, first_offs, x3, 12)
    second, second_offs = grow(second, second_offs, z3, 48)
    first, first_offs = grow(first, first_offs, z1, 16)
    second, second_offs = grow(second, second_offs, x1, 4)
    pieces = [first, exchange(first, z3), second, exchange(second, x3)]
    offs = [first_offs, [o ^ 48 for o in first_offs], second_offs, [o ^ 12 for o in second_offs]]
    for k in range(4):
        pieces.append(exchange(pieces[k], (0, 0, 0, 0, 1)))
        offs.append([o ^ 1 for o in offs[k]])
    return pieces, sum(offs, [])


def split(value):
    high = value.astype(BF16)
    return high, (value - high.astype(F32)).astype(BF16)


def left_operand(mixing_t):
    high, low = split(mixing_t)
    return jnp.concatenate(
        [
            jnp.concatenate([high, high], 1),
            jnp.concatenate([low, jnp.zeros_like(low)], 1),
        ],
        0,
    )


def product(left, right):
    wide = jnp.dot(left, right, preferred_element_type=F32)
    return wide[:PAIRW] + wide[PAIRW:]


def outer(a, b):
    return lax.dot_general(a, b, (((1,), (1,)), ((), ())), preferred_element_type=F32)


def self_gram(stacked):
    wide = outer(stacked, stacked)
    return wide[:PAIRW, :PAIRW] + wide[PAIRW:, :PAIRW] + wide[:PAIRW, PAIRW:]


def diagonal_row(gram):
    size = gram.shape[0]
    eye = lax.broadcasted_iota(jnp.int32, (size, size), 0) == lax.broadcasted_iota(
        jnp.int32, (size, size), 1
    )
    return jnp.sum(jnp.where(eye, gram, 0.0), axis=0, keepdims=True)


def scales(norm_row):
    return lax.rsqrt(norm_row / ROWS + EPS)


def lanes(shape):
    return lax.broadcasted_iota(jnp.int32, shape, 1)


def next_slots(i):
    upper = jnp.where(i == 0, 0, jnp.where(i == NPAIR - 1, 2 * NPAIR - 1, 2 * i + 2))
    lower = jnp.where(i == 0, 2, 2 * i - 1)
    return upper, lower


def prepare_kernel(x_ref, norm_ref, high_ref, low_ref):
    tiles = x_ref.shape[1] // PAIRW
    for t in range(tiles):
        tile = x_ref[:, t * PAIRW : (t + 1) * PAIRW]
        norm_ref[t : t + 1, :] = jnp.sum(tile * tile, axis=0, keepdims=True)
        high, low = split(tile.T)
        high_ref[2 * t] = high[:HALF]
        high_ref[2 * t + 1] = high[HALF:]
        low_ref[2 * t] = low[:HALF]
        low_ref[2 * t + 1] = low[HALF:]


def prepare(x):
    width = 1024
    steps = x.shape[1] // width
    blocks = width // HALF
    spec = pl.BlockSpec((blocks, HALF, SAMP), lambda g: (g, 0, 0))
    halves = jax.ShapeDtypeStruct((2 * NPAIR, HALF, SAMP), BF16)
    return pl.pallas_call(
        prepare_kernel,
        grid=(steps,),
        in_specs=[pl.BlockSpec((SAMP, width), lambda g: (0, g))],
        out_specs=[pl.BlockSpec((width // PAIRW, PAIRW), lambda g: (g, 0)), spec, spec],
        out_shape=[jax.ShapeDtypeStruct((NPAIR, PAIRW), F32), halves, halves],
        compiler_params=pltpu.CompilerParams(vmem_limit_bytes=32 * MIB),
        cost_estimate=pl.CostEstimate(flops=8 * MIB, bytes_accessed=16 * MIB, transcendentals=0),
        name="prepare",
    )(x)


def step0_kernel(tab_ref, order_ref, place_ref, norm_ref, high_ref, low_ref, *rest):
    pieces, rest = rest[:8], rest[8:]
    ohigh_ref, olow_ref, keep_ref, send_ref, onorm_ref, rot_ref, norms_ref, sems = rest
    copies = [
        pltpu.make_async_copy(piece, rot_ref.at[pl.ds(8 * k, 8)], sems.at[k])
        for k, piece in enumerate(pieces)
    ]
    for copy in copies:
        copy.start()
    norms_ref[0] = norm_ref[...]
    norms_ref[1] = pltpu.roll(norm_ref[...], HALF, 1)
    core, y_lo = place_ref[0], place_ref[1]
    for copy in copies:
        copy.wait()

    def one(q):
        i = tab_ref[q]
        bu, bl = order_ref[2 * i], order_ref[2 * i + 1]
        nu = norms_ref[bu % 2, pl.ds(bu // 2, 1), :]
        nl = norms_ref[1 - bl % 2, pl.ds(bl // 2, 1), :]
        scale = scales(jnp.where(lanes((1, PAIRW)) < HALF, nu, nl))
        left = left_operand(rot_ref[q] * scale)
        right = jnp.concatenate([high_ref[bu], high_ref[bl], low_ref[bu], low_ref[bl]], 0)
        moved = product(left, right)
        high, low = split(moved)
        su, sl = next_slots(i)
        ohigh_ref[su] = high[:HALF]
        ohigh_ref[sl] = high[HALF:]
        olow_ref[su] = low[:HALF]
        olow_ref[sl] = low[HALF:]
        gram = self_gram(jnp.concatenate([high, low], 0))
        onorm_ref[pl.ds(i, 1), :] = diagonal_row(gram)
        bottom = gram[HALF:]
        packed = jnp.where(
            lanes((32, PAIRW)) >= HALF, bottom[:32], pltpu.roll(bottom[32:], HALF, 1)
        )
        quarters = [
            gram[0:24],
            gram[24:48],
            jnp.concatenate([gram[48:64], packed[0:8]], 0),
            packed[8:32],
        ]
        mine = core == 0
        for yy in range(2):
            even, odd = quarters[2 * yy], quarters[2 * yy + 1]
            keep_ref[yy ^ y_lo, i] = jnp.where(mine, even, odd)
            send_ref[yy ^ y_lo, i] = jnp.where(mine, odd, even)

    def several(g, carry):
        for k in range(4):
            one(4 * g + k)
        return carry

    lax.fori_loop(0, NPAIR // 4, several, 0)


def step0(tab, order, place, norms, high, low, pieces):
    smem = pl.BlockSpec(memory_space=pltpu.SMEM)
    vmem = pl.BlockSpec(memory_space=pltpu.VMEM)
    halves = jax.ShapeDtypeStruct((2 * NPAIR, HALF, SAMP), BF16)
    grams = jax.ShapeDtypeStruct((2, NPAIR, QUARTER, PAIRW), F32)
    return pl.pallas_call(
        step0_kernel,
        in_specs=[smem] * 3 + [vmem] * 3 + [pl.BlockSpec(memory_space=pl.ANY)] * 8,
        out_specs=[vmem] * 5,
        out_shape=[halves, halves, grams, grams, jax.ShapeDtypeStruct((NPAIR, PAIRW), F32)],
        scratch_shapes=[
            pltpu.VMEM((NPAIR, PAIRW, PAIRW), F32),
            pltpu.VMEM((2, NPAIR, PAIRW), F32),
            pltpu.SemaphoreType.DMA((8,)),
        ],
        compiler_params=pltpu.CompilerParams(vmem_limit_bytes=36 * MIB),
        cost_estimate=pl.CostEstimate(flops=4 << 30, bytes_accessed=24 * MIB, transcendentals=0),
        name="step0",
    )(tab, order, place, norms, high, low, *pieces)


def step1_kernel(norm_ref, high_ref, low_ref, rot_ref, gram_ref, pay_ref, norms_ref):
    norms_ref[0] = norm_ref[...]
    norms_ref[1] = pltpu.roll(norm_ref[...], HALF, 1)

    def one(p, j):
        i = 2 * p + j
        nu = norms_ref[jnp.where(i == 1, 1, 0), pl.ds(jnp.maximum(i - 1, 0), 1), :]
        nl = norms_ref[
            jnp.where(i == NPAIR - 1, 1, 0), pl.ds(jnp.minimum(i + 1, NPAIR - 1), 1), :
        ]
        scale = scales(jnp.where(lanes((1, PAIRW)) < HALF, nu, nl))
        left = left_operand(rot_ref[i] * scale)
        right = jnp.concatenate(
            [high_ref[2 * i], high_ref[2 * i + 1], low_ref[2 * i], low_ref[2 * i + 1]], 0
        )
        moved = product(left, right)
        su, sl = next_slots(i)
        pay_ref[su // 4, pl.ds(pl.multiple_of((su % 4) * HALF, HALF), HALF), :] = moved[:HALF]
        pay_ref[sl // 4, pl.ds(pl.multiple_of((sl % 4) * HALF, HALF), HALF), :] = moved[HALF:]
        high, low = split(moved)
        wide = outer(
            jnp.concatenate([high[:HALF], low[:HALF]], 0),
            jnp.concatenate([high[HALF:], low[HALF:]], 0),
        )
        folded = wide[:HALF] + wide[HALF:]
        folded = folded + pltpu.roll(folded, HALF, 1)
        cross = jnp.where(lanes((32, PAIRW)) < HALF, folded[:32], folded[32:])
        here = slice(j * PAIRW, (j + 1) * PAIRW)
        pay_ref[p, 256 : 256 + QUARTER, here] = gram_ref[i]
        pay_ref[p, 256 + QUARTER : PAYROWS, here] = cross

    def several(g, carry):
        for k in range(4):
            one(2 * g + k // 2, k % 2)
        return carry

    lax.fori_loop(0, NPAIR // 4, several, 0)


def step1(norms, high, low, rot, gram):
    vmem = pl.BlockSpec(memory_space=pltpu.VMEM)
    return pl.pallas_call(
        step1_kernel,
        in_specs=[vmem] * 5,
        out_specs=vmem,
        out_shape=jax.ShapeDtypeStruct((NDEV, PAYROWS, SAMP), F32),
        scratch_shapes=[pltpu.VMEM((2, NPAIR, PAIRW), F32)],
        compiler_params=pltpu.CompilerParams(vmem_limit_bytes=36 * MIB),
        cost_estimate=pl.CostEstimate(flops=3 << 30, bytes_accessed=24 * MIB, transcendentals=0),
        name="step1",
    )(norms, high, low, rot, gram)


def gram2_kernel(y_ref, gram_ref, sums_ref):
    @pl.when(pl.program_id(0) == 0)
    def _():
        gram_ref[...] = jnp.zeros_like(gram_ref)
        sums_ref[...] = jnp.zeros_like(sums_ref)

    count = y_ref.shape[0]
    for j in range(2):
        tiles = [split(y_ref[s, j * PAIRW : (j + 1) * PAIRW, :]) for s in range(count)]
        stacked = jnp.concatenate([jnp.concatenate(t, 0) for t in tiles], 1)
        gram_ref[j] += self_gram(stacked)
    sums_ref[...] += sum(y_ref[s, 256:PAYROWS, :] for s in range(count))


def gram2(y):
    count = 4
    return pl.pallas_call(
        gram2_kernel,
        grid=(NDEV // count,),
        in_specs=[pl.BlockSpec((count, PAYROWS, SAMP), lambda g: (g, 0, 0))],
        out_specs=[
            pl.BlockSpec((2, PAIRW, PAIRW), lambda g: (0, 0, 0)),
            pl.BlockSpec((PAYROWS - 256, SAMP), lambda g: (0, 0)),
        ],
        out_shape=[
            jax.ShapeDtypeStruct((2, PAIRW, PAIRW), F32),
            jax.ShapeDtypeStruct((PAYROWS - 256, SAMP), F32),
        ],
        compiler_params=pltpu.CompilerParams(vmem_limit_bytes=24 * MIB),
        cost_estimate=pl.CostEstimate(flops=2 << 30, bytes_accessed=10 * MIB, transcendentals=0),
        name="gram2",
    )(y)


def step2_kernel(gram_ref, rot_ref, y_ref, out_ref, pg_ref):
    count = y_ref.shape[0]
    mixings = [rot_ref[j] * scales(diagonal_row(gram_ref[j])) for j in range(2)]
    for j in range(2):
        left = left_operand(mixings[j])
        for s in range(count):
            right = jnp.concatenate(split(y_ref[s, j * PAIRW : (j + 1) * PAIRW, :]), 0)
            out_ref[j * PAIRW : (j + 1) * PAIRW, s * SAMP : (s + 1) * SAMP] = product(left, right)

    @pl.when(pl.program_id(0) == 0)
    def _():
        for j in range(2):
            inner = jnp.dot(
                mixings[j], gram_ref[j], precision=lax.Precision.HIGHEST, preferred_element_type=F32
            )
            pg_ref[j] = lax.dot_general(
                inner,
                mixings[j],
                (((1,), (1,)), ((), ())),
                precision=lax.Precision.HIGHEST,
                preferred_element_type=F32,
            )


def step2(gram, rot, y):
    count = 4
    whole = pl.BlockSpec((2, PAIRW, PAIRW), lambda g: (0, 0, 0))
    return pl.pallas_call(
        step2_kernel,
        grid=(NDEV // count,),
        in_specs=[whole, whole, pl.BlockSpec((count, 256, SAMP), lambda g: (g, 0, 0))],
        out_specs=[pl.BlockSpec((256, count * SAMP), lambda g: (0, g)), whole],
        out_shape=[
            jax.ShapeDtypeStruct((256, NDEV * SAMP), F32),
            jax.ShapeDtypeStruct((2, PAIRW, PAIRW), F32),
        ],
        compiler_params=pltpu.CompilerParams(vmem_limit_bytes=24 * MIB),
        cost_estimate=pl.CostEstimate(flops=2 << 30, bytes_accessed=18 * MIB, transcendentals=0),
        name="step2",
    )(gram, rot, y)


def grams_kernel(ends_ref, sums_ref, gram_ref, above_ref, below_ref, last_ref, out_ref):
    shape = (HALF, PAIRW)
    left = lanes(shape) < HALF
    zero = jnp.zeros(shape, F32)

    def symmetric(top, bottom):
        full = jnp.concatenate([top, bottom], 0)
        turned = full.T
        low_left = (lanes((PAIRW, PAIRW)) < HALF) & (
            lax.broadcasted_iota(jnp.int32, (PAIRW, PAIRW), 0) >= HALF
        )
        return jnp.where(low_left, turned, full) * (1.0 / ROWS)

    def turn(value):
        return pltpu.roll(value, HALF, 1)

    first, last = ends_ref[0] == 1, ends_ref[1] == 1
    for j in range(2):
        here = slice(j * PAIRW, (j + 1) * PAIRW)
        top = sums_ref[0:64, here]
        packed = sums_ref[64:96, here]
        low = jnp.where(left, zero, jnp.concatenate([packed, turn(packed)], 0))
        out_ref[0, j] = symmetric(top, low)
        packed = sums_ref[96:128, here]
        cross = jnp.concatenate([turn(packed), packed], 0)
        if j == 0:
            upper = jnp.where(first, gram_ref[0, :HALF], gram_ref[1, :HALF])
            lower = jnp.where(first, turn(gram_ref[1, :HALF]), below_ref[...])
        else:
            upper = jnp.where(last, turn(gram_ref[1, HALF:]), above_ref[...])
            lower = gram_ref[0, HALF:]
        out_ref[1, j] = symmetric(jnp.where(left, upper, cross), jnp.where(left, zero, lower))
        out_ref[2, j] = last_ref[j] * (1.0 / ROWS)


def grams(ends, sums, gram, above, below, last):
    vmem = pl.BlockSpec(memory_space=pltpu.VMEM)
    return pl.pallas_call(
        grams_kernel,
        in_specs=[pl.BlockSpec(memory_space=pltpu.SMEM)] + [vmem] * 5,
        out_specs=vmem,
        out_shape=jax.ShapeDtypeStruct((3, 2, PAIRW, PAIRW), F32),
        compiler_params=pltpu.CompilerParams(vmem_limit_bytes=16 * MIB),
        cost_estimate=pl.CostEstimate(flops=1 << 20, bytes_accessed=2 * MIB, transcendentals=0),
        name="grams",
    )(ends, sums, gram, above, below, last)


def body(samples_slab, block_order, rotations):
    pair, row = lax.axis_index("pair"), lax.axis_index("row")
    core, y_lo = row % 2, row // 2
    turned = jnp.swapaxes(rotations, 2, 3)
    own0 = lax.dynamic_slice_in_dim(turned[0], core, 1, 0)
    own1 = lax.dynamic_slice_in_dim(turned[1].reshape(4, HALF, PAIRW), row, 1, 0)
    rot1 = lax.all_gather(own1, BOTH, axis=0, tiled=True).reshape(NPAIR, PAIRW, PAIRW)
    pieces, offs = gather_pairs(own0)
    tab = (2 * pair + core) ^ jnp.array(offs, jnp.int32)
    norm0, high, low = prepare(samples_slab[0])
    norm0 = sum_all(norm0)
    place = jnp.stack([core, y_lo]).astype(jnp.int32)
    high, low, keep, send, norm1 = step0(tab, block_order, place, norm0, high, low, pieces)
    norm1 = sum_all(norm1)
    keep = keep + exchange(send, (0, 0, 0, 0, 1))
    quarter = keep[0] + exchange(keep[1], (0, 0, 0, 1, 0))
    payload = step1(norm1, high, low, rot1, quarter)
    arrived = lax.all_to_all(payload, "pair", 0, 0)
    gram, sums = gram2(arrived)
    gram = sum_row(gram)
    placed = lax.dynamic_update_slice(
        jnp.zeros((4 * QUARTER, SAMP), F32), sums[:QUARTER], (row * QUARTER, 0)
    )
    sums = sum_row(jnp.concatenate([placed, sums[QUARTER:]], 0))
    above = lax.ppermute(gram[0, :HALF], "pair", [(k, k - 1) for k in range(1, NDEV)])
    below = lax.ppermute(gram[1, HALF:], "pair", [(k - 1, k) for k in range(1, NDEV)])
    rotated, last = step2(gram, turned[2], arrived)
    ends = jnp.stack([pair == 0, pair == NDEV - 1]).astype(jnp.int32)
    return rotated, grams(ends, sums, gram, above, below, last)


def solution(mesh):
    in_specs = (P("row", "pair", None), P(), P(None, "pair", None, None))
    out_specs = (P("pair", "row"), P(None, "pair", None, None))
    return jax.shard_map(body, mesh=mesh, in_specs=in_specs, out_specs=out_specs, check_vma=False)
```

time: 578 us -> 376 us (0.65)
  blocking collectives: 108 us -> 0 us
  waiting for transfers between devices: 280 us -> 210 us
  matrix products: 63.7 us -> 0 us
  Pallas kernels: 0 us -> 62.9 us
  local copies, waits for them, and re-layouts: 67.1 us -> 20 us
  starting transfers between devices: 17.4 us -> 61.7 us
  other arithmetic: 18.1 us -> 0.68 us
    all_to_all x0 -> x1, waiting for transfers between devices: none -> 138 us  [body(): arrived = lax.all_to_all(payload, 'pair', 0, 0)]
    all_to_all x1 -> x0, blocking collectives: 108 us -> none  [body(): lax.all_to_all(arranged, 'pair', split_axis=0, concat_axis=2, tiled=True)]
    ppermute x4 -> x35, waiting for transfers between devices: 177 us -> 72.2 us  [the longest x33 72.2 us: exchange(): return lax.ppermute(value, BOTH, pairs)]
    psum x3 -> x0, waiting for transfers between devices: 103 us -> none  [body(): gram_sum = lax.psum(partial_value, 'row')]
    dot_general x12 -> x0, matrix products: 63.7 us -> none  [the longest x3 32.6 us: transform(): jnp.einsum('kcd,kcr->kdr', mixing, pair_cols, precision=lax.Precision.HIG...]
    pallas_call x0 -> x6, Pallas kernels: none -> 62.9 us  [the longest x1 22.7 us: step1(): pl.pallas_call(step1_kernel, in_specs=[vmem] * 5, out_specs=vmem, out_sha...]
    ppermute x4 -> x35, starting transfers between devices: 16.9 us -> 51.4 us  [the longest x33 44.1 us: exchange(): return lax.ppermute(value, BOTH, pairs)]
    psum x3 -> x0, local copies, waits for them, and re-layouts: 16.6 us -> none  [body(): gram_sum = lax.psum(partial_value, 'row')]
  transfers between devices with their start and end apart: 7 -> 37, of which waited for: 7 -> 26; matrix products, arithmetic and copies ran while one was open for 0% -> 0% of each run, Pallas kernels for 0% -> 8%
where the time goes in v1:
time: 376 us; the launch traced here: 370 us
  waiting for transfers between devices  210 us (56%)
  Pallas kernels  62.9 us (17%)
  starting transfers between devices  61.7 us (16%)
  local copies, waits for them, and re-layouts  20 us (5%)
  between operations  14.4 us (4%)
    all_to_all x1, waiting for transfers between devices, body(): arrived = lax.all_to_all(payload, 'pair', 0, 0)  138 us
    ppermute x33, waiting for transfers between devices, exchange(): return lax.ppermute(value, BOTH, pairs)  72.2 us
    ppermute x33, starting transfers between devices, exchange(): return lax.ppermute(value, BOTH, pairs)  44.1 us
    pallas_call x1, Pallas kernels, step1(): pl.pallas_call(step1_kernel, in_specs=[vmem] * 5, out_specs=vmem, out_sha...  22.7 us
    unnamed x24, local copies, waits for them, and re-layouts  19.2 us
    pallas_call x1, Pallas kernels, step0(): pl.pallas_call(step0_kernel, in_specs=[smem] * 3 + [vmem] * 3 + [pl.Block...  16.2 us
    pallas_call x1, Pallas kernels, step2(): pl.pallas_call(step2_kernel, grid=(NDEV // count,), in_specs=[whole, whol...  11.3 us
    all_to_all x1, starting transfers between devices, body(): arrived = lax.all_to_all(payload, 'pair', 0, 0)  10.2 us
  transfers between devices with their start and end apart: 37, of which 26 were waited for; matrix products, arithmetic and copies ran while one was open for 0% of the time, Pallas kernels for 8%

profile of v1, /device:TPU:2, one launch (start us, length us, event | category | flops | bytes accessed | tf_op | source)
XLA Modules:
  0.0 369.8 jit_solution(14480980383378932178)
XLA Ops:
  9.1 3.1 collective-permute-start.11
  18.9 4.1 %collective-permute-start.13 = (f32[2,128,128]{2,1,0:T(8,128)S(1)}, f32[2,128,128]{2,1,0:T(8,128)S(1)}, u32[]{:S(2)}, u32[]{:S(2)}) collective-permute-start(f32[2,128,128]{2,1,0:T(8,128)S(1)} %pad_maximum_fusion.4), channel_id=1, source_target_pairs={{0,96},{1,97},{2,98},{3,99},{4,100},{5,101},{6,102},{7,103},{8,104... | collective-permute-start | bytes 393224 | tf_op jit(solution)/shard_map/ppermute | solution.py:36
  34.7 6.7 %collective-permute-done.10.rest_1_ = f32[8,128,128]{2,1,0:T(8,128)S(1)} collective-permute-done((f32[8,128,128]{2,1,0:T(8,128)S(1)}, f32[8,128,128]{2,1,0:T(8,128)S(1)}, u32[]{:S(2)}, u32[]{:S(2)}) %collective-permute-start.10) | collective-permute-done | bytes 524320 | tf_op jit(solution)/shard_map/ppermute | solution.py:36
  42.8 3.4 copy-done
  46.2 3.4 prepare.1
  55.2 3.7 collective-permute-done.1
  58.9 2.9 collective-permute-start.2
  73.0 3.9 %collective-permute-done.5 = f32[64,128]{1,0:T(8,128)S(1)} collective-permute-done((f32[64,128]{1,0:T(8,128)S(1)}, f32[64,128]{1,0:T(8,128)S(1)}, u32[]{:S(2)}, u32[]{:S(2)}) %collective-permute-start.5) | collective-permute-done | bytes 32800 | tf_op jit(solution)/shard_map/ppermute | solution.py:36
  76.9 2.8 collective-permute-start.6
  82.1 16.2 %step0.1 = (bf16[128,64,256]{2,1,0:T(8,128)(2,1)S(1)}, bf16[128,64,256]{2,1,0:T(8,128)(2,1)S(1)}, f32[2,64,24,128]{3,2,1,0:T(8,128)S(1)}, f32[2,64,24,128]{3,2,1,0:T(8,128)S(1)}, f32[64,128]{1,0:T(8,128)S(1)}) custom-call(s32[64]{0:T(128)S(1)} %broadcast_xor_fusion.tab_ref, s32[128]{0:T(128)S(1)} %copy-done.8, s32[2]{0:T(128)S(1)} %pad_add_fusion.place_ref, ...), custom_call_target="tpu_custom_call" | custom-call | flops 4294967296 | bytes 25165824 | tf_op jit(solution)/shard_map/step0/pallas_call | solution.py:223
  102.3 3.4 collective-permute-done.27
  109.3 17.0 %collective-permute-done.21 = f32[64,128]{1,0:T(8,128)S(1)} collective-permute-done((f32[64,128]{1,0:T(8,128)S(1)}, f32[64,128]{1,0:T(8,128)S(1)}, u32[]{:S(2)}, u32[]{:S(2)}) %collective-permute-start.21) | collective-permute-done | bytes 32800 | tf_op jit(solution)/shard_map/ppermute | solution.py:36
  126.3 2.7 collective-permute-start.22
  131.5 2.7 collective-permute-start.23
  140.4 3.9 %collective-permute-done.25 = f32[64,128]{1,0:T(8,128)S(1)} collective-permute-done((f32[64,128]{1,0:T(8,128)S(1)}, f32[64,128]{1,0:T(8,128)S(1)}, u32[]{:S(2)}, u32[]{:S(2)}) %collective-permute-start.25) | collective-permute-done | bytes 32800 | tf_op jit(solution)/shard_map/ppermute | solution.py:36
  144.3 2.8 collective-permute-start.26
  156.1 22.7 %step1.1 = f32[32,312,256]{2,1,0:T(8,128)} custom-call(f32[64,128]{1,0:T(8,128)S(1)} %add.93.norm_ref, bf16[128,64,256]{2,1,0:T(8,128)(2,1)S(1)} %copy-done.3, bf16[128,64,256]{2,1,0:T(8,128)(2,1)S(1)} %copy-done.5, f32[64,128,128]{2,1,0:T(8,128)S(1)} %bitcast.23, f32[64,24,128]{2,1,0:T(8,128)S(1)} %fusion.gram_ref), custom_call_target="tpu_custom_call" | custom-call | flops 3221225472 | bytes 25165824 | tf_op jit(solution)/shard_map/step1/pallas_call | solution.py:280
  178.8 10.2 %all-to-all-start = ((f32[32,312,256]{2,1,0:T(8,128)}), f32[32,312,256]{2,1,0:T(8,128)}, u32[]{:S(2)}, u32[]{:S(2)}) async-start(f32[32,312,256]{2,1,0:T(8,128)} %step1.1), calls=%async_computation | async-start | bytes 20447232 | tf_op jit(solution)/shard_map/all_to_all | solution.py:433
  189.1 137.8 %all-to-all-done.y_ref = f32[32,312,256]{2,1,0:T(8,128)} async-done(((f32[32,312,256]{2,1,0:T(8,128)}), f32[32,312,256]{2,1,0:T(8,128)}, u32[]{:S(2)}, u32[]{:S(2)}) %all-to-all-start) | async-done | bytes 10223648 | tf_op jit(solution)/shard_map/all_to_all | solution.py:433
  326.9 7.9 %gram2.1 = (f32[2,128,128]{2,1,0:T(8,128)S(1)}, f32[56,256]{1,0:T(8,128)S(1)}) custom-call(f32[32,312,256]{2,1,0:T(8,128)} %all-to-all-done.y_ref), custom_call_target="tpu_custom_call" | custom-call | flops 2147483648 | bytes 10485760 | tf_op jit(solution)/shard_map/gram2/pallas_call | solution.py:308
  338.5 4.2 %collective-permute-done.30 = f32[2,128,128]{2,1,0:T(8,128)S(1)} collective-permute-done((f32[2,128,128]{2,1,0:T(8,128)S(1)}, f32[2,128,128]{2,1,0:T(8,128)S(1)}, u32[]{:S(2)}, u32[]{:S(2)}) %collective-permute-start.30) | collective-permute-done | bytes 131104 | tf_op jit(solution)/shard_map/ppermute | solution.py:36
  342.7 3.9 %collective-permute-start.33 = (f32[64,128]{1,0:T(8,128)S(1)}, f32[64,128]{1,0:T(8,128)S(1)}, u32[]{:S(2)}, u32[]{:S(2)}) collective-permute-start(f32[64,128]{1,0:T(8,128)S(1)} %get-tuple-element.30), channel_id=1, source_target_pairs={{4,0},{8,4},{12,8},{16,12},{20,16},{24,20},{28,24},{32,28},{36,32}... | collective-permute-start | bytes 98312 | tf_op jit(solution)/shard_map/ppermute | solution.py:440
  346.7 3.4 collective-permute-start.34
  350.1 11.3 %step2.1 = (f32[256,8192]{1,0:T(8,128)}, f32[2,128,128]{2,1,0:T(8,128)S(1)}) custom-call(f32[2,128,128]{2,1,0:T(8,128)S(1)} %add.98.gram_ref, f32[2,128,128]{2,1,0:T(8,128)S(1)} %get-tuple-element.26.rot_ref, f32[32,312,256]{2,1,0:T(8,128)} %all-to-all-done.y_ref), custom_call_target="tpu_custom_call" | custom-call | flops 2147483648 | bytes 18874368 | tf_op jit(solution)/shard_map/step2/pallas_call | solution.py:353
  (119 shorter events, 71.1 us)
Async XLA Ops:
  7.2 142.4 %all-gather.2.cloned.1.call-start = ((), (), s32[]{:S(2)}) async-start(), calls=%async_computation.1 | async-start | bytes 4227072 | tf_op jit(solution)/shard_map/all_gather | solution.py:422
  9.1 5.6 %collective-permute-start.11 = (f32[1,128,128]{2,1,0:T(8,128)S(1)}, f32[1,128,128]{2,1,0:T(8,128)S(1)}, u32[]{:S(2)}, u32[]{:S(2)}) collective-permute-start(f32[1,128,128]{2,1,0:T(8,128)S(1)} %dynamic-slice_bitcast_fusion), channel_id=1, source_target_pairs={{0,6},{1,7},{2,4},{3,5},{4,2},{5,3},{6,0},{7,1},{8,14},{9,15},{10,... | collective-permute-start | bytes 196616 | tf_op jit(solution)/shard_map/ppermute | solution.py:36
  16.6 6.5 %collective-permute-start.8 = (f32[2,128,128]{2,1,0:T(8,128)S(1)}, f32[2,128,128]{2,1,0:T(8,128)S(1)}, u32[]{:S(2)}, u32[]{:S(2)}) collective-permute-start(f32[2,128,128]{2,1,0:T(8,128)S(1)} %pad_maximum_fusion.3), channel_id=1, source_target_pairs={{0,24},{1,25},{2,26},{3,27},{4,28},{5,29},{6,30},{7,31},{8,16},{9,... | collective-permute-start | bytes 393224 | tf_op jit(solution)/shard_map/ppermute | solution.py:36
  18.9 7.1 %collective-permute-start.13 = (f32[2,128,128]{2,1,0:T(8,128)S(1)}, f32[2,128,128]{2,1,0:T(8,128)S(1)}, u32[]{:S(2)}, u32[]{:S(2)}) collective-permute-start(f32[2,128,128]{2,1,0:T(8,128)S(1)} %pad_maximum_fusion.4), channel_id=1, source_target_pairs={{0,96},{1,97},{2,98},{3,99},{4,100},{5,101},{6,102},{7,103},{8,104... | collective-permute-start | bytes 393224 | tf_op jit(solution)/shard_map/ppermute | solution.py:36
  23.1 6.6 %collective-permute-start.9 = (f32[4,128,128]{2,1,0:T(8,128)S(1)}, f32[4,128,128]{2,1,0:T(8,128)S(1)}, u32[]{:S(2)}, u32[]{:S(2)}) collective-permute-start(f32[4,128,128]{2,1,0:T(8,128)S(1)} %pad_maximum_fusion.1), channel_id=1, source_target_pairs={{0,32},{1,33},{2,34},{3,35},{4,36},{5,37},{6,38},{7,39},{8,40},{9,... | collective-permute-start | bytes 786440 | tf_op jit(solution)/shard_map/ppermute | solution.py:36
  26.0 6.6 %collective-permute-start.14 = (f32[4,128,128]{2,1,0:T(8,128)S(1)}, f32[4,128,128]{2,1,0:T(8,128)S(1)}, u32[]{:S(2)}, u32[]{:S(2)}) collective-permute-start(f32[4,128,128]{2,1,0:T(8,128)S(1)} %pad_maximum_fusion.2), channel_id=1, source_target_pairs={{0,8},{1,9},{2,10},{3,11},{4,12},{5,13},{6,14},{7,15},{8,0},{9,1},... | collective-permute-start | bytes 786440 | tf_op jit(solution)/shard_map/ppermute | solution.py:36
  29.7 11.7 %collective-permute-start.10 = (f32[8,128,128]{2,1,0:T(8,128)S(1)}, f32[8,128,128]{2,1,0:T(8,128)S(1)}, u32[]{:S(2)}, u32[]{:S(2)}) collective-permute-start(f32[8,128,128]{2,1,0:T(8,128)S(1)} %pad_maximum_fusion.rest_0_), channel_id=1, source_target_pairs={{0,96},{1,97},{2,98},{3,99},{4,100},{5,101},{6,102},{7,103},{8,104... | collective-permute-start | bytes 1572872 | tf_op jit(solution)/shard_map/ppermute | solution.py:36
  32.6 10.1 %collective-permute-start.15 = (f32[8,128,128]{2,1,0:T(8,128)S(1)}, f32[8,128,128]{2,1,0:T(8,128)S(1)}, u32[]{:S(2)}, u32[]{:S(2)}) collective-permute-start(f32[8,128,128]{2,1,0:T(8,128)S(1)} %constant_dynamic-update-slice_fusion.rest_2_), channel_id=1, source_target_pairs={{0,24},{1,25},{2,26},{3,27},{4,28},{5,29},{6,30},{7,31},{8,16},{9,... | collective-permute-start | bytes 1572872 | tf_op jit(solution)/shard_map/ppermute | solution.py:36
  34.2 47.9 %collective-permute-start.16 = (f32[8,128,128]{2,1,0:T(8,128)S(1)}, f32[8,128,128]{2,1,0:T(8,128)S(1)}, u32[]{:S(2)}, u32[]{:S(2)}) collective-permute-start(f32[8,128,128]{2,1,0:T(8,128)S(1)} %pad_maximum_fusion.rest_0_), channel_id=1, source_target_pairs={{0,1},{1,0},{2,3},{3,2},{4,5},{5,4},{6,7},{7,6},{8,9},{9,8},{10,11... | collective-permute-start | bytes 1572872 | tf_op jit(solution)/shard_map/ppermute | solution.py:36
  34.2 47.9 %collective-permute-start.18 = (f32[8,128,128]{2,1,0:T(8,128)S(1)}, f32[8,128,128]{2,1,0:T(8,128)S(1)}, u32[]{:S(2)}, u32[]{:S(2)}) collective-permute-start(f32[8,128,128]{2,1,0:T(8,128)S(1)} %constant_dynamic-update-slice_fusion.rest_2_), channel_id=1, source_target_pairs={{0,1},{1,0},{2,3},{3,2},{4,5},{5,4},{6,7},{7,6},{8,9},{9,8},{10,11... | collective-permute-start | bytes 1572872 | tf_op jit(solution)/shard_map/ppermute | solution.py:36
  41.4 40.6 %collective-permute-start.17 = (f32[8,128,128]{2,1,0:T(8,128)S(1)}, f32[8,128,128]{2,1,0:T(8,128)}, u32[]{:S(2)}, u32[]{:S(2)}) collective-permute-start(f32[8,128,128]{2,1,0:T(8,128)S(1)} %collective-permute-done.10.rest_1_), channel_id=1, source_target_pairs={{0,1},{1,0},{2,3},{3,2},{4,5},{5,4},{6,7},{7,6},{8,9},{9,8},{10,11... | collective-permute-start | bytes 1572872 | tf_op jit(solution)/shard_map/ppermute | solution.py:36
  42.8 39.3 %collective-permute-start.19 = (f32[8,128,128]{2,1,0:T(8,128)S(1)}, f32[8,128,128]{2,1,0:T(8,128)}, u32[]{:S(2)}, u32[]{:S(2)}) collective-permute-start(f32[8,128,128]{2,1,0:T(8,128)S(1)} %collective-permute-done.15.rest_3_), channel_id=1, source_target_pairs={{0,1},{1,0},{2,3},{3,2},{4,5},{5,4},{6,7},{7,6},{8,9},{9,8},{10,11... | collective-permute-start | bytes 1572872 | tf_op jit(solution)/shard_map/ppermute | solution.py:36
  58.9 5.1 %collective-permute-start.2 = (f32[64,128]{1,0:T(8,128)S(1)}, f32[64,128]{1,0:T(8,128)S(1)}, u32[]{:S(2)}, u32[]{:S(2)}) collective-permute-start(f32[64,128]{1,0:T(8,128)S(1)} %add.80), channel_id=1, source_target_pairs={{0,6},{1,7},{2,4},{3,5},{4,2},{5,3},{6,0},{7,1},{8,14},{9,15},{10,... | collective-permute-start | bytes 98312 | tf_op jit(solution)/shard_map/ppermute | solution.py:36
  76.9 5.1 %collective-permute-start.6 = (f32[64,128]{1,0:T(8,128)S(1)}, f32[64,128]{1,0:T(8,128)S(1)}, u32[]{:S(2)}, u32[]{:S(2)}) collective-permute-start(f32[64,128]{1,0:T(8,128)S(1)} %add.84), channel_id=1, source_target_pairs={{0,96},{1,97},{2,98},{3,99},{4,100},{5,101},{6,102},{7,103},{8,104... | collective-permute-start | bytes 98312 | tf_op jit(solution)/shard_map/ppermute | solution.py:36
  106.0 43.5 %collective-permute-start.28 = (f32[64,24,128]{2,1,0:T(8,128)S(1)}, f32[64,24,128]{2,1,0:T(8,128)S(1)}, u32[]{:S(2)}, u32[]{:S(2)}) collective-permute-start(f32[64,24,128]{2,1,0:T(8,128)S(1)} %slice_bitcast_fusion), channel_id=1, source_target_pairs={{0,2},{1,3},{2,0},{3,1},{4,6},{5,7},{6,4},{7,5},{8,10},{9,11},{10,... | collective-permute-start | bytes 2359304 | tf_op jit(solution)/shard_map/ppermute | solution.py:36
  107.4 19.0 %collective-permute-start.21 = (f32[64,128]{1,0:T(8,128)S(1)}, f32[64,128]{1,0:T(8,128)S(1)}, u32[]{:S(2)}, u32[]{:S(2)}) collective-permute-start(f32[64,128]{1,0:T(8,128)S(1)} %add.87), channel_id=1, source_target_pairs={{0,2},{1,3},{2,0},{3,1},{4,6},{5,7},{6,4},{7,5},{8,10},{9,11},{10,... | collective-permute-start | bytes 98312 | tf_op jit(solution)/shard_map/ppermute | solution.py:36
  126.3 5.1 %collective-permute-start.22 = (f32[64,128]{1,0:T(8,128)S(1)}, f32[64,128]{1,0:T(8,128)S(1)}, u32[]{:S(2)}, u32[]{:S(2)}) collective-permute-start(f32[64,128]{1,0:T(8,128)S(1)} %add.88), channel_id=1, source_target_pairs={{0,6},{1,7},{2,4},{3,5},{4,2},{5,3},{6,0},{7,1},{8,14},{9,15},{10,... | collective-permute-start | bytes 98312 | tf_op jit(solution)/shard_map/ppermute | solution.py:36
  131.5 4.6 %collective-permute-start.23 = (f32[64,128]{1,0:T(8,128)S(1)}, f32[64,128]{1,0:T(8,128)S(1)}, u32[]{:S(2)}, u32[]{:S(2)}) collective-permute-start(f32[64,128]{1,0:T(8,128)S(1)} %add.89), channel_id=1, source_target_pairs={{0,8},{1,9},{2,10},{3,11},{4,12},{5,13},{6,14},{7,15},{8,0},{9,1},... | collective-permute-start | bytes 98312 | tf_op jit(solution)/shard_map/ppermute | solution.py:36
  144.3 5.1 %collective-permute-start.26 = (f32[64,128]{1,0:T(8,128)S(1)}, f32[64,128]{1,0:T(8,128)S(1)}, u32[]{:S(2)}, u32[]{:S(2)}) collective-permute-start(f32[64,128]{1,0:T(8,128)S(1)} %add.92), channel_id=1, source_target_pairs={{0,96},{1,97},{2,98},{3,99},{4,100},{5,101},{6,102},{7,103},{8,104... | collective-permute-start | bytes 98312 | tf_op jit(solution)/shard_map/ppermute | solution.py:36
  178.8 148.1 %all-to-all-start = ((f32[32,312,256]{2,1,0:T(8,128)}), f32[32,312,256]{2,1,0:T(8,128)}, u32[]{:S(2)}, u32[]{:S(2)}) async-start(f32[32,312,256]{2,1,0:T(8,128)} %step1.1), calls=%async_computation | async-start | bytes 20447232 | tf_op jit(solution)/shard_map/all_to_all | solution.py:433
  336.3 6.4 %collective-permute-start.30 = (f32[2,128,128]{2,1,0:T(8,128)S(1)}, f32[2,128,128]{2,1,0:T(8,128)S(1)}, u32[]{:S(2)}, u32[]{:S(2)}) collective-permute-start(f32[2,128,128]{2,1,0:T(8,128)S(1)} %add.97), channel_id=1, source_target_pairs={{0,2},{1,3},{2,0},{3,1},{4,6},{5,7},{6,4},{7,5},{8,10},{9,11},{10,... | collective-permute-start | bytes 393224 | tf_op jit(solution)/shard_map/ppermute | solution.py:36
  336.6 24.8 %collective-permute-start.32 = (f32[128,256]{1,0:T(8,128)S(1)}, f32[128,256]{1,0:T(8,128)S(1)}, u32[]{:S(2)}, u32[]{:S(2)}) collective-permute-start(f32[128,256]{1,0:T(8,128)S(1)} %fusion.1), channel_id=1, source_target_pairs={{0,2},{1,3},{2,0},{3,1},{4,6},{5,7},{6,4},{7,5},{8,10},{9,11},{10,... | collective-permute-start | bytes 393224 | tf_op jit(solution)/shard_map/ppermute | solution.py:36
  342.7 18.6 %collective-permute-start.33 = (f32[64,128]{1,0:T(8,128)S(1)}, f32[64,128]{1,0:T(8,128)S(1)}, u32[]{:S(2)}, u32[]{:S(2)}) collective-permute-start(f32[64,128]{1,0:T(8,128)S(1)} %get-tuple-element.30), channel_id=1, source_target_pairs={{4,0},{8,4},{12,8},{16,12},{20,16},{24,20},{28,24},{32,28},{36,32}... | collective-permute-start | bytes 98312 | tf_op jit(solution)/shard_map/ppermute | solution.py:440
  346.7 14.7 %collective-permute-start.34 = (f32[64,128]{1,0:T(8,128)S(1)}, f32[64,128]{1,0:T(8,128)S(1)}, u32[]{:S(2)}, u32[]{:S(2)}) collective-permute-start(f32[64,128]{1,0:T(8,128)S(1)} %get-tuple-element.29), channel_id=1, source_target_pairs={{0,4},{4,8},{8,12},{12,16},{16,20},{20,24},{24,28},{28,32},{32,36}... | collective-permute-start | bytes 98312 | tf_op jit(solution)/shard_map/ppermute | solution.py:441
  (23 other events, 123.5 us)
Sparse Core Ops, SparseCore 0:
  11.7 68.2 all-gather.1

commit v2 on v0

v2 whole, which is shorter than its diff:
```python
import functools
import itertools

import jax
import jax.numpy as jnp
from jax import lax
from jax.experimental import pallas as pl
from jax.experimental.pallas import tpu as pltpu
from jax.sharding import PartitionSpec as P


BOTH = ("pair", "row")
NZ, NX, NY, NC = 4, 4, 2, 2
NPAIR = 64
PAIRW = 128
HALF = 64
SAMP = 256
NDEV = 32
ROWS = 32768
EPS = 1e-06
QUARTER = 32
PAYROWS = 256 + QUARTER
MIB = 1 << 20
F32, BF16 = jnp.float32, jnp.bfloat16


def flat(z, x, yh, yl, c):
    return (((z * NX + x) * 2 + yh) * 2 + yl) * 2 + c


def exchange(value, flip):
    pairs = []
    for here in itertools.product(range(NZ), range(NX), range(2), range(2), range(2)):
        there = tuple(a ^ b for a, b in zip(here, flip))
        pairs.append((flat(*here), flat(*there)))
    return lax.ppermute(value, BOTH, pairs)


X1, X3, Z1, Z3 = (0, 1, 0, 0, 0), (0, 3, 0, 0, 0), (1, 0, 0, 0, 0), (3, 0, 0, 0, 0)
YLO, YBOTH, CORE = (0, 0, 0, 1, 0), (0, 0, 1, 1, 0), (0, 0, 0, 0, 1)


def add_over(value, *flips):
    for flip in flips:
        value = value + exchange(value, flip)
    return value


def together(*values):
    return lax.optimization_barrier(values)


def split(value):
    high = value.astype(BF16)
    return high, (value - high.astype(F32)).astype(BF16)


def left_operand(mixing_t):
    high, low = split(mixing_t)
    return jnp.concatenate(
        [
            jnp.concatenate([high, high], 1),
            jnp.concatenate([low, jnp.zeros_like(low)], 1),
        ],
        0,
    )


def product(left, right):
    wide = jnp.dot(left, right, preferred_element_type=F32)
    return wide[:PAIRW] + wide[PAIRW:]


def outer(a, b):
    return lax.dot_general(a, b, (((1,), (1,)), ((), ())), preferred_element_type=F32)


def self_gram(stacked):
    wide = outer(stacked, stacked)
    return wide[:PAIRW, :PAIRW] + wide[PAIRW:, :PAIRW] + wide[:PAIRW, PAIRW:]


def diagonal_row(gram):
    size = gram.shape[0]
    eye = lax.broadcasted_iota(jnp.int32, (size, size), 0) == lax.broadcasted_iota(
        jnp.int32, (size, size), 1
    )
    return jnp.sum(jnp.where(eye, gram, 0.0), axis=0, keepdims=True)


def scales(norm_row):
    return lax.rsqrt(norm_row / ROWS + EPS)


def lanes(shape):
    return lax.broadcasted_iota(jnp.int32, shape, 1)


def next_slots(i):
    upper = jnp.where(i == 0, 0, jnp.where(i == NPAIR - 1, 2 * NPAIR - 1, 2 * i + 2))
    lower = jnp.where(i == 0, 2, 2 * i - 1)
    return upper, lower


TILES = NPAIR // 2


def norms_kernel(place_ref, x_ref, norm_ref, held_ref, sems):
    count = sems.shape[0]
    width = NPAIR // count

    def copy(g):
        part = pl.ds(g * width * PAIRW, width * PAIRW)
        return pltpu.make_async_copy(x_ref.at[:, part], held_ref.at[:, part], sems.at[g])

    for g in range(count):
        copy(g).start()
    for g in range(count):
        copy(g).wait()
        for t in range(width * g, width * (g + 1)):
            tile = held_ref[:, t * PAIRW : (t + 1) * PAIRW]
            row = jnp.sum(tile * tile, axis=0, keepdims=True)
            norm_ref[(t // TILES) ^ place_ref[2], t % TILES : t % TILES + 1, :] = row


def norms(place, x):
    return pl.pallas_call(
        norms_kernel,
        in_specs=[pl.BlockSpec(memory_space=pltpu.SMEM), pl.BlockSpec(memory_space=pl.ANY)],
        out_specs=pl.BlockSpec(memory_space=pltpu.VMEM),
        out_shape=jax.ShapeDtypeStruct((2, TILES, PAIRW), F32),
        scratch_shapes=[pltpu.VMEM((SAMP, NPAIR * PAIRW), F32), pltpu.SemaphoreType.DMA((8,))],
        compiler_params=pltpu.CompilerParams(vmem_limit_bytes=58 * MIB),
        cost_estimate=pl.CostEstimate(flops=8 * MIB, bytes_accessed=8 * MIB, transcendentals=0),
        name="norms",
    )(place, x)


def prepare_kernel(x_ref, halves_ref):
    tiles = x_ref.shape[1] // PAIRW
    for t in range(tiles):
        tile = x_ref[:, t * PAIRW : (t + 1) * PAIRW]
        high, low = split(tile.T)
        for h in range(2):
            halves_ref[2 * t + h, 0] = high[h * HALF : (h + 1) * HALF]
            halves_ref[2 * t + h, 1] = low[h * HALF : (h + 1) * HALF]


def prepare(x):
    width = 1024
    blocks = width // HALF
    return pl.pallas_call(
        prepare_kernel,
        grid=(x.shape[1] // width,),
        in_specs=[pl.BlockSpec((SAMP, width), lambda g: (0, g))],
        out_specs=pl.BlockSpec((blocks, 2, HALF, SAMP), lambda g: (g, 0, 0, 0)),
        out_shape=jax.ShapeDtypeStruct((2 * NPAIR, 2, HALF, SAMP), BF16),
        compiler_params=pltpu.CompilerParams(vmem_limit_bytes=58 * MIB),
        cost_estimate=pl.CostEstimate(flops=8 * MIB, bytes_accessed=16 * MIB, transcendentals=0),
        name="prepare",
    )(x)


SENT = PAIRW + TILES


def spread_kernel(place_ref, rot_ref, norm_ref, given_ref, copies_ref, quarter_ref, turned_ref):
    row, core = place_ref[0], place_ref[2]
    own = rot_ref[0, core].T
    norm = norm_ref[0] + given_ref[...]

    def copy(k, carry):
        copies_ref[k, :PAIRW] = own
        copies_ref[k, PAIRW:] = norm
        return carry

    lax.fori_loop(0, NDEV, copy, 0, unroll=4)
    for t in range(1, 3):
        for j in range(2):
            turned_ref[t - 1, j] = rot_ref[t, j].T
    half = pl.ds(pl.multiple_of((row % 2) * HALF, HALF), HALF)
    quarter_ref[...] = turned_ref[0, row // 2, half, :]


def spread(place, rotations, norm, given):
    vmem = pl.BlockSpec(memory_space=pltpu.VMEM)
    return pl.pallas_call(
        spread_kernel,
        in_specs=[pl.BlockSpec(memory_space=pltpu.SMEM), vmem, vmem, vmem],
        out_specs=[vmem] * 3,
        out_shape=[
            jax.ShapeDtypeStruct((NDEV, SENT, PAIRW), F32),
            jax.ShapeDtypeStruct((HALF, PAIRW), F32),
            jax.ShapeDtypeStruct((2, 2, PAIRW, PAIRW), F32),
        ],
        compiler_params=pltpu.CompilerParams(vmem_limit_bytes=8 * MIB),
        cost_estimate=pl.CostEstimate(flops=MIB, bytes_accessed=3 * MIB, transcendentals=0),
        name="spread",
    )(place, rotations, norm, given)


def collect_kernel(arrived_ref, norm_ref):
    norm_ref[...] = sum(arrived_ref[s, PAIRW:] for s in range(NDEV))


def collect(arrived):
    vmem = pl.BlockSpec(memory_space=pltpu.VMEM)
    return pl.pallas_call(
        collect_kernel,
        in_specs=[vmem],
        out_specs=vmem,
        out_shape=jax.ShapeDtypeStruct((TILES, PAIRW), F32),
        compiler_params=pltpu.CompilerParams(vmem_limit_bytes=8 * MIB),
        cost_estimate=pl.CostEstimate(flops=MIB, bytes_accessed=MIB, transcendentals=0),
        name="collect",
    )(arrived)


GROUP = 8
GROUPS = NPAIR // GROUP
OPERAND = (NPAIR, 2, 2, HALF, SAMP)


def whole_copy(ref, sem):
    return pltpu.make_async_copy(ref, ref, sem)


def step0_kernel(
    tab_ref, order_ref, place_ref, normc_ref, normo_ref, halves_ref, mine_ref, given_ref,
    next_ref, parts_ref, onorm_ref, right_ref, rot_ref, moved_ref, norms_ref, sems, out_sem
):

    def fetch(q, carry):
        i = tab_ref[q]
        for h in range(2):
            pltpu.make_async_copy(
                halves_ref.at[order_ref[2 * i + h]], right_ref.at[q, :, h], sems.at[0, q // GROUP]
            ).start()
        return carry

    lax.fori_loop(0, NPAIR, fetch, 0)
    for k in range(GROUPS):
        piece = (mine_ref, given_ref)[k // 4].at[pl.ds(GROUP * (k % 4), GROUP), pl.ds(0, PAIRW)]
        pltpu.make_async_copy(piece, rot_ref.at[pl.ds(GROUP * k, GROUP)], sems.at[1, k]).start()
    core = place_ref[2]
    for half, norm_ref in ((core, normc_ref), (1 - core, normo_ref)):
        rows = pl.ds(pl.multiple_of(half * TILES, TILES), TILES)
        norms_ref[0, rows, :] = norm_ref[...]
        norms_ref[1, rows, :] = pltpu.roll(norm_ref[...], HALF, 1)

    def spot(quarter, j):
        mine = quarter ^ place_ref[j]
        return (mine & 1) * 2 + (mine >> 1)

    def group(g, carry):
        part = pl.ds(GROUP * g, GROUP)
        whole_copy(right_ref.at[part], sems.at[0, g]).wait()
        whole_copy(rot_ref.at[part], sems.at[1, g]).wait()
        todo = [GROUP * g + k for k in range(GROUP)]
        index = [tab_ref[q] for q in todo]
        lefts = []
        for q, i in zip(todo, index):
            bu, bl = order_ref[2 * i], order_ref[2 * i + 1]
            nu = norms_ref[bu % 2, pl.ds(bu // 2, 1), :]
            nl = norms_ref[1 - bl % 2, pl.ds(bl // 2, 1), :]
            scale = scales(jnp.where(lanes((1, PAIRW)) < HALF, nu, nl))
            lefts.append(left_operand(rot_ref[q] * scale))
        values = [
            split(product(left, right_ref[q].reshape(2 * PAIRW, SAMP)))
            for left, q in zip(lefts, todo)
        ]
        for i, pieces_of in zip(index, values):
            slots = next_slots(i)
            for part_of, value in enumerate(pieces_of):
                for h, slot in enumerate(slots):
                    moved_ref[slot // 2, part_of, slot % 2] = value[h * HALF : (h + 1) * HALF]
        for i, (high, low) in zip(index, values):
            gram = self_gram(jnp.concatenate([high, low], 0))
            onorm_ref[pl.ds(i, 1), :] = diagonal_row(gram)
            bottom = gram[HALF:]
            packed = jnp.where(
                lanes((32, PAIRW)) >= HALF, bottom[:32], pltpu.roll(bottom[32:], HALF, 1)
            )
            p, j = i // 2, i % 2
            parts_ref[spot(0, j), j, p] = gram[:32]
            parts_ref[spot(1, j), j, p] = gram[32:HALF]
            parts_ref[spot(2, j), j, p] = packed
        return carry

    lax.fori_loop(0, GROUPS, group, 0)
    copy = pltpu.make_async_copy(moved_ref, next_ref, out_sem)
    copy.start()

    def cross(g, carry):
        wides = []
        for k in range(GROUP):
            upper = moved_ref[GROUP * g + k, :, 0].reshape(PAIRW, SAMP)
            lower = moved_ref[GROUP * g + k, :, 1].reshape(PAIRW, SAMP)
            wides.append(outer(upper, lower))
        for k, wide in enumerate(wides):
            folded = wide[:HALF] + wide[HALF:]
            folded = folded + pltpu.roll(folded, HALF, 1)
            parts_ref[spot(3, k % 2), k % 2, GROUP // 2 * g + k // 2] = jnp.where(
                lanes((32, PAIRW)) < HALF, folded[:32], folded[32:]
            )
        return carry

    lax.fori_loop(0, GROUPS, cross, 0)
    copy.wait()


def step0(tab, order, place, normc, normo, halves, mine, given):
    smem = pl.BlockSpec(memory_space=pltpu.SMEM)
    vmem = pl.BlockSpec(memory_space=pltpu.VMEM)
    anywhere = pl.BlockSpec(memory_space=pl.ANY)
    return pl.pallas_call(
        step0_kernel,
        in_specs=[smem] * 3 + [vmem] * 2 + [anywhere] * 3,
        out_specs=[anywhere, vmem, vmem],
        out_shape=[
            jax.ShapeDtypeStruct(OPERAND, BF16),
            jax.ShapeDtypeStruct((4, 2, NDEV, QUARTER, PAIRW), F32),
            jax.ShapeDtypeStruct((NPAIR, PAIRW), F32),
        ],
        scratch_shapes=[
            pltpu.VMEM(OPERAND, BF16),
            pltpu.VMEM((NPAIR, PAIRW, PAIRW), F32),
            pltpu.VMEM(OPERAND, BF16),
            pltpu.VMEM((2, NPAIR, PAIRW), F32),
            pltpu.SemaphoreType.DMA((2, GROUPS)),
            pltpu.SemaphoreType.DMA,
        ],
        compiler_params=pltpu.CompilerParams(vmem_limit_bytes=44 * MIB),
        cost_estimate=pl.CostEstimate(flops=4 << 30, bytes_accessed=24 * MIB, transcendentals=0),
        name="step0",
    )(tab, order, place, normc, normo, halves, mine, given)


def step1_kernel(
    norm_ref, operand_ref, rotation_ref, parta_ref, partb_ref, pay_ref, right_ref, rot_ref,
    norms_ref, sems
):
    for g in range(GROUPS):
        part = pl.ds(GROUP * g, GROUP)
        pltpu.make_async_copy(operand_ref.at[part], right_ref.at[part], sems.at[0, g]).start()
        pltpu.make_async_copy(rotation_ref.at[part], rot_ref.at[part], sems.at[1, g]).start()
    norms_ref[0] = norm_ref[...]
    norms_ref[1] = pltpu.roll(norm_ref[...], HALF, 1)
    pay_ref[:, 256:PAYROWS, :PAIRW] = parta_ref[...]
    pay_ref[:, 256:PAYROWS, PAIRW:] = partb_ref[...]

    def group(g, carry):
        part = pl.ds(GROUP * g, GROUP)
        whole_copy(right_ref.at[part], sems.at[0, g]).wait()
        whole_copy(rot_ref.at[part], sems.at[1, g]).wait()
        index = [GROUP * g + k for k in range(GROUP)]
        lefts = []
        for i in index:
            nu = norms_ref[jnp.where(i == 1, 1, 0), pl.ds(jnp.maximum(i - 1, 0), 1), :]
            nl = norms_ref[
                jnp.where(i == NPAIR - 1, 1, 0), pl.ds(jnp.minimum(i + 1, NPAIR - 1), 1), :
            ]
            scale = scales(jnp.where(lanes((1, PAIRW)) < HALF, nu, nl))
            lefts.append(left_operand(rot_ref[i] * scale))
        values = [
            product(left, right_ref[i].reshape(2 * PAIRW, SAMP)) for left, i in zip(lefts, index)
        ]
        for i, value in zip(index, values):
            for h, slot in enumerate(next_slots(i)):
                spot = pl.ds(pl.multiple_of((slot % 4) * HALF, HALF), HALF)
                pay_ref[slot // 4, spot, :] = value[h * HALF : (h + 1) * HALF]
        return carry

    lax.fori_loop(0, GROUPS, group, 0)


def step1(norm, operand, rot, parta, partb):
    vmem = pl.BlockSpec(memory_space=pltpu.VMEM)
    anywhere = pl.BlockSpec(memory_space=pl.ANY)
    return pl.pallas_call(
        step1_kernel,
        in_specs=[vmem, anywhere, anywhere, vmem, vmem],
        out_specs=vmem,
        out_shape=jax.ShapeDtypeStruct((NDEV, PAYROWS, SAMP), F32),
        scratch_shapes=[
            pltpu.VMEM(OPERAND, BF16),
            pltpu.VMEM((NPAIR, PAIRW, PAIRW), F32),
            pltpu.VMEM((2, NPAIR, PAIRW), F32),
            pltpu.SemaphoreType.DMA((2, GROUPS)),
        ],
        compiler_params=pltpu.CompilerParams(vmem_limit_bytes=28 * MIB),
        cost_estimate=pl.CostEstimate(flops=3 << 30, bytes_accessed=24 * MIB, transcendentals=0),
        name="step1",
    )(norm, operand, rot, parta, partb)


CHUNK = 4
CHUNKS = NDEV // CHUNK


def parts_kernel(place_ref, y_ref, placed_ref):
    sums = []
    for z_odd in range(2):
        source = [s for s in range(NDEV) if (s // (2 * NX)) % 2 == z_odd]
        sums.append(sum(y_ref[s, 256:PAYROWS, :] for s in source))
    placed_ref[...] = jnp.zeros_like(placed_ref)
    row, core = place_ref[0], place_ref[2]
    spots = [pl.ds(pl.multiple_of(QUARTER * q, QUARTER), QUARTER) for q in (row, core, core + 2)]
    placed_ref[0, spots[0], :] = sums[0][:, :PAIRW] + sums[1][:, :PAIRW]
    placed_ref[1, spots[1], :] = sums[0][:, PAIRW:]
    placed_ref[1, spots[2], :] = sums[1][:, PAIRW:]


def parts(place, y):
    vmem = pl.BlockSpec(memory_space=pltpu.VMEM)
    return pl.pallas_call(
        parts_kernel,
        in_specs=[pl.BlockSpec(memory_space=pltpu.SMEM), vmem],
        out_specs=vmem,
        out_shape=jax.ShapeDtypeStruct((2, 4 * QUARTER, PAIRW), F32),
        compiler_params=pltpu.CompilerParams(vmem_limit_bytes=14 * MIB),
        cost_estimate=pl.CostEstimate(flops=MIB, bytes_accessed=MIB, transcendentals=0),
        name="parts",
    )(place, y)


def gram2_kernel(y_ref, norm_ref, gram_ref):
    totals = [None, None]
    for g in range(CHUNKS):
        source = range(CHUNK * g, CHUNK * (g + 1))
        for j in range(2):
            halves = [split(y_ref[s, j * PAIRW : (j + 1) * PAIRW, :]) for s in source]
            high = jnp.concatenate([h for h, _ in halves], 1)
            low = jnp.concatenate([l for _, l in halves], 1)
            term = outer(high, jnp.concatenate([high, low], 0))
            totals[j] = term if g == 0 else totals[j] + term
    for j in range(2):
        mixed = totals[j][:, PAIRW:]
        gram = totals[j][:, :PAIRW] + mixed + mixed.T
        gram_ref[j] = gram
        norm_ref[j] = jnp.broadcast_to(diagonal_row(gram), (8, PAIRW))


def gram2(y):
    vmem = pl.BlockSpec(memory_space=pltpu.VMEM)
    return pl.pallas_call(
        gram2_kernel,
        in_specs=[vmem],
        out_specs=[vmem, vmem],
        out_shape=[
            jax.ShapeDtypeStruct((2, 8, PAIRW), F32),
            jax.ShapeDtypeStruct((2, PAIRW, PAIRW), F32),
        ],
        compiler_params=pltpu.CompilerParams(vmem_limit_bytes=14 * MIB),
        cost_estimate=pl.CostEstimate(flops=2 << 30, bytes_accessed=10 * MIB, transcendentals=0),
        name="gram2",
    )(y)


def step2_kernel(norm_ref, rot_ref, y_ref, out_ref, turned_ref, out_sem):
    lefts = [left_operand(rot_ref[j] * scales(norm_ref[j, 0:1])) for j in range(2)]
    for g in range(CHUNKS):
        for j in range(2):
            here = slice(j * PAIRW, (j + 1) * PAIRW)
            for s in range(CHUNK * g, CHUNK * (g + 1)):
                right = jnp.concatenate(split(y_ref[s, here, :]), 0)
                turned_ref[here, s * SAMP : (s + 1) * SAMP] = product(lefts[j], right)
        part = pl.ds(CHUNK * SAMP * g, CHUNK * SAMP)
        pltpu.make_async_copy(turned_ref.at[:, part], out_ref.at[:, part], out_sem).start()
    whole_copy(turned_ref, out_sem).wait()


def step2(norm, rot, y):
    vmem = pl.BlockSpec(memory_space=pltpu.VMEM)
    return pl.pallas_call(
        step2_kernel,
        in_specs=[vmem, vmem, vmem],
        out_specs=pl.BlockSpec(memory_space=pl.ANY),
        out_shape=jax.ShapeDtypeStruct((256, NDEV * SAMP), F32),
        scratch_shapes=[pltpu.VMEM((2 * PAIRW, NDEV * SAMP), F32), pltpu.SemaphoreType.DMA],
        compiler_params=pltpu.CompilerParams(vmem_limit_bytes=24 * MIB),
        cost_estimate=pl.CostEstimate(flops=2 << 30, bytes_accessed=18 * MIB, transcendentals=0),
        name="step2",
    )(norm, rot, y)


def sandwich(mixing_t, gram):
    inner = jnp.dot(
        mixing_t, gram, precision=lax.Precision.HIGHEST, preferred_element_type=F32
    )
    return lax.dot_general(
        inner,
        mixing_t,
        (((1,), (1,)), ((), ())),
        precision=lax.Precision.HIGHEST,
        preferred_element_type=F32,
    )


def grams_kernel(place_ref, rows_ref, rot1_ref, rot2_ref, out_ref):
    sums = [rows_ref[256:384], rows_ref[384:512]]
    below, above = rows_ref[512:576], rows_ref[576:608]
    shape = (HALF, PAIRW)
    left = lanes(shape) < HALF
    zero = jnp.zeros(shape, F32)

    def turn(value):
        return pltpu.roll(value, HALF, 1)

    def unpack(packed):
        return jnp.concatenate([packed, turn(packed)], 0)

    def symmetric(upper, cross, lower):
        full = jnp.concatenate([jnp.where(left, upper, cross), jnp.where(left, zero, lower)], 0)
        low_left = (lanes((PAIRW, PAIRW)) < HALF) & (
            lax.broadcasted_iota(jnp.int32, (PAIRW, PAIRW), 0) >= HALF
        )
        return jnp.where(low_left, full.T, full)

    first, last = place_ref[3] == 1, place_ref[4] == 1
    tops = [part[0:64] for part in sums]
    lows = [unpack(part[64:96]) for part in sums]
    for j in range(2):
        out_ref[0, j] = symmetric(tops[j], tops[j], lows[j]) * (1.0 / ROWS)
        packed = sums[j][96:128]
        cross = jnp.concatenate([turn(packed), packed], 0)
        if j == 0:
            upper = jnp.where(first, tops[0], below)
            lower = lows[1]
        else:
            upper = jnp.where(first, turn(lows[0]), tops[0])
            lower = jnp.where(last, turn(tops[1]), unpack(above))
        gram = symmetric(upper, cross, lower)
        for t, rot, full in ((1, rot1_ref[j], gram), (2, rot2_ref[j], rows_ref[j * PAIRW : (j + 1) * PAIRW])):
            out_ref[t, j] = sandwich(rot * scales(diagonal_row(full)), full) * (1.0 / ROWS)


def grams(place, rows, rot1, rot2):
    vmem = pl.BlockSpec(memory_space=pltpu.VMEM)
    return pl.pallas_call(
        grams_kernel,
        in_specs=[pl.BlockSpec(memory_space=pltpu.SMEM)] + [vmem] * 3,
        out_specs=vmem,
        out_shape=jax.ShapeDtypeStruct((3, 2, PAIRW, PAIRW), F32),
        compiler_params=pltpu.CompilerParams(vmem_limit_bytes=16 * MIB),
        cost_estimate=pl.CostEstimate(flops=1 << 20, bytes_accessed=2 * MIB, transcendentals=0),
        name="grams",
    )(place, rows, rot1, rot2)


def body(samples_slab, block_order, rotations):
    pair, row = lax.axis_index("pair"), lax.axis_index("row")
    core = row % 2
    z_odd = (pair // (NX * 2)) % 2
    place = jnp.stack([row, 2 * z_odd + core, core, pair == 0, pair == NDEV - 1]).astype(jnp.int32)
    even = 2 * jnp.arange(NDEV, dtype=jnp.int32)
    tab = jnp.concatenate([even + core, even + (1 - core)])
    x = samples_slab[0]
    norm0 = norms(place, x)
    copies, quarter1, turned = spread(place, rotations, norm0, exchange(norm0[1], CORE))
    rot1 = lax.all_gather(quarter1, BOTH, axis=0, tiled=True).reshape(NPAIR, PAIRW, PAIRW)
    mine = lax.all_to_all(copies, "pair", 0, 0)
    halves = prepare(x)
    mine, halves = together(mine, halves)
    theirs = exchange(mine, CORE)
    norm0 = add_over(collect(mine), YLO)
    operand, given, norm1 = step0(
        tab, block_order, place, norm0, exchange(norm0, CORE), halves, mine, theirs
    )
    kept = given[:2] + exchange(given[2:], CORE)
    norm1 = add_over(norm1, Z1, YLO)
    kept, _ = together(kept, norm1)
    quarters = [kept[0, j] + exchange(kept[1, j], flip) for j, flip in enumerate((YLO, Z1))]
    norm1 = add_over(norm1, Z3, YBOTH, X1, X3, CORE)
    payload = step1(norm1, operand, rot1, *quarters)
    arrived = lax.all_to_all(payload, "pair", 0, 0)
    sums = parts(place, arrived)
    arrived, sums = together(arrived, sums)
    below = lax.ppermute(sums[1, :HALF], "pair", [(k, k + 1) for k in range(NDEV - 1)])
    above = lax.ppermute(sums[0, 64:96], "pair", [(k + 1, k) for k in range(NDEV - 1)])
    norm2, gram = gram2(arrived)
    rows = [gram.reshape(2 * PAIRW, PAIRW), sums.reshape(2 * PAIRW, PAIRW), below, above]
    norm2 = add_over(norm2, CORE)
    rows = add_over(jnp.concatenate(rows, 0), CORE)
    norm2 = add_over(norm2, YLO)
    norm2, rows = together(norm2, rows)
    rows = add_over(rows, YLO)
    rotated = step2(norm2, turned[1], arrived)
    return rotated, grams(place, rows, turned[0], turned[1])


def solution(mesh):
    in_specs = (P("row", "pair", None), P(), P(None, "pair", None, None))
    out_specs = (P("pair", "row"), P(None, "pair", None, None))
    return jax.shard_map(body, mesh=mesh, in_specs=in_specs, out_specs=out_specs, check_vma=False)
```

time: 578 us -> 277 us (0.48); the launches traced: 568 us -> 275 us
  waiting for transfers between devices: 280 us -> 58.5 us
  matrix products: 63.7 us -> 0 us
  local copies, waits for them, and re-layouts: 67.1 us -> 9.47 us
  Pallas kernels: 0 us -> 43.8 us
  other arithmetic: 18.1 us -> 0.91 us
  starting transfers between devices: 17.4 us -> 32.8 us
  blocking collectives: 108 us -> 115 us
    ppermute x4 -> x20, waiting for transfers between devices: 177 us -> 32.9 us  [the longest x18 32.9 us: exchange(): return lax.ppermute(value, BOTH, pairs)]
    psum x3 -> x0, waiting for transfers between devices: 103 us -> none  [body(): gram_sum = lax.psum(partial_value, 'row')]
    dot_general x12 -> x0, matrix products: 63.7 us -> none  [the longest x3 32.6 us: transform(): jnp.einsum('kcd,kcr->kdr', mixing, pair_cols, precision=lax.Precision.HIG...]
    pallas_call x0 -> x10, Pallas kernels: none -> 43.8 us  [the longest x1 12.6 us: step0(): pl.pallas_call(step0_kernel, in_specs=[smem] * 3 + [vmem] * 2 + [anywhere...]
    all_to_all x0 -> x1, waiting for transfers between devices: none -> 25 us  [body(): mine = lax.all_to_all(copies, 'pair', 0, 0)]
    psum x3 -> x0, local copies, waits for them, and re-layouts: 16.6 us -> none  [body(): gram_sum = lax.psum(partial_value, 'row')]
    gather x4 -> x0, local copies, waits for them, and re-layouts: 13.2 us -> none  [the longest x1 7.69 us: body(): arranged = jnp.take(transposed, block_order, axis=0)]
    all_to_all x0 -> x1, starting transfers between devices: none -> 11.1 us  [body(): mine = lax.all_to_all(copies, 'pair', 0, 0)]
  transfers between devices with their start and end apart: 7 -> 22, of which waited for: 7 -> 14; matrix products, arithmetic and copies ran while one was open for 0% -> 0% of each run, Pallas kernels for 0% -> 11%
where the time goes in v2:
time: 277 us; the launch traced here: 275 us
  blocking collectives  115 us (42%)
  waiting for transfers between devices  58.5 us (21%)
  Pallas kernels  43.8 us (16%)
  starting transfers between devices  32.8 us (12%)
  between operations  14.3 us (5%)
  local copies, waits for them, and re-layouts  9.47 us (3%)
    all_to_all x1, blocking collectives, body(): arrived = lax.all_to_all(payload, 'pair', 0, 0)  115 us
    ppermute x18, waiting for transfers between devices, exchange(): return lax.ppermute(value, BOTH, pairs)  32.9 us
    all_to_all x1, waiting for transfers between devices, body(): mine = lax.all_to_all(copies, 'pair', 0, 0)  25 us
    ppermute x18, starting transfers between devices, exchange(): return lax.ppermute(value, BOTH, pairs)  13.4 us
    pallas_call x1, Pallas kernels, step0(): pl.pallas_call(step0_kernel, in_specs=[smem] * 3 + [vmem] * 2 + [anywhere...  12.6 us
    all_to_all x1, starting transfers between devices, body(): mine = lax.all_to_all(copies, 'pair', 0, 0)  11.1 us
    pallas_call x1, Pallas kernels, prepare(): pl.pallas_call(prepare_kernel, grid=(x.shape[1] // width,), in_specs=[pl....  9.91 us
    unnamed x14, local copies, waits for them, and re-layouts  7.82 us
  transfers between devices with their start and end apart: 22, of which 14 were waited for; matrix products, arithmetic and copies ran while one was open for 0% of the time, Pallas kernels for 11%

profile of v2, /device:TPU:2, one launch (start us, length us, event | category | flops | bytes accessed | tf_op | source)
XLA Modules:
  0.0 274.6 jit_solution(3114898491079571545)
XLA Ops:
  7.9 5.0 %norms.1.norm_ref = f32[2,32,128]{2,1,0:T(8,128)} custom-call(s32[5]{0:T(128)} %stack.31.place_ref, f32[256,8192]{1,0:T(8,128)} %bitcast.32), custom_call_target="tpu_custom_call" | custom-call | flops 8388608 | bytes 8388608 | tf_op jit(solution)/shard_map/norms/pallas_call | solution.py:127
  18.6 11.1 %all-to-all-start = ((f32[32,160,128]{2,1,0:T(8,128)}), f32[32,160,128]{2,1,0:T(8,128)S(1)}, u32[]{:S(2)}, u32[]{:S(2)}) async-start(f32[32,160,128]{2,1,0:T(8,128)} %copy-done.2), calls=%async_computation | async-start | bytes 5242880 | tf_op jit(solution)/shard_map/all_to_all | solution.py:562
  30.4 9.9 %prepare.1.halves_ref = bf16[128,2,64,256]{3,2,1,0:T(8,128)(2,1)} custom-call(f32[256,8192]{1,0:T(8,128)} %bitcast.33), custom_call_target="tpu_custom_call" | custom-call | flops 8388608 | bytes 16777216 | tf_op jit(solution)/shard_map/prepare/pallas_call | solution.py:152
  40.3 25.0 %all-to-all-done.arrived_ref.mine_ref = f32[32,160,128]{2,1,0:T(8,128)S(1)} async-done(((f32[32,160,128]{2,1,0:T(8,128)}), f32[32,160,128]{2,1,0:T(8,128)S(1)}, u32[]{:S(2)}, u32[]{:S(2)}) %all-to-all-start) | async-done | bytes 2621472 | tf_op jit(solution)/shard_map/all_to_all | solution.py:562
  66.1 3.1 %collective-permute-done.1 = f32[32,128]{1,0:T(8,128)S(1)} collective-permute-done((f32[32,128]{1,0:T(8,128)S(1)}, f32[32,128]{1,0:T(8,128)S(1)}, u32[]{:S(2)}, u32[]{:S(2)}) %collective-permute-start.1) | collective-permute-done | bytes 16416 | tf_op jit(solution)/shard_map/ppermute | solution.py:36
  70.4 12.6 %step0.1 = (bf16[64,2,2,64,256]{4,3,2,1,0:T(8,128)(2,1)}, f32[4,2,32,32,128]{4,3,2,1,0:T(8,128)S(1)}, f32[64,128]{1,0:T(8,128)S(1)}) custom-call(s32[64]{0:T(128)S(1)} %pad_add_fusion.tab_ref, s32[128]{0:T(128)S(1)} %copy-done.6, s32[5]{0:T(128)S(1)} %copy-done.5, f32[32,128]{1,0:T(8,128)S(1)} %add.75.normc_ref, ...), custom_call_target="tpu_custom_call" | custom-call | flops 4294967296 | bytes 25165824 | tf_op jit(solution)/shard_map/step0/pallas_call | solution.py:316
  83.4 3.9 %collective-permute-done.4 = f32[64,128]{1,0:T(8,128)S(1)} collective-permute-done((f32[64,128]{1,0:T(8,128)S(1)}, f32[64,128]{1,0:T(8,128)S(1)}, u32[]{:S(2)}, u32[]{:S(2)}) %collective-permute-start.4) | collective-permute-done | bytes 32800 | tf_op jit(solution)/shard_map/ppermute | solution.py:36
  88.0 3.3 %collective-permute-done.5 = f32[64,128]{1,0:T(8,128)S(1)} collective-permute-done((f32[64,128]{1,0:T(8,128)S(1)}, f32[64,128]{1,0:T(8,128)S(1)}, u32[]{:S(2)}, u32[]{:S(2)}) %collective-permute-start.5) | collective-permute-done | bytes 32800 | tf_op jit(solution)/shard_map/ppermute | solution.py:36
  93.9 3.8 %collective-permute-done.6 = f32[64,128]{1,0:T(8,128)S(1)} collective-permute-done((f32[64,128]{1,0:T(8,128)S(1)}, f32[64,128]{1,0:T(8,128)S(1)}, u32[]{:S(2)}, u32[]{:S(2)}) %collective-permute-start.6) | collective-permute-done | bytes 32800 | tf_op jit(solution)/shard_map/ppermute | solution.py:36
  97.7 2.4 collective-permute-start.7
  100.1 2.8 %collective-permute-done.7 = f32[64,128]{1,0:T(8,128)S(1)} collective-permute-done((f32[64,128]{1,0:T(8,128)S(1)}, f32[64,128]{1,0:T(8,128)S(1)}, u32[]{:S(2)}, u32[]{:S(2)}) %collective-permute-start.7) | collective-permute-done | bytes 32800 | tf_op jit(solution)/shard_map/ppermute | solution.py:36
  102.9 3.6 %collective-permute-start.8 = (f32[64,128]{1,0:T(8,128)S(1)}, f32[64,128]{1,0:T(8,128)S(1)}, u32[]{:S(2)}, u32[]{:S(2)}) collective-permute-start(f32[64,128]{1,0:T(8,128)S(1)} %add.79), channel_id=1, source_target_pairs={{0,8},{1,9},{2,10},{3,11},{4,12},{5,13},{6,14},{7,15},{8,0},{9,1},... | collective-permute-start | bytes 98312 | tf_op jit(solution)/shard_map/ppermute | solution.py:36
  106.5 2.2 collective-permute-done.8
  108.9 3.8 %collective-permute-done.9 = f32[64,128]{1,0:T(8,128)S(1)} collective-permute-done((f32[64,128]{1,0:T(8,128)S(1)}, f32[64,128]{1,0:T(8,128)S(1)}, u32[]{:S(2)}, u32[]{:S(2)}) %collective-permute-start.9) | collective-permute-done | bytes 32800 | tf_op jit(solution)/shard_map/ppermute | solution.py:36
  114.1 3.4 %copy-done = bf16[64,2,2,64,256]{4,3,2,1,0:T(8,128)(2,1)S(1)} copy-done((bf16[64,2,2,64,256]{4,3,2,1,0:T(8,128)(2,1)S(1)}, bf16[64,2,2,64,256]{4,3,2,1,0:T(8,128)(2,1)}, u32[]{:S(2)}) %copy-start) | copy-done | bytes 8388632
  119.7 4.8 %step1.1 = f32[32,288,256]{2,1,0:T(8,128)S(1)} custom-call(f32[64,128]{1,0:T(8,128)S(1)} %add.82.norm_ref, bf16[64,2,2,64,256]{4,3,2,1,0:T(8,128)(2,1)S(1)} %copy-done, f32[64,128,128]{2,1,0:T(8,128)S(1)} %bitcast.27, f32[32,32,128]{2,1,0:T(8,128)S(1)} %get-tuple-element.33.parta_ref, f32[32,32,128]{2,1,0:T(8,128)S(1)} %get-tuple-element.32.partb_ref), custom_call_target="tpu_custom_call" | custom-call | flops 3221225472 | bytes 25165824 | tf_op jit(solution)/shard_map/step1/pallas_call | solution.py:380
  124.5 114.9 %all_to_all.10.y_ref = f32[32,288,256]{2,1,0:T(8,128)S(1)} all-to-all(f32[32,288,256]{2,1,0:T(8,128)S(1)} %step1.1), channel_id=1, replica_groups=mesh['pair'=32,'row'=4] {'pair'}, dimensions={0} | all-to-all | bytes 18874368 | tf_op jit(solution)/shard_map/all_to_all | solution.py:576
  240.0 2.4 collective-permute-start.16
  242.4 5.9 %collective-permute-start.17 = (f32[32,128]{1,0:T(8,128)S(1)}, f32[32,128]{1,0:T(8,128)S(1)}, u32[]{:S(2)}, u32[]{:S(2)}) collective-permute-start(f32[32,128]{1,0:T(8,128)S(1)} %slice_bitcast_fusion.6), channel_id=1, source_target_pairs={{4,0},{8,4},{12,8},{16,12},{20,16},{24,20},{28,24},{32,28},{36,32}... | collective-permute-start | bytes 49160 | tf_op jit(solution)/shard_map/ppermute | solution.py:580
  248.3 3.0 %gram2.1 = (f32[2,8,128]{2,1,0:T(8,128)S(1)}, f32[2,128,128]{2,1,0:T(8,128)S(1)}) custom-call(f32[32,288,256]{2,1,0:T(8,128)S(1)} %all_to_all.10.y_ref), custom_call_target="tpu_custom_call" | custom-call | flops 2147483648 | bytes 10485760 | tf_op jit(solution)/shard_map/gram2/pallas_call | solution.py:446
  254.5 2.3 collective-permute-done.15
  258.3 3.8 %step2.1 = f32[256,8192]{1,0:T(8,128)} custom-call(f32[2,8,128]{2,1,0:T(8,128)S(1)} %add.87.norm_ref, f32[2,128,128]{2,1,0:T(8,128)S(1)} %get-tuple-element.37.rot_ref.rot2_ref, f32[32,288,256]{2,1,0:T(8,128)S(1)} %all_to_all.10.y_ref), custom_call_target="tpu_custom_call" | custom-call | flops 2147483648 | bytes 18874368 | tf_op jit(solution)/shard_map/step2/pallas_call | solution.py:475
  262.1 3.1 %collective-permute-done.19 = f32[608,128]{1,0:T(8,128)S(1)} collective-permute-done((f32[608,128]{1,0:T(8,128)S(1)}, f32[608,128]{1,0:T(8,128)S(1)}, u32[]{:S(2)}, u32[]{:S(2)}) %collective-permute-start.19) | collective-permute-done | bytes 311328 | tf_op jit(solution)/shard_map/ppermute | solution.py:36
  265.2 2.6 grams.1
  (70 shorter events, 22.0 us)
Async XLA Ops:
  7.9 6.9 %copy-start.5 = (s32[5]{0:T(128)S(1)}, s32[5]{0:T(128)}, u32[]{:S(2)}) copy-start(s32[5]{0:T(128)} %stack.31.place_ref) | copy-start | bytes 64
  13.6 1.2 collective-permute-start
  18.6 46.7 %all-to-all-start = ((f32[32,160,128]{2,1,0:T(8,128)}), f32[32,160,128]{2,1,0:T(8,128)S(1)}, u32[]{:S(2)}, u32[]{:S(2)}) async-start(f32[32,160,128]{2,1,0:T(8,128)} %copy-done.2), calls=%async_computation | async-start | bytes 5242880 | tf_op jit(solution)/shard_map/all_to_all | solution.py:562
  29.7 84.4 %all-gather.2.cloned.1.call-start = ((), (), s32[]{:S(2)}) async-start(), calls=%async_computation.2 | async-start | bytes 4227072 | tf_op jit(solution)/shard_map/all_gather | solution.py:561
  40.3 30.0 %copy-start.6 = (s32[128]{0:T(128)S(1)}, s32[128]{0:T(128)}, u32[]{:S(2)}) copy-start(s32[128]{0:T(128)} %order_ref.1) | copy-start | bytes 1540
  65.3 5.1 %collective-permute-start.3 = (f32[32,160,128]{2,1,0:T(8,128)S(1)}, f32[32,160,128]{2,1,0:T(8,128)}, u32[]{:S(2)}, u32[]{:S(2)}) collective-permute-start(f32[32,160,128]{2,1,0:T(8,128)S(1)} %all-to-all-done.arrived_ref.mine_ref), channel_id=1, source_target_pairs={{0,1},{1,0},{2,3},{3,2},{4,5},{5,4},{6,7},{7,6},{8,9},{9,8},{10,11... | collective-permute-start | bytes 7864328 | tf_op jit(solution)/shard_map/ppermute | solution.py:36
  65.3 3.8 %collective-permute-start.1 = (f32[32,128]{1,0:T(8,128)S(1)}, f32[32,128]{1,0:T(8,128)S(1)}, u32[]{:S(2)}, u32[]{:S(2)}) collective-permute-start(f32[32,128]{1,0:T(8,128)S(1)} %collect.1), channel_id=1, source_target_pairs={{0,2},{1,3},{2,0},{3,1},{4,6},{5,7},{6,4},{7,5},{8,10},{9,11},{10,... | collective-permute-start | bytes 49160 | tf_op jit(solution)/shard_map/ppermute | solution.py:36
  69.2 1.2 collective-permute-start.2
  83.2 8.1 %collective-permute-start.11 = (f32[2,2,32,32,128]{4,3,2,1,0:T(8,128)S(1)}, f32[2,2,32,32,128]{4,3,2,1,0:T(8,128)S(1)}, u32[]{:S(2)}, u32[]{:S(2)}) collective-permute-start(f32[2,2,32,32,128]{4,3,2,1,0:T(8,128)S(1)} %slice.36), channel_id=1, source_target_pairs={{0,1},{1,0},{2,3},{3,2},{4,5},{5,4},{6,7},{7,6},{8,9},{9,8},{10,11... | collective-permute-start | bytes 6291464 | tf_op jit(solution)/shard_map/ppermute | solution.py:36
  83.4 3.9 %collective-permute-start.4 = (f32[64,128]{1,0:T(8,128)S(1)}, f32[64,128]{1,0:T(8,128)S(1)}, u32[]{:S(2)}, u32[]{:S(2)}) collective-permute-start(f32[64,128]{1,0:T(8,128)S(1)} %get-tuple-element.20), channel_id=1, source_target_pairs={{0,32},{1,33},{2,34},{3,35},{4,36},{5,37},{6,38},{7,39},{8,40},{9,... | collective-permute-start | bytes 98312 | tf_op jit(solution)/shard_map/ppermute | solution.py:36
  87.3 3.9 %collective-permute-start.5 = (f32[64,128]{1,0:T(8,128)S(1)}, f32[64,128]{1,0:T(8,128)S(1)}, u32[]{:S(2)}, u32[]{:S(2)}) collective-permute-start(f32[64,128]{1,0:T(8,128)S(1)} %add.76), channel_id=1, source_target_pairs={{0,2},{1,3},{2,0},{3,1},{4,6},{5,7},{6,4},{7,5},{8,10},{9,11},{10,... | collective-permute-start | bytes 98312 | tf_op jit(solution)/shard_map/ppermute | solution.py:36
  91.8 22.0 %collective-permute-start.12 = (f32[32,32,128]{2,1,0:T(8,128)S(1)}, f32[32,32,128]{2,1,0:T(8,128)S(1)}, u32[]{:S(2)}, u32[]{:S(2)}) collective-permute-start(f32[32,32,128]{2,1,0:T(8,128)S(1)} %get-tuple-element.35), channel_id=1, source_target_pairs={{0,2},{1,3},{2,0},{3,1},{4,6},{5,7},{6,4},{7,5},{8,10},{9,11},{10,... | collective-permute-start | bytes 1572872 | tf_op jit(solution)/shard_map/ppermute | solution.py:36
  92.6 21.3 %collective-permute-start.13 = (f32[32,32,128]{2,1,0:T(8,128)S(1)}, f32[32,32,128]{2,1,0:T(8,128)S(1)}, u32[]{:S(2)}, u32[]{:S(2)}) collective-permute-start(f32[32,32,128]{2,1,0:T(8,128)S(1)} %get-tuple-element.34), channel_id=1, source_target_pairs={{0,32},{1,33},{2,34},{3,35},{4,36},{5,37},{6,38},{7,39},{8,40},{9,... | collective-permute-start | bytes 1572872 | tf_op jit(solution)/shard_map/ppermute | solution.py:36
  92.6 5.1 %collective-permute-start.6 = (f32[64,128]{1,0:T(8,128)S(1)}, f32[64,128]{1,0:T(8,128)S(1)}, u32[]{:S(2)}, u32[]{:S(2)}) collective-permute-start(f32[64,128]{1,0:T(8,128)S(1)} %add.77), channel_id=1, source_target_pairs={{0,96},{1,97},{2,98},{3,99},{4,100},{5,101},{6,102},{7,103},{8,104... | collective-permute-start | bytes 98312 | tf_op jit(solution)/shard_map/ppermute | solution.py:36
  97.7 5.2 %collective-permute-start.7 = (f32[64,128]{1,0:T(8,128)S(1)}, f32[64,128]{1,0:T(8,128)S(1)}, u32[]{:S(2)}, u32[]{:S(2)}) collective-permute-start(f32[64,128]{1,0:T(8,128)S(1)} %add.78), channel_id=1, source_target_pairs={{0,6},{1,7},{2,4},{3,5},{4,2},{5,3},{6,0},{7,1},{8,14},{9,15},{10,... | collective-permute-start | bytes 98312 | tf_op jit(solution)/shard_map/ppermute | solution.py:36
  102.9 5.8 %collective-permute-start.8 = (f32[64,128]{1,0:T(8,128)S(1)}, f32[64,128]{1,0:T(8,128)S(1)}, u32[]{:S(2)}, u32[]{:S(2)}) collective-permute-start(f32[64,128]{1,0:T(8,128)S(1)} %add.79), channel_id=1, source_target_pairs={{0,8},{1,9},{2,10},{3,11},{4,12},{5,13},{6,14},{7,15},{8,0},{9,1},... | collective-permute-start | bytes 98312 | tf_op jit(solution)/shard_map/ppermute | solution.py:36
  108.7 3.9 %collective-permute-start.9 = (f32[64,128]{1,0:T(8,128)S(1)}, f32[64,128]{1,0:T(8,128)S(1)}, u32[]{:S(2)}, u32[]{:S(2)}) collective-permute-start(f32[64,128]{1,0:T(8,128)S(1)} %add.80), channel_id=1, source_target_pairs={{0,24},{1,25},{2,26},{3,27},{4,28},{5,29},{6,30},{7,31},{8,16},{9,... | collective-permute-start | bytes 98312 | tf_op jit(solution)/shard_map/ppermute | solution.py:36
  112.7 1.2 collective-permute-start.10
  240.0 11.3 %collective-permute-start.16 = (f32[64,128]{1,0:T(8,128)S(1)}, f32[64,128]{1,0:T(8,128)S(1)}, u32[]{:S(2)}, u32[]{:S(2)}) collective-permute-start(f32[64,128]{1,0:T(8,128)S(1)} %slice_bitcast_fusion.4), channel_id=1, source_target_pairs={{0,4},{4,8},{8,12},{12,16},{16,20},{20,24},{24,28},{28,32},{32,36}... | collective-permute-start | bytes 98312 | tf_op jit(solution)/shard_map/ppermute | solution.py:579
  242.4 8.9 %collective-permute-start.17 = (f32[32,128]{1,0:T(8,128)S(1)}, f32[32,128]{1,0:T(8,128)S(1)}, u32[]{:S(2)}, u32[]{:S(2)}) collective-permute-start(f32[32,128]{1,0:T(8,128)S(1)} %slice_bitcast_fusion.6), channel_id=1, source_target_pairs={{4,0},{8,4},{12,8},{16,12},{20,16},{24,20},{28,24},{32,28},{36,32}... | collective-permute-start | bytes 49160 | tf_op jit(solution)/shard_map/ppermute | solution.py:580
  251.3 5.5 %collective-permute-start.18 = (f32[608,128]{1,0:T(8,128)S(1)}, f32[608,128]{1,0:T(8,128)S(1)}, u32[]{:S(2)}, u32[]{:S(2)}) collective-permute-start(f32[608,128]{1,0:T(8,128)S(1)} %pad_maximum_fusion), channel_id=1, source_target_pairs={{0,1},{1,0},{2,3},{3,2},{4,5},{5,4},{6,7},{7,6},{8,9},{9,8},{10,11... | collective-permute-start | bytes 933896 | tf_op jit(solution)/shard_map/ppermute | solution.py:36
  251.6 1.6 collective-permute-start.14
  253.2 3.7 %collective-permute-start.15 = (f32[2,8,128]{2,1,0:T(8,128)S(1)}, f32[2,8,128]{2,1,0:T(8,128)S(1)}, u32[]{:S(2)}, u32[]{:S(2)}) collective-permute-start(f32[2,8,128]{2,1,0:T(8,128)S(1)} %add.86), channel_id=1, source_target_pairs={{0,2},{1,3},{2,0},{3,1},{4,6},{5,7},{6,4},{7,5},{8,10},{9,11},{10,... | collective-permute-start | bytes 24584 | tf_op jit(solution)/shard_map/ppermute | solution.py:36
  256.9 8.3 %collective-permute-start.19 = (f32[608,128]{1,0:T(8,128)S(1)}, f32[608,128]{1,0:T(8,128)S(1)}, u32[]{:S(2)}, u32[]{:S(2)}) collective-permute-start(f32[608,128]{1,0:T(8,128)S(1)} %fusion.2), channel_id=1, source_target_pairs={{0,2},{1,3},{2,0},{3,1},{4,6},{5,7},{6,4},{7,5},{8,10},{9,11},{10,... | collective-permute-start | bytes 933896 | tf_op jit(solution)/shard_map/ppermute | solution.py:36
  (5 other events, 14.7 us)
Sparse Core Ops, SparseCore 0:
  34.2 77.5 all-gather.1

commit v3 on v2

--- a/solution.py
+++ b/solution.py
@@ -18,7 +18,7 @@
 NDEV = 32
 ROWS = 32768
 EPS = 1e-06
-QUARTER = 32
+QUARTER = 24
 PAYROWS = 256 + QUARTER
 MIB = 1 << 20
 F32, BF16 = jnp.float32, jnp.bfloat16
@@ -96,6 +96,11 @@
     return lax.broadcasted_iota(jnp.int32, shape, 1)
 
 
+def upper_or_diagonal(rows=HALF):
+    shape = (rows, PAIRW)
+    return lax.broadcasted_iota(jnp.int32, shape, 0) <= lanes(shape)
+
+
 def next_slots(i):
     upper = jnp.where(i == 0, 0, jnp.where(i == NPAIR - 1, 2 * NPAIR - 1, 2 * i + 2))
     lower = jnp.where(i == 0, 2, 2 * i - 1)
@@ -105,7 +110,10 @@
 TILES = NPAIR // 2
 
 
-def norms_kernel(place_ref, x_ref, norm_ref, held_ref, sems):
+def norms_kernel(
+    place_ref, x_ref, rotations_ref, keep_ref, give_ref, own_ref, quarter_ref, turned_ref,
+    held_ref, rot_ref, rows_ref, sems, rot_sem
+):
     count = sems.shape[0]
     width = NPAIR // count
 
@@ -113,27 +121,54 @@
         part = pl.ds(g * width * PAIRW, width * PAIRW)
         return pltpu.make_async_copy(x_ref.at[:, part], held_ref.at[:, part], sems.at[g])
 
+    rot_copy = pltpu.make_async_copy(rotations_ref, rot_ref, rot_sem)
+    rot_copy.start()
     for g in range(count):
         copy(g).start()
+    row, core = place_ref[0], place_ref[2]
+    rot_copy.wait()
+    own_ref[...] = rot_ref[0, core].T
+    for t in range(1, 3):
+        for j in range(2):
+            turned_ref[t - 1, j] = rot_ref[t, j].T
+    half = pl.ds(pl.multiple_of((row % 2) * HALF, HALF), HALF)
+    quarter_ref[...] = turned_ref[0, row // 2, half, :]
     for g in range(count):
         copy(g).wait()
         for t in range(width * g, width * (g + 1)):
             tile = held_ref[:, t * PAIRW : (t + 1) * PAIRW]
-            row = jnp.sum(tile * tile, axis=0, keepdims=True)
-            norm_ref[(t // TILES) ^ place_ref[2], t % TILES : t % TILES + 1, :] = row
-
-
-def norms(place, x):
+            rows_ref[t // TILES, t % TILES : t % TILES + 1, :] = jnp.sum(
+                tile * tile, axis=0, keepdims=True
+            )
+    keep_ref[...] = rows_ref[core]
+    give_ref[...] = rows_ref[1 - core]
+
+
+def norms(place, x, rotations):
+    vmem = pl.BlockSpec(memory_space=pltpu.VMEM)
+    hbm = pl.BlockSpec(memory_space=pltpu.HBM)
     return pl.pallas_call(
         norms_kernel,
-        in_specs=[pl.BlockSpec(memory_space=pltpu.SMEM), pl.BlockSpec(memory_space=pl.ANY)],
-        out_specs=pl.BlockSpec(memory_space=pltpu.VMEM),
-        out_shape=jax.ShapeDtypeStruct((2, TILES, PAIRW), F32),
-        scratch_shapes=[pltpu.VMEM((SAMP, NPAIR * PAIRW), F32), pltpu.SemaphoreType.DMA((8,))],
+        in_specs=[pl.BlockSpec(memory_space=pltpu.SMEM), hbm, hbm],
+        out_specs=[vmem] * 5,
+        out_shape=[
+            jax.ShapeDtypeStruct((TILES, PAIRW), F32),
+            jax.ShapeDtypeStruct((TILES, PAIRW), F32),
+            jax.ShapeDtypeStruct((PAIRW, PAIRW), F32),
+            jax.ShapeDtypeStruct((HALF, PAIRW), F32),
+            jax.ShapeDtypeStruct((2, 2, PAIRW, PAIRW), F32),
+        ],
+        scratch_shapes=[
+            pltpu.VMEM((SAMP, NPAIR * PAIRW), F32),
+            pltpu.VMEM((3, 2, PAIRW, PAIRW), F32),
+            pltpu.VMEM((2, TILES, PAIRW), F32),
+            pltpu.SemaphoreType.DMA((8,)),
+            pltpu.SemaphoreType.DMA,
+        ],
         compiler_params=pltpu.CompilerParams(vmem_limit_bytes=58 * MIB),
         cost_estimate=pl.CostEstimate(flops=8 * MIB, bytes_accessed=8 * MIB, transcendentals=0),
         name="norms",
-    )(place, x)
+    )(place, x, rotations)
 
 
 def prepare_kernel(x_ref, halves_ref):
@@ -156,7 +191,7 @@
         out_specs=pl.BlockSpec((blocks, 2, HALF, SAMP), lambda g: (g, 0, 0, 0)),
         out_shape=jax.ShapeDtypeStruct((2 * NPAIR, 2, HALF, SAMP), BF16),
         compiler_params=pltpu.CompilerParams(vmem_limit_bytes=58 * MIB),
-        cost_estimate=pl.CostEstimate(flops=8 * MIB, bytes_accessed=16 * MIB, transcendentals=0),
+        cost_estimate=pl.CostEstimate(flops=MIB, bytes_accessed=MIB // 8, transcendentals=0),
         name="prepare",
     )(x)
 
@@ -164,10 +199,9 @@
 SENT = PAIRW + TILES
 
 
-def spread_kernel(place_ref, rot_ref, norm_ref, given_ref, copies_ref, quarter_ref, turned_ref):
-    row, core = place_ref[0], place_ref[2]
-    own = rot_ref[0, core].T
-    norm = norm_ref[0] + given_ref[...]
+def spread_kernel(own_ref, norm_ref, given_ref, copies_ref):
+    own = own_ref[...]
+    norm = norm_ref[...] + given_ref[...]
 
     def copy(k, carry):
         copies_ref[k, :PAIRW] = own
@@ -175,28 +209,19 @@
         return carry
 
     lax.fori_loop(0, NDEV, copy, 0, unroll=4)
-    for t in range(1, 3):
-        for j in range(2):
-            turned_ref[t - 1, j] = rot_ref[t, j].T
-    half = pl.ds(pl.multiple_of((row % 2) * HALF, HALF), HALF)
-    quarter_ref[...] = turned_ref[0, row // 2, half, :]
-
-
-def spread(place, rotations, norm, given):
+
+
+def spread(own, norm, given):
     vmem = pl.BlockSpec(memory_space=pltpu.VMEM)
     return pl.pallas_call(
         spread_kernel,
-        in_specs=[pl.BlockSpec(memory_space=pltpu.SMEM), vmem, vmem, vmem],
-        out_specs=[vmem] * 3,
-        out_shape=[
-            jax.ShapeDtypeStruct((NDEV, SENT, PAIRW), F32),
-            jax.ShapeDtypeStruct((HALF, PAIRW), F32),
-            jax.ShapeDtypeStruct((2, 2, PAIRW, PAIRW), F32),
-        ],
-        compiler_params=pltpu.CompilerParams(vmem_limit_bytes=8 * MIB),
-        cost_estimate=pl.CostEstimate(flops=MIB, bytes_accessed=3 * MIB, transcendentals=0),
+        in_specs=[vmem] * 3,
+        out_specs=vmem,
+        out_shape=jax.ShapeDtypeStruct((NDEV, SENT, PAIRW), F32),
+        compiler_params=pltpu.CompilerParams(vmem_limit_bytes=58 * MIB),
+        cost_estimate=pl.CostEstimate(flops=MIB, bytes_accessed=MIB // 8, transcendentals=0),
         name="spread",
-    )(place, rotations, norm, given)
+    )(own, norm, given)
 
 
 def collect_kernel(arrived_ref, norm_ref):
@@ -211,7 +236,7 @@
         out_specs=vmem,
         out_shape=jax.ShapeDtypeStruct((TILES, PAIRW), F32),
         compiler_params=pltpu.CompilerParams(vmem_limit_bytes=8 * MIB),
-        cost_estimate=pl.CostEstimate(flops=MIB, bytes_accessed=MIB, transcendentals=0),
+        cost_estimate=pl.CostEstimate(flops=MIB, bytes_accessed=MIB // 8, transcendentals=0),
         name="collect",
     )(arrived)
 
@@ -219,6 +244,7 @@
 GROUP = 8
 GROUPS = NPAIR // GROUP
 OPERAND = (NPAIR, 2, 2, HALF, SAMP)
+ROOM = 4
 
 
 def whole_copy(ref, sem):
@@ -230,18 +256,21 @@
     next_ref, parts_ref, onorm_ref, right_ref, rot_ref, moved_ref, norms_ref, sems, out_sem
 ):
 
-    def fetch(q, carry):
-        i = tab_ref[q]
-        for h in range(2):
-            pltpu.make_async_copy(
-                halves_ref.at[order_ref[2 * i + h]], right_ref.at[q, :, h], sems.at[0, q // GROUP]
-            ).start()
-        return carry
-
-    lax.fori_loop(0, NPAIR, fetch, 0)
     for k in range(GROUPS):
         piece = (mine_ref, given_ref)[k // 4].at[pl.ds(GROUP * (k % 4), GROUP), pl.ds(0, PAIRW)]
         pltpu.make_async_copy(piece, rot_ref.at[pl.ds(GROUP * k, GROUP)], sems.at[1, k]).start()
+
+    def fetch(g):
+        for k in range(GROUP):
+            q = GROUP * g + k
+            i = tab_ref[q]
+            for h in range(2):
+                pltpu.make_async_copy(
+                    halves_ref.at[order_ref[2 * i + h]], right_ref.at[q, :, h], sems.at[0, g]
+                ).start()
+
+    for g in range(GROUPS):
+        fetch(g)
     core = place_ref[2]
     for half, norm_ref in ((core, normc_ref), (1 - core, normo_ref)):
         rows = pl.ds(pl.multiple_of(half * TILES, TILES), TILES)
@@ -277,18 +306,17 @@
         for i, (high, low) in zip(index, values):
             gram = self_gram(jnp.concatenate([high, low], 0))
             onorm_ref[pl.ds(i, 1), :] = diagonal_row(gram)
-            bottom = gram[HALF:]
-            packed = jnp.where(
-                lanes((32, PAIRW)) >= HALF, bottom[:32], pltpu.roll(bottom[32:], HALF, 1)
-            )
+            both = jnp.where(upper_or_diagonal(), gram[:HALF], pltpu.roll(gram[HALF:], HALF, 1))
+            both = jnp.where(lanes((HALF, PAIRW)) < HALF, both, gram[:HALF])
             p, j = i // 2, i % 2
-            parts_ref[spot(0, j), j, p] = gram[:32]
-            parts_ref[spot(1, j), j, p] = gram[32:HALF]
-            parts_ref[spot(2, j), j, p] = packed
+            parts_ref[spot(0, j), j, p] = both[0:24]
+            parts_ref[spot(1, j), j, p] = both[24:48]
+            parts_ref[spot(2, j), j, p, 0:16] = both[48:64]
         return carry
 
     lax.fori_loop(0, GROUPS, group, 0)
-    copy = pltpu.make_async_copy(moved_ref, next_ref, out_sem)
+
+    copy = pltpu.make_async_copy(moved_ref, next_ref.at[pl.ds(0, NPAIR)], out_sem)
     copy.start()
 
     def cross(g, carry):
@@ -300,9 +328,10 @@
         for k, wide in enumerate(wides):
             folded = wide[:HALF] + wide[HALF:]
             folded = folded + pltpu.roll(folded, HALF, 1)
-            parts_ref[spot(3, k % 2), k % 2, GROUP // 2 * g + k // 2] = jnp.where(
-                lanes((32, PAIRW)) < HALF, folded[:32], folded[32:]
-            )
+            packed = jnp.where(lanes((32, PAIRW)) < HALF, folded[:32], folded[32:])
+            p, j = GROUP // 2 * g + k // 2, k % 2
+            parts_ref[spot(2, j), j, p, 16:24] = packed[:8]
+            parts_ref[spot(3, j), j, p] = packed[8:]
         return carry
 
     lax.fori_loop(0, GROUPS, cross, 0)
@@ -312,13 +341,13 @@
 def step0(tab, order, place, normc, normo, halves, mine, given):
     smem = pl.BlockSpec(memory_space=pltpu.SMEM)
     vmem = pl.BlockSpec(memory_space=pltpu.VMEM)
-    anywhere = pl.BlockSpec(memory_space=pl.ANY)
+    hbm = pl.BlockSpec(memory_space=pltpu.HBM)
     return pl.pallas_call(
         step0_kernel,
-        in_specs=[smem] * 3 + [vmem] * 2 + [anywhere] * 3,
-        out_specs=[anywhere, vmem, vmem],
+        in_specs=[smem] * 3 + [vmem] * 2 + [hbm] * 3,
+        out_specs=[hbm, vmem, vmem],
         out_shape=[
-            jax.ShapeDtypeStruct(OPERAND, BF16),
+            jax.ShapeDtypeStruct((ROOM * NPAIR,) + OPERAND[1:], BF16),
             jax.ShapeDtypeStruct((4, 2, NDEV, QUARTER, PAIRW), F32),
             jax.ShapeDtypeStruct((NPAIR, PAIRW), F32),
         ],
@@ -331,28 +360,24 @@
             pltpu.SemaphoreType.DMA,
         ],
         compiler_params=pltpu.CompilerParams(vmem_limit_bytes=44 * MIB),
-        cost_estimate=pl.CostEstimate(flops=4 << 30, bytes_accessed=24 * MIB, transcendentals=0),
+        cost_estimate=pl.CostEstimate(flops=MIB, bytes_accessed=MIB // 8, transcendentals=0),
         name="step0",
     )(tab, order, place, normc, normo, halves, mine, given)
 
 
 def step1_kernel(
-    norm_ref, operand_ref, rotation_ref, parta_ref, partb_ref, pay_ref, right_ref, rot_ref,
-    norms_ref, sems
+    norm_ref, operand_ref, rot_ref, parta_ref, partb_ref, pay_ref, right_ref, norms_ref, sems
 ):
     for g in range(GROUPS):
         part = pl.ds(GROUP * g, GROUP)
-        pltpu.make_async_copy(operand_ref.at[part], right_ref.at[part], sems.at[0, g]).start()
-        pltpu.make_async_copy(rotation_ref.at[part], rot_ref.at[part], sems.at[1, g]).start()
+        pltpu.make_async_copy(operand_ref.at[part], right_ref.at[part], sems.at[g]).start()
     norms_ref[0] = norm_ref[...]
     norms_ref[1] = pltpu.roll(norm_ref[...], HALF, 1)
     pay_ref[:, 256:PAYROWS, :PAIRW] = parta_ref[...]
     pay_ref[:, 256:PAYROWS, PAIRW:] = partb_ref[...]
 
     def group(g, carry):
-        part = pl.ds(GROUP * g, GROUP)
-        whole_copy(right_ref.at[part], sems.at[0, g]).wait()
-        whole_copy(rot_ref.at[part], sems.at[1, g]).wait()
+        whole_copy(right_ref.at[pl.ds(GROUP * g, GROUP)], sems.at[g]).wait()
         index = [GROUP * g + k for k in range(GROUP)]
         lefts = []
         for i in index:
@@ -376,19 +401,17 @@
 
 def step1(norm, operand, rot, parta, partb):
     vmem = pl.BlockSpec(memory_space=pltpu.VMEM)
-    anywhere = pl.BlockSpec(memory_space=pl.ANY)
     return pl.pallas_call(
         step1_kernel,
-        in_specs=[vmem, anywhere, anywhere, vmem, vmem],
+        in_specs=[vmem, pl.BlockSpec(memory_space=pltpu.HBM), vmem, vmem, vmem],
         out_specs=vmem,
         out_shape=jax.ShapeDtypeStruct((NDEV, PAYROWS, SAMP), F32),
         scratch_shapes=[
             pltpu.VMEM(OPERAND, BF16),
-            pltpu.VMEM((NPAIR, PAIRW, PAIRW), F32),
             pltpu.VMEM((2, NPAIR, PAIRW), F32),
-            pltpu.SemaphoreType.DMA((2, GROUPS)),
+            pltpu.SemaphoreType.DMA((GROUPS,)),
         ],
-        compiler_params=pltpu.CompilerParams(vmem_limit_bytes=28 * MIB),
+        compiler_params=pltpu.CompilerParams(vmem_limit_bytes=34 * MIB),
         cost_estimate=pl.CostEstimate(flops=3 << 30, bytes_accessed=24 * MIB, transcendentals=0),
         name="step1",
     )(norm, operand, rot, parta, partb)
@@ -434,11 +457,13 @@
             low = jnp.concatenate([l for _, l in halves], 1)
             term = outer(high, jnp.concatenate([high, low], 0))
             totals[j] = term if g == 0 else totals[j] + term
+    both = []
     for j in range(2):
         mixed = totals[j][:, PAIRW:]
         gram = totals[j][:, :PAIRW] + mixed + mixed.T
-        gram_ref[j] = gram
+        both.append(gram)
         norm_ref[j] = jnp.broadcast_to(diagonal_row(gram), (8, PAIRW))
+    gram_ref[...] = jnp.where(upper_or_diagonal(PAIRW), both[0], both[1])
 
 
 def gram2(y):
@@ -449,7 +474,7 @@
         out_specs=[vmem, vmem],
         out_shape=[
             jax.ShapeDtypeStruct((2, 8, PAIRW), F32),
-            jax.ShapeDtypeStruct((2, PAIRW, PAIRW), F32),
+            jax.ShapeDtypeStruct((PAIRW, PAIRW), F32),
         ],
         compiler_params=pltpu.CompilerParams(vmem_limit_bytes=14 * MIB),
         cost_estimate=pl.CostEstimate(flops=2 << 30, bytes_accessed=10 * MIB, transcendentals=0),
@@ -485,80 +510,91 @@
 
 
 def sandwich(mixing_t, gram):
-    inner = jnp.dot(
-        mixing_t, gram, precision=lax.Precision.HIGHEST, preferred_element_type=F32
-    )
-    return lax.dot_general(
-        inner,
-        mixing_t,
-        (((1,), (1,)), ((), ())),
-        precision=lax.Precision.HIGHEST,
-        preferred_element_type=F32,
-    )
-
-
-def grams_kernel(place_ref, rows_ref, rot1_ref, rot2_ref, out_ref):
-    sums = [rows_ref[256:384], rows_ref[384:512]]
-    below, above = rows_ref[512:576], rows_ref[576:608]
+    left = left_operand(mixing_t)
+    inner = product(left, jnp.concatenate(split(gram), 0))
+    turned = product(left, jnp.concatenate(split(inner.T), 0))
+    return turned.T
+
+
+def grams_kernel(place_ref, norm_ref, norm2_ref, rows_ref, rot1_ref, rot2_ref, out_ref):
     shape = (HALF, PAIRW)
     left = lanes(shape) < HALF
     zero = jnp.zeros(shape, F32)
+    keeps = upper_or_diagonal()
+    eye = lax.broadcasted_iota(jnp.int32, shape, 0) == lanes(shape)
 
     def turn(value):
         return pltpu.roll(value, HALF, 1)
 
-    def unpack(packed):
-        return jnp.concatenate([packed, turn(packed)], 0)
+    def blocks(both, norm_row):
+        other = jnp.concatenate([jnp.where(left, both, zero), zero], 0).T[:HALF]
+        lower = jnp.where(keeps, other, both)
+        return jnp.where(keeps, both, other), jnp.where(eye, turn(norm_row), lower)
 
     def symmetric(upper, cross, lower):
-        full = jnp.concatenate([jnp.where(left, upper, cross), jnp.where(left, zero, lower)], 0)
+        full = jnp.concatenate(
+            [jnp.where(left, upper, cross), jnp.where(left, zero, turn(lower))], 0
+        )
         low_left = (lanes((PAIRW, PAIRW)) < HALF) & (
             lax.broadcasted_iota(jnp.int32, (PAIRW, PAIRW), 0) >= HALF
         )
         return jnp.where(low_left, full.T, full)
 
+    p = place_ref[5]
     first, last = place_ref[3] == 1, place_ref[4] == 1
-    tops = [part[0:64] for part in sums]
-    lows = [unpack(part[64:96]) for part in sums]
+    sums = [rows_ref[128:224], rows_ref[224:320]]
+    square = rows_ref[:PAIRW]
+    above_diagonal = upper_or_diagonal(PAIRW)
+    on_diagonal = lax.broadcasted_iota(jnp.int32, square.shape, 0) == lanes(square.shape)
+    step2_grams = [
+        jnp.where(above_diagonal, square, square.T),
+        jnp.where(on_diagonal, norm2_ref[1, 0:1], jnp.where(above_diagonal, square.T, square)),
+    ]
+
+    def norm_row(i):
+        return norm_ref[pl.ds(i, 1), :]
+
+    own = [blocks(sums[j][:HALF], norm_row(2 * p + j)) for j in range(2)]
+    below = blocks(rows_ref[320:384], norm_row(2 * p))[0]
+    above = blocks(rows_ref[384:448], norm_row(jnp.minimum(2 * p + 2, NPAIR - 1)))[1]
+    uppers = [jnp.where(first, own[0][0], below), jnp.where(first, own[0][1], own[0][0])]
+    lowers = [own[1][1], jnp.where(last, own[1][0], above)]
     for j in range(2):
-        out_ref[0, j] = symmetric(tops[j], tops[j], lows[j]) * (1.0 / ROWS)
-        packed = sums[j][96:128]
-        cross = jnp.concatenate([turn(packed), packed], 0)
-        if j == 0:
-            upper = jnp.where(first, tops[0], below)
-            lower = lows[1]
-        else:
-            upper = jnp.where(first, turn(lows[0]), tops[0])
-            lower = jnp.where(last, turn(tops[1]), unpack(above))
-        gram = symmetric(upper, cross, lower)
-        for t, rot, full in ((1, rot1_ref[j], gram), (2, rot2_ref[j], rows_ref[j * PAIRW : (j + 1) * PAIRW])):
+        out_ref[0, j] = symmetric(own[j][0], sums[j][:HALF], own[j][1]) * (1.0 / ROWS)
+        packed = sums[j][HALF:]
+        gram = symmetric(uppers[j], jnp.concatenate([turn(packed), packed], 0), lowers[j])
+        for t, rot, full in (
+            (1, rot1_ref[j], gram), (2, rot2_ref[j], step2_grams[j])
+        ):
             out_ref[t, j] = sandwich(rot * scales(diagonal_row(full)), full) * (1.0 / ROWS)
 
 
-def grams(place, rows, rot1, rot2):
+def grams(place, norm, norm2, rows, rot1, rot2):
     vmem = pl.BlockSpec(memory_space=pltpu.VMEM)
     return pl.pallas_call(
         grams_kernel,
-        in_specs=[pl.BlockSpec(memory_space=pltpu.SMEM)] + [vmem] * 3,
+        in_specs=[pl.BlockSpec(memory_space=pltpu.SMEM)] + [vmem] * 5,
         out_specs=vmem,
         out_shape=jax.ShapeDtypeStruct((3, 2, PAIRW, PAIRW), F32),
         compiler_params=pltpu.CompilerParams(vmem_limit_bytes=16 * MIB),
         cost_estimate=pl.CostEstimate(flops=1 << 20, bytes_accessed=2 * MIB, transcendentals=0),
         name="grams",
-    )(place, rows, rot1, rot2)
+    )(place, norm, norm2, rows, rot1, rot2)
 
 
 def body(samples_slab, block_order, rotations):
     pair, row = lax.axis_index("pair"), lax.axis_index("row")
     core = row % 2
     z_odd = (pair // (NX * 2)) % 2
-    place = jnp.stack([row, 2 * z_odd + core, core, pair == 0, pair == NDEV - 1]).astype(jnp.int32)
+    place = jnp.stack(
+        [row, 2 * z_odd + core, core, pair == 0, pair == NDEV - 1, pair]
+    ).astype(jnp.int32)
     even = 2 * jnp.arange(NDEV, dtype=jnp.int32)
     tab = jnp.concatenate([even + core, even + (1 - core)])
     x = samples_slab[0]
-    norm0 = norms(place, x)
-    copies, quarter1, turned = spread(place, rotations, norm0, exchange(norm0[1], CORE))
+    norm0, give, own0, quarter1, turned = norms(place, x, rotations)
     rot1 = lax.all_gather(quarter1, BOTH, axis=0, tiled=True).reshape(NPAIR, PAIRW, PAIRW)
+    copies = spread(own0, norm0, exchange(give, CORE))
     mine = lax.all_to_all(copies, "pair", 0, 0)
     halves = prepare(x)
     mine, halves = together(mine, halves)
@@ -577,16 +613,16 @@
     sums = parts(place, arrived)
     arrived, sums = together(arrived, sums)
     below = lax.ppermute(sums[1, :HALF], "pair", [(k, k + 1) for k in range(NDEV - 1)])
-    above = lax.ppermute(sums[0, 64:96], "pair", [(k + 1, k) for k in range(NDEV - 1)])
+    above = lax.ppermute(sums[0, :HALF], "pair", [(k + 1, k) for k in range(NDEV - 1)])
     norm2, gram = gram2(arrived)
-    rows = [gram.reshape(2 * PAIRW, PAIRW), sums.reshape(2 * PAIRW, PAIRW), below, above]
     norm2 = add_over(norm2, CORE)
+    rows = [gram, sums.reshape(8 * QUARTER, PAIRW), below, above]
     rows = add_over(jnp.concatenate(rows, 0), CORE)
     norm2 = add_over(norm2, YLO)
     norm2, rows = together(norm2, rows)
     rows = add_over(rows, YLO)
     rotated = step2(norm2, turned[1], arrived)
-    return rotated, grams(place, rows, turned[0], turned[1])
+    return rotated, grams(place, norm1, norm2, rows, turned[0], turned[1])
 
 
 def solution(mesh):

time: 277 us -> 268 us (0.968)
  local copies, waits for them, and re-layouts: 9.47 us -> 3.57 us
    unnamed x14 -> x10, local copies, waits for them, and re-layouts: 7.82 us -> 2.79 us
  transfers between devices with their start and end apart: 22 -> 22, of which waited for: 14 -> 14; matrix products, arithmetic and copies ran while one was open for 0% -> 0% of each run, Pallas kernels for 11% -> 12%
where the time goes in v3:
time: 268 us; the launch traced here: 266 us
  blocking collectives  113 us (42%)
  waiting for transfers between devices  57.5 us (21%)
  Pallas kernels  45.8 us (17%)
  starting transfers between devices  31.3 us (12%)
  between operations  14.3 us (5%)
  local copies, waits for them, and re-layouts  3.57 us (1%)
    all_to_all x1, blocking collectives, body(): arrived = lax.all_to_all(payload, 'pair', 0, 0)  113 us
    ppermute x18, waiting for transfers between devices, exchange(): return lax.ppermute(value, BOTH, pairs)  31.7 us
    all_to_all x1, waiting for transfers between devices, body(): mine = lax.all_to_all(copies, 'pair', 0, 0)  25.8 us
    pallas_call x1, Pallas kernels, step0(): pl.pallas_call(step0_kernel, in_specs=[smem] * 3 + [vmem] * 2 + [hbm] * 3...  13.1 us
    ppermute x18, starting transfers between devices, exchange(): return lax.ppermute(value, BOTH, pairs)  11.8 us
    all_to_all x1, starting transfers between devices, body(): mine = lax.all_to_all(copies, 'pair', 0, 0)  11.1 us
    pallas_call x1, Pallas kernels, prepare(): pl.pallas_call(prepare_kernel, grid=(x.shape[1] // width,), in_specs=[pl....  9.91 us
    ppermute x1, starting transfers between devices, body(): lax.ppermute(sums[0, :HALF], 'pair', [(k + 1, k) for k in range(NDEV - 1)])  5.94 us
  transfers between devices with their start and end apart: 22, of which 14 were waited for; matrix products, arithmetic and copies ran while one was open for 0% of the time, Pallas kernels for 12%

profile of v3, /device:TPU:2, one launch (start us, length us, event | category | flops | bytes accessed | tf_op | source)
XLA Modules:
  0.0 265.9 jit_solution(2002601731190659708)
XLA Ops:
  7.9 5.5 %norms.1 = (f32[32,128]{1,0:T(8,128)}, f32[32,128]{1,0:T(8,128)}, f32[128,128]{1,0:T(8,128)}, f32[64,128]{1,0:T(8,128)}, f32[2,2,128,128]{3,2,1,0:T(8,128)}) custom-call(s32[6]{0:T(128)} %stack.35.place_ref, f32[256,8192]{1,0:T(8,128)} %bitcast.28, f32[3,2,128,128]{3,2,1,0:T(8,128)} %rotations_ref.1), custom_call_target="tpu_custom_call" | custom-call | flops 8388608 | bytes 8388608 | tf_op jit(solution)/shard_map/norms/pallas_call | solution.py:150
  15.5 2.5 spread.1
  18.0 11.1 %all-to-all-start = ((f32[32,160,128]{2,1,0:T(8,128)}), f32[32,160,128]{2,1,0:T(8,128)S(1)}, u32[]{:S(2)}, u32[]{:S(2)}) async-start(f32[32,160,128]{2,1,0:T(8,128)} %spread.1), calls=%async_computation | async-start | bytes 5242880 | tf_op jit(solution)/shard_map/all_to_all | solution.py:598
  29.1 9.9 %prepare.1.halves_ref = bf16[128,2,64,256]{3,2,1,0:T(8,128)(2,1)} custom-call(f32[256,8192]{1,0:T(8,128)} %bitcast.29), custom_call_target="tpu_custom_call" | custom-call | flops 1048576 | bytes 131072 | tf_op jit(solution)/shard_map/prepare/pallas_call | solution.py:187
  39.1 25.8 %all-to-all-done.arrived_ref.mine_ref = f32[32,160,128]{2,1,0:T(8,128)S(1)} async-done(((f32[32,160,128]{2,1,0:T(8,128)}), f32[32,160,128]{2,1,0:T(8,128)S(1)}, u32[]{:S(2)}, u32[]{:S(2)}) %all-to-all-start) | async-done | bytes 2621472 | tf_op jit(solution)/shard_map/all_to_all | solution.py:598
  65.6 3.2 %collective-permute-done.1 = f32[32,128]{1,0:T(8,128)S(1)} collective-permute-done((f32[32,128]{1,0:T(8,128)S(1)}, f32[32,128]{1,0:T(8,128)S(1)}, u32[]{:S(2)}, u32[]{:S(2)}) %collective-permute-start.1) | collective-permute-done | bytes 16416 | tf_op jit(solution)/shard_map/ppermute | solution.py:36
  69.9 13.1 %step0.1 = (bf16[256,2,2,64,256]{4,3,2,1,0:T(8,128)(2,1)}, f32[4,2,32,24,128]{4,3,2,1,0:T(8,128)S(1)}, f32[64,128]{1,0:T(8,128)S(1)}) custom-call(s32[64]{0:T(128)S(1)} %pad_add_fusion.tab_ref, s32[128]{0:T(128)S(1)} %copy-done.2, s32[6]{0:T(128)S(1)} %copy-done.1, f32[32,128]{1,0:T(8,128)S(1)} %add.75.normc_ref, ...), custom_call_target="tpu_custom_call" | custom-call | flops 1048576 | bytes 131072 | tf_op jit(solution)/shard_map/step0/pallas_call | solution.py:345
  83.5 3.9 %collective-permute-done.4 = f32[64,128]{1,0:T(8,128)S(1)} collective-permute-done((f32[64,128]{1,0:T(8,128)S(1)}, f32[64,128]{1,0:T(8,128)S(1)}, u32[]{:S(2)}, u32[]{:S(2)}) %collective-permute-start.4) | collective-permute-done | bytes 32800 | tf_op jit(solution)/shard_map/ppermute | solution.py:36
  87.9 3.7 %collective-permute-done.5 = f32[64,128]{1,0:T(8,128)S(1)} collective-permute-done((f32[64,128]{1,0:T(8,128)S(1)}, f32[64,128]{1,0:T(8,128)S(1)}, u32[]{:S(2)}, u32[]{:S(2)}) %collective-permute-start.5) | collective-permute-done | bytes 32800 | tf_op jit(solution)/shard_map/ppermute | solution.py:36
  93.5 4.3 %collective-permute-done.6 = f32[64,128]{1,0:T(8,128)S(1)} collective-permute-done((f32[64,128]{1,0:T(8,128)S(1)}, f32[64,128]{1,0:T(8,128)S(1)}, u32[]{:S(2)}, u32[]{:S(2)}) %collective-permute-start.6) | collective-permute-done | bytes 32800 | tf_op jit(solution)/shard_map/ppermute | solution.py:36
  97.8 1.8 collective-permute-start.7
  99.6 3.3 %collective-permute-done.7 = f32[64,128]{1,0:T(8,128)S(1)} collective-permute-done((f32[64,128]{1,0:T(8,128)S(1)}, f32[64,128]{1,0:T(8,128)S(1)}, u32[]{:S(2)}, u32[]{:S(2)}) %collective-permute-start.7) | collective-permute-done | bytes 32800 | tf_op jit(solution)/shard_map/ppermute | solution.py:36
  103.0 2.5 collective-permute-start.8
  105.5 1.9 collective-permute-done.8
  108.6 2.7 collective-permute-done.9
  112.6 2.2 copy-done
  114.8 5.0 %step1.1 = f32[32,280,256]{2,1,0:T(8,128)S(1)} custom-call(f32[64,128]{1,0:T(8,128)S(1)} %add.82.norm_ref, bf16[256,2,2,64,256]{4,3,2,1,0:T(8,128)(2,1)} %get-tuple-element.25.operand_ref, f32[64,128,128]{2,1,0:T(8,128)S(1)} %bitcast.25, f32[32,24,128]{2,1,0:T(8,128)S(1)} %get-tuple-element.37.parta_ref, f32[32,24,128]{2,1,0:T(8,128)S(1)} %get-tuple-element.36.partb_ref), custom_call_target="tpu_custom_call" | custom-call | flops 3221225472 | bytes 25165824 | tf_op jit(solution)/shard_map/step1/pallas_call | solution.py:404
  119.8 112.9 %all_to_all.10.y_ref = f32[32,280,256]{2,1,0:T(8,128)S(1)} all-to-all(f32[32,280,256]{2,1,0:T(8,128)S(1)} %step1.1), channel_id=1, replica_groups=mesh['pair'=32,'row'=4] {'pair'}, dimensions={0} | all-to-all | bytes 18350080 | tf_op jit(solution)/shard_map/all_to_all | solution.py:612
  233.4 2.4 collective-permute-start.16
  235.8 5.9 %collective-permute-start.17 = (f32[64,128]{1,0:T(8,128)S(1)}, f32[64,128]{1,0:T(8,128)S(1)}, u32[]{:S(2)}, u32[]{:S(2)}) collective-permute-start(f32[64,128]{1,0:T(8,128)S(1)} %get-tuple-element.43), channel_id=1, source_target_pairs={{4,0},{8,4},{12,8},{16,12},{20,16},{24,20},{28,24},{32,28},{36,32}... | collective-permute-start | bytes 98312 | tf_op jit(solution)/shard_map/ppermute | solution.py:616
  241.8 3.0 %gram2.1 = (f32[2,8,128]{2,1,0:T(8,128)S(1)}, f32[128,128]{1,0:T(8,128)S(1)}) custom-call(f32[32,280,256]{2,1,0:T(8,128)S(1)} %all_to_all.10.y_ref), custom_call_target="tpu_custom_call" | custom-call | flops 2147483648 | bytes 10485760 | tf_op jit(solution)/shard_map/gram2/pallas_call | solution.py:471
  247.5 2.5 collective-permute-done.15
  251.3 3.8 %step2.1 = f32[256,8192]{1,0:T(8,128)} custom-call(f32[2,8,128]{2,1,0:T(8,128)S(1)} %add.87.norm_ref.norm2_ref, f32[2,128,128]{2,1,0:T(8,128)S(1)} %get-tuple-element.41.rot_ref.rot2_ref, f32[32,280,256]{2,1,0:T(8,128)S(1)} %all_to_all.10.y_ref), custom_call_target="tpu_custom_call" | custom-call | flops 2147483648 | bytes 18874368 | tf_op jit(solution)/shard_map/step2/pallas_call | solution.py:500
  256.7 2.3 grams.1
  (64 shorter events, 16.3 us)
Async XLA Ops:
  7.2 105.5 %all-gather.2.cloned.1.call-start = ((), (), s32[]{:S(2)}) async-start(), calls=%async_computation.2 | async-start | bytes 4227072 | tf_op jit(solution)/shard_map/all_gather | solution.py:596
  13.4 1.5 collective-permute-start
  18.0 46.8 %all-to-all-start = ((f32[32,160,128]{2,1,0:T(8,128)}), f32[32,160,128]{2,1,0:T(8,128)S(1)}, u32[]{:S(2)}, u32[]{:S(2)}) async-start(f32[32,160,128]{2,1,0:T(8,128)} %spread.1), calls=%async_computation | async-start | bytes 5242880 | tf_op jit(solution)/shard_map/all_to_all | solution.py:598
  39.1 30.9 %copy-start.1 = (s32[6]{0:T(128)S(1)}, s32[6]{0:T(128)}, u32[]{:S(2)}) copy-start(s32[6]{0:T(128)} %stack.35.place_ref) | copy-start | bytes 76
  39.1 30.9 %copy-start.2 = (s32[128]{0:T(128)S(1)}, s32[128]{0:T(128)}, u32[]{:S(2)}) copy-start(s32[128]{0:T(128)} %order_ref.1) | copy-start | bytes 1540
  64.9 5.1 %collective-permute-start.3 = (f32[32,160,128]{2,1,0:T(8,128)S(1)}, f32[32,160,128]{2,1,0:T(8,128)}, u32[]{:S(2)}, u32[]{:S(2)}) collective-permute-start(f32[32,160,128]{2,1,0:T(8,128)S(1)} %all-to-all-done.arrived_ref.mine_ref), channel_id=1, source_target_pairs={{0,1},{1,0},{2,3},{3,2},{4,5},{5,4},{6,7},{7,6},{8,9},{9,8},{10,11... | collective-permute-start | bytes 7864328 | tf_op jit(solution)/shard_map/ppermute | solution.py:36
  64.9 3.8 %collective-permute-start.1 = (f32[32,128]{1,0:T(8,128)S(1)}, f32[32,128]{1,0:T(8,128)S(1)}, u32[]{:S(2)}, u32[]{:S(2)}) collective-permute-start(f32[32,128]{1,0:T(8,128)S(1)} %collect.1), channel_id=1, source_target_pairs={{0,2},{1,3},{2,0},{3,1},{4,6},{5,7},{6,4},{7,5},{8,10},{9,11},{10,... | collective-permute-start | bytes 49160 | tf_op jit(solution)/shard_map/ppermute | solution.py:36
  68.7 1.2 collective-permute-start.2
  83.2 8.4 %collective-permute-start.11 = (f32[2,2,32,24,128]{4,3,2,1,0:T(8,128)S(1)}, f32[2,2,32,24,128]{4,3,2,1,0:T(8,128)S(1)}, u32[]{:S(2)}, u32[]{:S(2)}) collective-permute-start(f32[2,2,32,24,128]{4,3,2,1,0:T(8,128)S(1)} %slice.32), channel_id=1, source_target_pairs={{0,1},{1,0},{2,3},{3,2},{4,5},{5,4},{6,7},{7,6},{8,9},{9,8},{10,11... | collective-permute-start | bytes 4718600 | tf_op jit(solution)/shard_map/ppermute | solution.py:36
  83.5 3.9 %collective-permute-start.4 = (f32[64,128]{1,0:T(8,128)S(1)}, f32[64,128]{1,0:T(8,128)S(1)}, u32[]{:S(2)}, u32[]{:S(2)}) collective-permute-start(f32[64,128]{1,0:T(8,128)S(1)} %get-tuple-element.24), channel_id=1, source_target_pairs={{0,32},{1,33},{2,34},{3,35},{4,36},{5,37},{6,38},{7,39},{8,40},{9,... | collective-permute-start | bytes 98312 | tf_op jit(solution)/shard_map/ppermute | solution.py:36
  87.4 4.2 %collective-permute-start.5 = (f32[64,128]{1,0:T(8,128)S(1)}, f32[64,128]{1,0:T(8,128)S(1)}, u32[]{:S(2)}, u32[]{:S(2)}) collective-permute-start(f32[64,128]{1,0:T(8,128)S(1)} %add.76), channel_id=1, source_target_pairs={{0,2},{1,3},{2,0},{3,1},{4,6},{5,7},{6,4},{7,5},{8,10},{9,11},{10,... | collective-permute-start | bytes 98312 | tf_op jit(solution)/shard_map/ppermute | solution.py:36
  91.8 20.7 %collective-permute-start.12 = (f32[32,24,128]{2,1,0:T(8,128)S(1)}, f32[32,24,128]{2,1,0:T(8,128)S(1)}, u32[]{:S(2)}, u32[]{:S(2)}) collective-permute-start(f32[32,24,128]{2,1,0:T(8,128)S(1)} %get-tuple-element.39), channel_id=1, source_target_pairs={{0,2},{1,3},{2,0},{3,1},{4,6},{5,7},{6,4},{7,5},{8,10},{9,11},{10,... | collective-permute-start | bytes 1179656 | tf_op jit(solution)/shard_map/ppermute | solution.py:36
  92.5 20.0 %collective-permute-start.13 = (f32[32,24,128]{2,1,0:T(8,128)S(1)}, f32[32,24,128]{2,1,0:T(8,128)S(1)}, u32[]{:S(2)}, u32[]{:S(2)}) collective-permute-start(f32[32,24,128]{2,1,0:T(8,128)S(1)} %get-tuple-element.38), channel_id=1, source_target_pairs={{0,32},{1,33},{2,34},{3,35},{4,36},{5,37},{6,38},{7,39},{8,40},{9,... | collective-permute-start | bytes 1179656 | tf_op jit(solution)/shard_map/ppermute | solution.py:36
  92.7 5.1 %collective-permute-start.6 = (f32[64,128]{1,0:T(8,128)S(1)}, f32[64,128]{1,0:T(8,128)S(1)}, u32[]{:S(2)}, u32[]{:S(2)}) collective-permute-start(f32[64,128]{1,0:T(8,128)S(1)} %add.77), channel_id=1, source_target_pairs={{0,96},{1,97},{2,98},{3,99},{4,100},{5,101},{6,102},{7,103},{8,104... | collective-permute-start | bytes 98312 | tf_op jit(solution)/shard_map/ppermute | solution.py:36
  97.8 5.1 %collective-permute-start.7 = (f32[64,128]{1,0:T(8,128)S(1)}, f32[64,128]{1,0:T(8,128)S(1)}, u32[]{:S(2)}, u32[]{:S(2)}) collective-permute-start(f32[64,128]{1,0:T(8,128)S(1)} %add.78), channel_id=1, source_target_pairs={{0,6},{1,7},{2,4},{3,5},{4,2},{5,3},{6,0},{7,1},{8,14},{9,15},{10,... | collective-permute-start | bytes 98312 | tf_op jit(solution)/shard_map/ppermute | solution.py:36
  103.0 4.4 %collective-permute-start.8 = (f32[64,128]{1,0:T(8,128)S(1)}, f32[64,128]{1,0:T(8,128)S(1)}, u32[]{:S(2)}, u32[]{:S(2)}) collective-permute-start(f32[64,128]{1,0:T(8,128)S(1)} %add.79), channel_id=1, source_target_pairs={{0,8},{1,9},{2,10},{3,11},{4,12},{5,13},{6,14},{7,15},{8,0},{9,1},... | collective-permute-start | bytes 98312 | tf_op jit(solution)/shard_map/ppermute | solution.py:36
  107.4 3.9 %collective-permute-start.9 = (f32[64,128]{1,0:T(8,128)S(1)}, f32[64,128]{1,0:T(8,128)S(1)}, u32[]{:S(2)}, u32[]{:S(2)}) collective-permute-start(f32[64,128]{1,0:T(8,128)S(1)} %add.80), channel_id=1, source_target_pairs={{0,24},{1,25},{2,26},{3,27},{4,28},{5,29},{6,30},{7,31},{8,16},{9,... | collective-permute-start | bytes 98312 | tf_op jit(solution)/shard_map/ppermute | solution.py:36
  111.3 1.2 collective-permute-start.10
  233.4 11.4 %collective-permute-start.16 = (f32[64,128]{1,0:T(8,128)S(1)}, f32[64,128]{1,0:T(8,128)S(1)}, u32[]{:S(2)}, u32[]{:S(2)}) collective-permute-start(f32[64,128]{1,0:T(8,128)S(1)} %get-tuple-element.42), channel_id=1, source_target_pairs={{0,4},{4,8},{8,12},{12,16},{16,20},{20,24},{24,28},{28,32},{32,36}... | collective-permute-start | bytes 98312 | tf_op jit(solution)/shard_map/ppermute | solution.py:615
  235.8 8.9 %collective-permute-start.17 = (f32[64,128]{1,0:T(8,128)S(1)}, f32[64,128]{1,0:T(8,128)S(1)}, u32[]{:S(2)}, u32[]{:S(2)}) collective-permute-start(f32[64,128]{1,0:T(8,128)S(1)} %get-tuple-element.43), channel_id=1, source_target_pairs={{4,0},{8,4},{12,8},{16,12},{20,16},{24,20},{28,24},{32,28},{36,32}... | collective-permute-start | bytes 98312 | tf_op jit(solution)/shard_map/ppermute | solution.py:616
  244.8 5.2 %collective-permute-start.18 = (f32[448,128]{1,0:T(8,128)S(1)}, f32[448,128]{1,0:T(8,128)S(1)}, u32[]{:S(2)}, u32[]{:S(2)}) collective-permute-start(f32[448,128]{1,0:T(8,128)S(1)} %pad_maximum_fusion), channel_id=1, source_target_pairs={{0,1},{1,0},{2,3},{3,2},{4,5},{5,4},{6,7},{7,6},{8,9},{9,8},{10,11... | collective-permute-start | bytes 688136 | tf_op jit(solution)/shard_map/ppermute | solution.py:36
  244.9 1.5 collective-permute-start.14
  246.4 3.7 %collective-permute-start.15 = (f32[2,8,128]{2,1,0:T(8,128)S(1)}, f32[2,8,128]{2,1,0:T(8,128)S(1)}, u32[]{:S(2)}, u32[]{:S(2)}) collective-permute-start(f32[2,8,128]{2,1,0:T(8,128)S(1)} %add.86), channel_id=1, source_target_pairs={{0,2},{1,3},{2,0},{3,1},{4,6},{5,7},{6,4},{7,5},{8,10},{9,11},{10,... | collective-permute-start | bytes 24584 | tf_op jit(solution)/shard_map/ppermute | solution.py:36
  250.1 6.6 %collective-permute-start.19 = (f32[448,128]{1,0:T(8,128)S(1)}, f32[448,128]{1,0:T(8,128)S(1)}, u32[]{:S(2)}, u32[]{:S(2)}) collective-permute-start(f32[448,128]{1,0:T(8,128)S(1)} %fusion.2), channel_id=1, source_target_pairs={{0,2},{1,3},{2,0},{3,1},{4,6},{5,7},{6,4},{7,5},{8,10},{9,11},{10,... | collective-permute-start | bytes 688136 | tf_op jit(solution)/shard_map/ppermute | solution.py:36
  (3 other events, 18.3 us)
Sparse Core Ops, SparseCore 0:
  13.5 90.1 all-gather.1

commit v4 on v3

--- a/solution.py
+++ b/solution.py
@@ -111,7 +111,7 @@
 
 
 def norms_kernel(
-    place_ref, x_ref, rotations_ref, keep_ref, give_ref, own_ref, quarter_ref, turned_ref,
+    x_ref, rotations_ref, keep_ref, give_ref, own_ref, quarter_ref, turned_ref,
     held_ref, rot_ref, rows_ref, sems, rot_sem
 ):
     count = sems.shape[0]
@@ -125,14 +125,15 @@
     rot_copy.start()
     for g in range(count):
         copy(g).start()
-    row, core = place_ref[0], place_ref[2]
+    row = lax.axis_index("row")
+    core = lax.rem(row, 2)
     rot_copy.wait()
     own_ref[...] = rot_ref[0, core].T
     for t in range(1, 3):
         for j in range(2):
             turned_ref[t - 1, j] = rot_ref[t, j].T
-    half = pl.ds(pl.multiple_of((row % 2) * HALF, HALF), HALF)
-    quarter_ref[...] = turned_ref[0, row // 2, half, :]
+    half = pl.ds(pl.multiple_of(core * HALF, HALF), HALF)
+    quarter_ref[...] = turned_ref[0, lax.div(row, 2), half, :]
     for g in range(count):
         copy(g).wait()
         for t in range(width * g, width * (g + 1)):
@@ -144,12 +145,12 @@
     give_ref[...] = rows_ref[1 - core]
 
 
-def norms(place, x, rotations):
+def norms(x, rotations):
     vmem = pl.BlockSpec(memory_space=pltpu.VMEM)
     hbm = pl.BlockSpec(memory_space=pltpu.HBM)
     return pl.pallas_call(
         norms_kernel,
-        in_specs=[pl.BlockSpec(memory_space=pltpu.SMEM), hbm, hbm],
+        in_specs=[hbm, hbm],
         out_specs=[vmem] * 5,
         out_shape=[
             jax.ShapeDtypeStruct((TILES, PAIRW), F32),
@@ -168,7 +169,7 @@
         compiler_params=pltpu.CompilerParams(vmem_limit_bytes=58 * MIB),
         cost_estimate=pl.CostEstimate(flops=8 * MIB, bytes_accessed=8 * MIB, transcendentals=0),
         name="norms",
-    )(place, x, rotations)
+    )(x, rotations)
 
 
 def prepare_kernel(x_ref, halves_ref):
@@ -256,21 +257,19 @@
     next_ref, parts_ref, onorm_ref, right_ref, rot_ref, moved_ref, norms_ref, sems, out_sem
 ):
 
+    def fetch(q, carry):
+        i = tab_ref[q]
+        for h in range(2):
+            pltpu.make_async_copy(
+                halves_ref.at[order_ref[2 * i + h]], right_ref.at[q, :, h], sems.at[0, q // GROUP]
+            ).start()
+        return carry
+
+    lax.fori_loop(0, NPAIR, fetch, 0)
     for k in range(GROUPS):
         piece = (mine_ref, given_ref)[k // 4].at[pl.ds(GROUP * (k % 4), GROUP), pl.ds(0, PAIRW)]
         pltpu.make_async_copy(piece, rot_ref.at[pl.ds(GROUP * k, GROUP)], sems.at[1, k]).start()
 
-    def fetch(g):
-        for k in range(GROUP):
-            q = GROUP * g + k
-            i = tab_ref[q]
-            for h in range(2):
-                pltpu.make_async_copy(
-                    halves_ref.at[order_ref[2 * i + h]], right_ref.at[q, :, h], sems.at[0, g]
-                ).start()
-
-    for g in range(GROUPS):
-        fetch(g)
     core = place_ref[2]
     for half, norm_ref in ((core, normc_ref), (1 - core, normo_ref)):
         rows = pl.ds(pl.multiple_of(half * TILES, TILES), TILES)
@@ -592,7 +591,7 @@
     even = 2 * jnp.arange(NDEV, dtype=jnp.int32)
     tab = jnp.concatenate([even + core, even + (1 - core)])
     x = samples_slab[0]
-    norm0, give, own0, quarter1, turned = norms(place, x, rotations)
+    norm0, give, own0, quarter1, turned = norms(x, rotations)
     rot1 = lax.all_gather(quarter1, BOTH, axis=0, tiled=True).reshape(NPAIR, PAIRW, PAIRW)
     copies = spread(own0, norm0, exchange(give, CORE))
     mine = lax.all_to_all(copies, "pair", 0, 0)
@@ -607,7 +606,7 @@
     norm1 = add_over(norm1, Z1, YLO)
     kept, _ = together(kept, norm1)
     quarters = [kept[0, j] + exchange(kept[1, j], flip) for j, flip in enumerate((YLO, Z1))]
-    norm1 = add_over(norm1, Z3, YBOTH, X1, X3, CORE)
+    norm1 = add_over(norm1, CORE, Z3, YBOTH, X1, X3)
     payload = step1(norm1, operand, rot1, *quarters)
     arrived = lax.all_to_all(payload, "pair", 0, 0)
     sums = parts(place, arrived)

time: 268 us -> 263 us (0.981)
  blocking collectives: 113 us -> 109 us
    all_to_all x1, blocking collectives: 113 us -> 109 us  [body(): arrived = lax.all_to_all(payload, 'pair', 0, 0)]
where the time goes in v4:
time: 263 us; the launch traced here: 260 us
  blocking collectives  109 us (41%)
  waiting for transfers between devices  57 us (22%)
  Pallas kernels  44.5 us (17%)
  starting transfers between devices  32.1 us (12%)
  between operations  14.3 us (5%)
  local copies, waits for them, and re-layouts  3.06 us (1%)
    all_to_all x1, blocking collectives, body(): arrived = lax.all_to_all(payload, 'pair', 0, 0)  109 us
    ppermute x18, waiting for transfers between devices, exchange(): return lax.ppermute(value, BOTH, pairs)  31.1 us
    all_to_all x1, waiting for transfers between devices, body(): mine = lax.all_to_all(copies, 'pair', 0, 0)  25.8 us
    ppermute x18, starting transfers between devices, exchange(): return lax.ppermute(value, BOTH, pairs)  12.6 us
    pallas_call x1, Pallas kernels, step0(): pl.pallas_call(step0_kernel, in_specs=[smem] * 3 + [vmem] * 2 + [hbm] * 3...  12.5 us
    all_to_all x1, starting transfers between devices, body(): mine = lax.all_to_all(copies, 'pair', 0, 0)  11.1 us
    pallas_call x1, Pallas kernels, prepare(): pl.pallas_call(prepare_kernel, grid=(x.shape[1] // width,), in_specs=[pl....  9.91 us
    ppermute x1, starting transfers between devices, body(): lax.ppermute(sums[0, :HALF], 'pair', [(k + 1, k) for k in range(NDEV - 1)])  6.09 us
  transfers between devices with their start and end apart: 22, of which 14 were waited for; matrix products, arithmetic and copies ran while one was open for 0% of the time, Pallas kernels for 12%

profile of v4, /device:TPU:2, one launch (start us, length us, event | category | flops | bytes accessed | tf_op | source)
XLA Modules:
  0.0 260.4 jit_solution(13609628016383539464)
XLA Ops:
  7.2 4.9 %norms.1 = (f32[32,128]{1,0:T(8,128)}, f32[32,128]{1,0:T(8,128)}, f32[128,128]{1,0:T(8,128)}, f32[64,128]{1,0:T(8,128)}, f32[2,2,128,128]{3,2,1,0:T(8,128)}) custom-call(f32[256,8192]{1,0:T(8,128)} %bitcast.28, f32[3,2,128,128]{3,2,1,0:T(8,128)} %rotations_ref.1), custom_call_target="tpu_custom_call" | custom-call | flops 8388608 | bytes 8388608 | tf_op jit(solution)/shard_map/norms/pallas_call | solution.py:151
  14.2 2.5 spread.1
  16.7 11.1 %all-to-all-start = ((f32[32,160,128]{2,1,0:T(8,128)}), f32[32,160,128]{2,1,0:T(8,128)S(1)}, u32[]{:S(2)}, u32[]{:S(2)}) async-start(f32[32,160,128]{2,1,0:T(8,128)} %spread.1), calls=%async_computation | async-start | bytes 5242880 | tf_op jit(solution)/shard_map/all_to_all | solution.py:597
  27.8 9.9 %prepare.1.halves_ref = bf16[128,2,64,256]{3,2,1,0:T(8,128)(2,1)} custom-call(f32[256,8192]{1,0:T(8,128)} %bitcast.29), custom_call_target="tpu_custom_call" | custom-call | flops 1048576 | bytes 131072 | tf_op jit(solution)/shard_map/prepare/pallas_call | solution.py:188
  37.8 25.8 %all-to-all-done.arrived_ref.mine_ref = f32[32,160,128]{2,1,0:T(8,128)S(1)} async-done(((f32[32,160,128]{2,1,0:T(8,128)}), f32[32,160,128]{2,1,0:T(8,128)S(1)}, u32[]{:S(2)}, u32[]{:S(2)}) %all-to-all-start) | async-done | bytes 2621472 | tf_op jit(solution)/shard_map/all_to_all | solution.py:597
  64.3 3.2 %collective-permute-done.1 = f32[32,128]{1,0:T(8,128)S(1)} collective-permute-done((f32[32,128]{1,0:T(8,128)S(1)}, f32[32,128]{1,0:T(8,128)S(1)}, u32[]{:S(2)}, u32[]{:S(2)}) %collective-permute-start.1) | collective-permute-done | bytes 16416 | tf_op jit(solution)/shard_map/ppermute | solution.py:36
  68.6 12.5 %step0.1 = (bf16[256,2,2,64,256]{4,3,2,1,0:T(8,128)(2,1)}, f32[4,2,32,24,128]{4,3,2,1,0:T(8,128)S(1)}, f32[64,128]{1,0:T(8,128)S(1)}) custom-call(s32[64]{0:T(128)S(1)} %pad_add_fusion.tab_ref, s32[128]{0:T(128)S(1)} %copy-done.1, s32[6]{0:T(128)S(1)} %stack.35.place_ref, f32[32,128]{1,0:T(8,128)S(1)} %add.75.normc_ref, ...), custom_call_target="tpu_custom_call" | custom-call | flops 1048576 | bytes 131072 | tf_op jit(solution)/shard_map/step0/pallas_call | solution.py:344
  81.5 3.9 %collective-permute-done.4 = f32[64,128]{1,0:T(8,128)S(1)} collective-permute-done((f32[64,128]{1,0:T(8,128)S(1)}, f32[64,128]{1,0:T(8,128)S(1)}, u32[]{:S(2)}, u32[]{:S(2)}) %collective-permute-start.4) | collective-permute-done | bytes 32800 | tf_op jit(solution)/shard_map/ppermute | solution.py:36
  86.0 3.7 %collective-permute-done.5 = f32[64,128]{1,0:T(8,128)S(1)} collective-permute-done((f32[64,128]{1,0:T(8,128)S(1)}, f32[64,128]{1,0:T(8,128)S(1)}, u32[]{:S(2)}, u32[]{:S(2)}) %collective-permute-start.5) | collective-permute-done | bytes 32800 | tf_op jit(solution)/shard_map/ppermute | solution.py:36
  92.8 4.2 %collective-permute-done.7 = f32[64,128]{1,0:T(8,128)S(1)} collective-permute-done((f32[64,128]{1,0:T(8,128)S(1)}, f32[64,128]{1,0:T(8,128)S(1)}, u32[]{:S(2)}, u32[]{:S(2)}) %collective-permute-start.7) | collective-permute-done | bytes 32800 | tf_op jit(solution)/shard_map/ppermute | solution.py:36
  97.0 2.2 collective-permute-start.8
  99.3 2.9 %collective-permute-done.8 = f32[64,128]{1,0:T(8,128)S(1)} collective-permute-done((f32[64,128]{1,0:T(8,128)S(1)}, f32[64,128]{1,0:T(8,128)S(1)}, u32[]{:S(2)}, u32[]{:S(2)}) %collective-permute-start.8) | collective-permute-done | bytes 32800 | tf_op jit(solution)/shard_map/ppermute | solution.py:36
  102.2 2.7 %collective-permute-start.9 = (f32[64,128]{1,0:T(8,128)S(1)}, f32[64,128]{1,0:T(8,128)S(1)}, u32[]{:S(2)}, u32[]{:S(2)}) collective-permute-start(f32[64,128]{1,0:T(8,128)S(1)} %add.80), channel_id=1, source_target_pairs={{0,8},{1,9},{2,10},{3,11},{4,12},{5,13},{6,14},{7,15},{8,0},{9,1},... | collective-permute-start | bytes 98312 | tf_op jit(solution)/shard_map/ppermute | solution.py:36
  104.8 1.9 collective-permute-done.9
  107.6 3.1 %collective-permute-done.10 = f32[64,128]{1,0:T(8,128)S(1)} collective-permute-done((f32[64,128]{1,0:T(8,128)S(1)}, f32[64,128]{1,0:T(8,128)S(1)}, u32[]{:S(2)}, u32[]{:S(2)}) %collective-permute-start.10) | collective-permute-done | bytes 32800 | tf_op jit(solution)/shard_map/ppermute | solution.py:36
  110.8 2.2 copy-done
  113.0 5.0 %step1.1 = f32[32,280,256]{2,1,0:T(8,128)S(1)} custom-call(f32[64,128]{1,0:T(8,128)S(1)} %add.82.norm_ref, bf16[256,2,2,64,256]{4,3,2,1,0:T(8,128)(2,1)} %get-tuple-element.25.operand_ref, f32[64,128,128]{2,1,0:T(8,128)S(1)} %bitcast.25, f32[32,24,128]{2,1,0:T(8,128)S(1)} %get-tuple-element.37.parta_ref, f32[32,24,128]{2,1,0:T(8,128)S(1)} %get-tuple-element.36.partb_ref), custom_call_target="tpu_custom_call" | custom-call | flops 3221225472 | bytes 25165824 | tf_op jit(solution)/shard_map/step1/pallas_call | solution.py:403
  118.0 109.1 %all_to_all.10.y_ref = f32[32,280,256]{2,1,0:T(8,128)S(1)} all-to-all(f32[32,280,256]{2,1,0:T(8,128)S(1)} %step1.1), channel_id=1, replica_groups=mesh['pair'=32,'row'=4] {'pair'}, dimensions={0} | all-to-all | bytes 18350080 | tf_op jit(solution)/shard_map/all_to_all | solution.py:611
  227.7 2.3 collective-permute-start.16
  230.0 6.1 %collective-permute-start.17 = (f32[64,128]{1,0:T(8,128)S(1)}, f32[64,128]{1,0:T(8,128)S(1)}, u32[]{:S(2)}, u32[]{:S(2)}) collective-permute-start(f32[64,128]{1,0:T(8,128)S(1)} %get-tuple-element.43), channel_id=1, source_target_pairs={{4,0},{8,4},{12,8},{16,12},{20,16},{24,20},{28,24},{32,28},{36,32}... | collective-permute-start | bytes 98312 | tf_op jit(solution)/shard_map/ppermute | solution.py:615
  236.1 3.0 %gram2.1 = (f32[2,8,128]{2,1,0:T(8,128)S(1)}, f32[128,128]{1,0:T(8,128)S(1)}) custom-call(f32[32,280,256]{2,1,0:T(8,128)S(1)} %all_to_all.10.y_ref), custom_call_target="tpu_custom_call" | custom-call | flops 2147483648 | bytes 10485760 | tf_op jit(solution)/shard_map/gram2/pallas_call | solution.py:470
  242.1 2.3 collective-permute-done.15
  246.0 3.8 %step2.1 = f32[256,8192]{1,0:T(8,128)} custom-call(f32[2,8,128]{2,1,0:T(8,128)S(1)} %add.87.norm_ref.norm2_ref, f32[2,128,128]{2,1,0:T(8,128)S(1)} %get-tuple-element.41.rot_ref.rot2_ref, f32[32,280,256]{2,1,0:T(8,128)S(1)} %all_to_all.10.y_ref), custom_call_target="tpu_custom_call" | custom-call | flops 2147483648 | bytes 18874368 | tf_op jit(solution)/shard_map/step2/pallas_call | solution.py:499
  251.2 2.3 grams.1
  (62 shorter events, 15.7 us)
Async XLA Ops:
  7.2 103.6 %all-gather.2.cloned.1.call-start = ((), (), s32[]{:S(2)}) async-start(), calls=%async_computation.2 | async-start | bytes 4227072 | tf_op jit(solution)/shard_map/all_gather | solution.py:595
  12.1 1.5 collective-permute-start
  16.7 46.8 %all-to-all-start = ((f32[32,160,128]{2,1,0:T(8,128)}), f32[32,160,128]{2,1,0:T(8,128)S(1)}, u32[]{:S(2)}, u32[]{:S(2)}) async-start(f32[32,160,128]{2,1,0:T(8,128)} %spread.1), calls=%async_computation | async-start | bytes 5242880 | tf_op jit(solution)/shard_map/all_to_all | solution.py:597
  37.7 30.9 %copy-start.1 = (s32[128]{0:T(128)S(1)}, s32[128]{0:T(128)}, u32[]{:S(2)}) copy-start(s32[128]{0:T(128)} %order_ref.1) | copy-start | bytes 1540
  63.6 5.1 %collective-permute-start.3 = (f32[32,160,128]{2,1,0:T(8,128)S(1)}, f32[32,160,128]{2,1,0:T(8,128)}, u32[]{:S(2)}, u32[]{:S(2)}) collective-permute-start(f32[32,160,128]{2,1,0:T(8,128)S(1)} %all-to-all-done.arrived_ref.mine_ref), channel_id=1, source_target_pairs={{0,1},{1,0},{2,3},{3,2},{4,5},{5,4},{6,7},{7,6},{8,9},{9,8},{10,11... | collective-permute-start | bytes 7864328 | tf_op jit(solution)/shard_map/ppermute | solution.py:36
  63.6 3.8 %collective-permute-start.1 = (f32[32,128]{1,0:T(8,128)S(1)}, f32[32,128]{1,0:T(8,128)S(1)}, u32[]{:S(2)}, u32[]{:S(2)}) collective-permute-start(f32[32,128]{1,0:T(8,128)S(1)} %collect.1), channel_id=1, source_target_pairs={{0,2},{1,3},{2,0},{3,1},{4,6},{5,7},{6,4},{7,5},{8,10},{9,11},{10,... | collective-permute-start | bytes 49160 | tf_op jit(solution)/shard_map/ppermute | solution.py:36
  67.4 1.2 collective-permute-start.2
  81.2 8.5 %collective-permute-start.11 = (f32[2,2,32,24,128]{4,3,2,1,0:T(8,128)S(1)}, f32[2,2,32,24,128]{4,3,2,1,0:T(8,128)S(1)}, u32[]{:S(2)}, u32[]{:S(2)}) collective-permute-start(f32[2,2,32,24,128]{4,3,2,1,0:T(8,128)S(1)} %slice.32), channel_id=1, source_target_pairs={{0,1},{1,0},{2,3},{3,2},{4,5},{5,4},{6,7},{7,6},{8,9},{9,8},{10,11... | collective-permute-start | bytes 4718600 | tf_op jit(solution)/shard_map/ppermute | solution.py:36
  81.5 3.9 %collective-permute-start.4 = (f32[64,128]{1,0:T(8,128)S(1)}, f32[64,128]{1,0:T(8,128)S(1)}, u32[]{:S(2)}, u32[]{:S(2)}) collective-permute-start(f32[64,128]{1,0:T(8,128)S(1)} %get-tuple-element.24), channel_id=1, source_target_pairs={{0,32},{1,33},{2,34},{3,35},{4,36},{5,37},{6,38},{7,39},{8,40},{9,... | collective-permute-start | bytes 98312 | tf_op jit(solution)/shard_map/ppermute | solution.py:36
  85.4 4.3 %collective-permute-start.5 = (f32[64,128]{1,0:T(8,128)S(1)}, f32[64,128]{1,0:T(8,128)S(1)}, u32[]{:S(2)}, u32[]{:S(2)}) collective-permute-start(f32[64,128]{1,0:T(8,128)S(1)} %add.76), channel_id=1, source_target_pairs={{0,2},{1,3},{2,0},{3,1},{4,6},{5,7},{6,4},{7,5},{8,10},{9,11},{10,... | collective-permute-start | bytes 98312 | tf_op jit(solution)/shard_map/ppermute | solution.py:36
  89.9 20.7 %collective-permute-start.12 = (f32[32,24,128]{2,1,0:T(8,128)S(1)}, f32[32,24,128]{2,1,0:T(8,128)S(1)}, u32[]{:S(2)}, u32[]{:S(2)}) collective-permute-start(f32[32,24,128]{2,1,0:T(8,128)S(1)} %get-tuple-element.39), channel_id=1, source_target_pairs={{0,2},{1,3},{2,0},{3,1},{4,6},{5,7},{6,4},{7,5},{8,10},{9,11},{10,... | collective-permute-start | bytes 1179656 | tf_op jit(solution)/shard_map/ppermute | solution.py:36
  90.6 20.1 %collective-permute-start.13 = (f32[32,24,128]{2,1,0:T(8,128)S(1)}, f32[32,24,128]{2,1,0:T(8,128)S(1)}, u32[]{:S(2)}, u32[]{:S(2)}) collective-permute-start(f32[32,24,128]{2,1,0:T(8,128)S(1)} %get-tuple-element.38), channel_id=1, source_target_pairs={{0,32},{1,33},{2,34},{3,35},{4,36},{5,37},{6,38},{7,39},{8,40},{9,... | collective-permute-start | bytes 1179656 | tf_op jit(solution)/shard_map/ppermute | solution.py:36
  90.6 1.2 collective-permute-start.6
  91.8 5.2 %collective-permute-start.7 = (f32[64,128]{1,0:T(8,128)S(1)}, f32[64,128]{1,0:T(8,128)S(1)}, u32[]{:S(2)}, u32[]{:S(2)}) collective-permute-start(f32[64,128]{1,0:T(8,128)S(1)} %add.78), channel_id=1, source_target_pairs={{0,96},{1,97},{2,98},{3,99},{4,100},{5,101},{6,102},{7,103},{8,104... | collective-permute-start | bytes 98312 | tf_op jit(solution)/shard_map/ppermute | solution.py:36
  97.0 5.1 %collective-permute-start.8 = (f32[64,128]{1,0:T(8,128)S(1)}, f32[64,128]{1,0:T(8,128)S(1)}, u32[]{:S(2)}, u32[]{:S(2)}) collective-permute-start(f32[64,128]{1,0:T(8,128)S(1)} %add.79), channel_id=1, source_target_pairs={{0,6},{1,7},{2,4},{3,5},{4,2},{5,3},{6,0},{7,1},{8,14},{9,15},{10,... | collective-permute-start | bytes 98312 | tf_op jit(solution)/shard_map/ppermute | solution.py:36
  102.2 4.6 %collective-permute-start.9 = (f32[64,128]{1,0:T(8,128)S(1)}, f32[64,128]{1,0:T(8,128)S(1)}, u32[]{:S(2)}, u32[]{:S(2)}) collective-permute-start(f32[64,128]{1,0:T(8,128)S(1)} %add.80), channel_id=1, source_target_pairs={{0,8},{1,9},{2,10},{3,11},{4,12},{5,13},{6,14},{7,15},{8,0},{9,1},... | collective-permute-start | bytes 98312 | tf_op jit(solution)/shard_map/ppermute | solution.py:36
  106.7 3.9 %collective-permute-start.10 = (f32[64,128]{1,0:T(8,128)S(1)}, f32[64,128]{1,0:T(8,128)S(1)}, u32[]{:S(2)}, u32[]{:S(2)}) collective-permute-start(f32[64,128]{1,0:T(8,128)S(1)} %add.81), channel_id=1, source_target_pairs={{0,24},{1,25},{2,26},{3,27},{4,28},{5,29},{6,30},{7,31},{8,16},{9,... | collective-permute-start | bytes 98312 | tf_op jit(solution)/shard_map/ppermute | solution.py:36
  227.7 11.4 %collective-permute-start.16 = (f32[64,128]{1,0:T(8,128)S(1)}, f32[64,128]{1,0:T(8,128)S(1)}, u32[]{:S(2)}, u32[]{:S(2)}) collective-permute-start(f32[64,128]{1,0:T(8,128)S(1)} %get-tuple-element.42), channel_id=1, source_target_pairs={{0,4},{4,8},{8,12},{12,16},{16,20},{20,24},{24,28},{28,32},{32,36}... | collective-permute-start | bytes 98312 | tf_op jit(solution)/shard_map/ppermute | solution.py:614
  230.0 16.0 %copy-start.2 = (f32[2,2,128,128]{3,2,1,0:T(8,128)S(1)}, f32[2,2,128,128]{3,2,1,0:T(8,128)}, u32[]{:S(2)}) copy-start(f32[2,2,128,128]{3,2,1,0:T(8,128)} %get-tuple-element.34) | copy-start | bytes 786436
  230.0 9.1 %collective-permute-start.17 = (f32[64,128]{1,0:T(8,128)S(1)}, f32[64,128]{1,0:T(8,128)S(1)}, u32[]{:S(2)}, u32[]{:S(2)}) collective-permute-start(f32[64,128]{1,0:T(8,128)S(1)} %get-tuple-element.43), channel_id=1, source_target_pairs={{4,0},{8,4},{12,8},{16,12},{20,16},{24,20},{28,24},{32,28},{36,32}... | collective-permute-start | bytes 98312 | tf_op jit(solution)/shard_map/ppermute | solution.py:615
  239.1 5.2 %collective-permute-start.18 = (f32[448,128]{1,0:T(8,128)S(1)}, f32[448,128]{1,0:T(8,128)S(1)}, u32[]{:S(2)}, u32[]{:S(2)}) collective-permute-start(f32[448,128]{1,0:T(8,128)S(1)} %pad_maximum_fusion), channel_id=1, source_target_pairs={{0,1},{1,0},{2,3},{3,2},{4,5},{5,4},{6,7},{7,6},{8,9},{9,8},{10,11... | collective-permute-start | bytes 688136 | tf_op jit(solution)/shard_map/ppermute | solution.py:36
  239.2 1.5 collective-permute-start.14
  240.7 3.7 %collective-permute-start.15 = (f32[2,8,128]{2,1,0:T(8,128)S(1)}, f32[2,8,128]{2,1,0:T(8,128)S(1)}, u32[]{:S(2)}, u32[]{:S(2)}) collective-permute-start(f32[2,8,128]{2,1,0:T(8,128)S(1)} %add.86), channel_id=1, source_target_pairs={{0,2},{1,3},{2,0},{3,1},{4,6},{5,7},{6,4},{7,5},{8,10},{9,11},{10,... | collective-permute-start | bytes 24584 | tf_op jit(solution)/shard_map/ppermute | solution.py:36
  244.4 6.8 %collective-permute-start.19 = (f32[448,128]{1,0:T(8,128)S(1)}, f32[448,128]{1,0:T(8,128)S(1)}, u32[]{:S(2)}, u32[]{:S(2)}) collective-permute-start(f32[448,128]{1,0:T(8,128)S(1)} %fusion.2), channel_id=1, source_target_pairs={{0,2},{1,3},{2,0},{3,1},{4,6},{5,7},{6,4},{7,5},{8,10},{9,11},{10,... | collective-permute-start | bytes 688136 | tf_op jit(solution)/shard_map/ppermute | solution.py:36
  (2 other events, 2.8 us)
Sparse Core Ops, SparseCore 0:
  12.2 90.2 all-gather.1

commit v5 on v4

--- a/solution.py
+++ b/solution.py
@@ -242,7 +242,7 @@
     )(arrived)
 
 
-GROUP = 8
+GROUP = 16
 GROUPS = NPAIR // GROUP
 OPERAND = (NPAIR, 2, 2, HALF, SAMP)
 ROOM = 4
@@ -267,7 +267,8 @@
 
     lax.fori_loop(0, NPAIR, fetch, 0)
     for k in range(GROUPS):
-        piece = (mine_ref, given_ref)[k // 4].at[pl.ds(GROUP * (k % 4), GROUP), pl.ds(0, PAIRW)]
+        source, first = divmod(GROUP * k, NDEV)
+        piece = (mine_ref, given_ref)[source].at[pl.ds(first, GROUP), pl.ds(0, PAIRW)]
         pltpu.make_async_copy(piece, rot_ref.at[pl.ds(GROUP * k, GROUP)], sems.at[1, k]).start()
 
     core = place_ref[2]

time: 263 us -> 262 us (level)
  waiting for transfers between devices: 57 us -> 60 us
  starting transfers between devices: 32.1 us -> 29.3 us
    ppermute x18, waiting for transfers between devices: 31.1 us -> 34.2 us  [exchange(): return lax.ppermute(value, BOTH, pairs)]
    ppermute x18, starting transfers between devices: 12.6 us -> 9.64 us  [exchange(): return lax.ppermute(value, BOTH, pairs)]
where the time goes in v5:
time: 262 us; the launch traced here: 261 us
  blocking collectives  110 us (42%)
  waiting for transfers between devices  60 us (23%)
  Pallas kernels  43.6 us (17%)
  starting transfers between devices  29.3 us (11%)
  between operations  14.3 us (5%)
  local copies, waits for them, and re-layouts  3.06 us (1%)
    all_to_all x1, blocking collectives, body(): arrived = lax.all_to_all(payload, 'pair', 0, 0)  110 us
    ppermute x18, waiting for transfers between devices, exchange(): return lax.ppermute(value, BOTH, pairs)  34.2 us
    all_to_all x1, waiting for transfers between devices, body(): mine = lax.all_to_all(copies, 'pair', 0, 0)  25.8 us
    pallas_call x1, Pallas kernels, step0(): pl.pallas_call(step0_kernel, in_specs=[smem] * 3 + [vmem] * 2 + [hbm] * 3...  12.1 us
    all_to_all x1, starting transfers between devices, body(): mine = lax.all_to_all(copies, 'pair', 0, 0)  11.1 us
    pallas_call x1, Pallas kernels, prepare(): pl.pallas_call(prepare_kernel, grid=(x.shape[1] // width,), in_specs=[pl....  9.91 us
    ppermute x18, starting transfers between devices, exchange(): return lax.ppermute(value, BOTH, pairs)  9.64 us
    ppermute x1, starting transfers between devices, body(): lax.ppermute(sums[0, :HALF], 'pair', [(k + 1, k) for k in range(NDEV - 1)])  6.64 us
  transfers between devices with their start and end apart: 22, of which 14 were waited for; matrix products, arithmetic and copies ran while one was open for 0% of the time, Pallas kernels for 12%

profile of v5, /device:TPU:2, one launch (start us, length us, event | category | flops | bytes accessed | tf_op | source)
XLA Modules:
  0.0 261.2 jit_solution(6326958668214608573)
XLA Ops:
  7.2 4.9 %norms.1 = (f32[32,128]{1,0:T(8,128)}, f32[32,128]{1,0:T(8,128)}, f32[128,128]{1,0:T(8,128)}, f32[64,128]{1,0:T(8,128)}, f32[2,2,128,128]{3,2,1,0:T(8,128)}) custom-call(f32[256,8192]{1,0:T(8,128)} %bitcast.28, f32[3,2,128,128]{3,2,1,0:T(8,128)} %rotations_ref.1), custom_call_target="tpu_custom_call" | custom-call | flops 8388608 | bytes 8388608 | tf_op jit(solution)/shard_map/norms/pallas_call | solution.py:151
  14.2 2.5 spread.1
  16.7 11.1 %all-to-all-start = ((f32[32,160,128]{2,1,0:T(8,128)}), f32[32,160,128]{2,1,0:T(8,128)S(1)}, u32[]{:S(2)}, u32[]{:S(2)}) async-start(f32[32,160,128]{2,1,0:T(8,128)} %spread.1), calls=%async_computation | async-start | bytes 5242880 | tf_op jit(solution)/shard_map/all_to_all | solution.py:598
  27.8 9.9 %prepare.1.halves_ref = bf16[128,2,64,256]{3,2,1,0:T(8,128)(2,1)} custom-call(f32[256,8192]{1,0:T(8,128)} %bitcast.29), custom_call_target="tpu_custom_call" | custom-call | flops 1048576 | bytes 131072 | tf_op jit(solution)/shard_map/prepare/pallas_call | solution.py:188
  37.8 25.8 %all-to-all-done.arrived_ref.mine_ref = f32[32,160,128]{2,1,0:T(8,128)S(1)} async-done(((f32[32,160,128]{2,1,0:T(8,128)}), f32[32,160,128]{2,1,0:T(8,128)S(1)}, u32[]{:S(2)}, u32[]{:S(2)}) %all-to-all-start) | async-done | bytes 2621472 | tf_op jit(solution)/shard_map/all_to_all | solution.py:598
  64.3 3.2 %collective-permute-done.1 = f32[32,128]{1,0:T(8,128)S(1)} collective-permute-done((f32[32,128]{1,0:T(8,128)S(1)}, f32[32,128]{1,0:T(8,128)S(1)}, u32[]{:S(2)}, u32[]{:S(2)}) %collective-permute-start.1) | collective-permute-done | bytes 16416 | tf_op jit(solution)/shard_map/ppermute | solution.py:36
  68.6 12.1 %step0.1 = (bf16[256,2,2,64,256]{4,3,2,1,0:T(8,128)(2,1)}, f32[4,2,32,24,128]{4,3,2,1,0:T(8,128)S(1)}, f32[64,128]{1,0:T(8,128)S(1)}) custom-call(s32[64]{0:T(128)S(1)} %pad_add_fusion.tab_ref, s32[128]{0:T(128)S(1)} %copy-done.1, s32[6]{0:T(128)S(1)} %stack.35.place_ref, f32[32,128]{1,0:T(8,128)S(1)} %add.75.normc_ref, ...), custom_call_target="tpu_custom_call" | custom-call | flops 1048576 | bytes 131072 | tf_op jit(solution)/shard_map/step0/pallas_call | solution.py:345
  81.1 3.9 %collective-permute-done.4 = f32[64,128]{1,0:T(8,128)S(1)} collective-permute-done((f32[64,128]{1,0:T(8,128)S(1)}, f32[64,128]{1,0:T(8,128)S(1)}, u32[]{:S(2)}, u32[]{:S(2)}) %collective-permute-start.4) | collective-permute-done | bytes 32800 | tf_op jit(solution)/shard_map/ppermute | solution.py:36
  85.6 3.6 %collective-permute-done.5 = f32[64,128]{1,0:T(8,128)S(1)} collective-permute-done((f32[64,128]{1,0:T(8,128)S(1)}, f32[64,128]{1,0:T(8,128)S(1)}, u32[]{:S(2)}, u32[]{:S(2)}) %collective-permute-start.5) | collective-permute-done | bytes 32800 | tf_op jit(solution)/shard_map/ppermute | solution.py:36
  92.4 4.3 %collective-permute-done.7 = f32[64,128]{1,0:T(8,128)S(1)} collective-permute-done((f32[64,128]{1,0:T(8,128)S(1)}, f32[64,128]{1,0:T(8,128)S(1)}, u32[]{:S(2)}, u32[]{:S(2)}) %collective-permute-start.7) | collective-permute-done | bytes 32800 | tf_op jit(solution)/shard_map/ppermute | solution.py:36
  96.7 1.9 collective-permute-start.8
  98.6 3.2 %collective-permute-done.8 = f32[64,128]{1,0:T(8,128)S(1)} collective-permute-done((f32[64,128]{1,0:T(8,128)S(1)}, f32[64,128]{1,0:T(8,128)S(1)}, u32[]{:S(2)}, u32[]{:S(2)}) %collective-permute-start.8) | collective-permute-done | bytes 32800 | tf_op jit(solution)/shard_map/ppermute | solution.py:36
  101.9 2.9 %collective-permute-start.9 = (f32[64,128]{1,0:T(8,128)S(1)}, f32[64,128]{1,0:T(8,128)S(1)}, u32[]{:S(2)}, u32[]{:S(2)}) collective-permute-start(f32[64,128]{1,0:T(8,128)S(1)} %add.80), channel_id=1, source_target_pairs={{0,8},{1,9},{2,10},{3,11},{4,12},{5,13},{6,14},{7,15},{8,0},{9,1},... | collective-permute-start | bytes 98312 | tf_op jit(solution)/shard_map/ppermute | solution.py:36
  107.2 3.3 %collective-permute-done.10 = f32[64,128]{1,0:T(8,128)S(1)} collective-permute-done((f32[64,128]{1,0:T(8,128)S(1)}, f32[64,128]{1,0:T(8,128)S(1)}, u32[]{:S(2)}, u32[]{:S(2)}) %collective-permute-start.10) | collective-permute-done | bytes 32800 | tf_op jit(solution)/shard_map/ppermute | solution.py:36
  110.7 2.2 copy-done
  112.9 4.6 %step1.1 = f32[32,280,256]{2,1,0:T(8,128)S(1)} custom-call(f32[64,128]{1,0:T(8,128)S(1)} %add.82.norm_ref, bf16[256,2,2,64,256]{4,3,2,1,0:T(8,128)(2,1)} %get-tuple-element.25.operand_ref, f32[64,128,128]{2,1,0:T(8,128)S(1)} %bitcast.25, f32[32,24,128]{2,1,0:T(8,128)S(1)} %get-tuple-element.37.parta_ref, f32[32,24,128]{2,1,0:T(8,128)S(1)} %get-tuple-element.36.partb_ref), custom_call_target="tpu_custom_call" | custom-call | flops 3221225472 | bytes 25165824 | tf_op jit(solution)/shard_map/step1/pallas_call | solution.py:404
  117.5 110.5 %all_to_all.10.y_ref = f32[32,280,256]{2,1,0:T(8,128)S(1)} all-to-all(f32[32,280,256]{2,1,0:T(8,128)S(1)} %step1.1), channel_id=1, replica_groups=mesh['pair'=32,'row'=4] {'pair'}, dimensions={0} | all-to-all | bytes 18350080 | tf_op jit(solution)/shard_map/all_to_all | solution.py:612
  228.6 1.9 collective-permute-start.16
  230.5 6.6 %collective-permute-start.17 = (f32[64,128]{1,0:T(8,128)S(1)}, f32[64,128]{1,0:T(8,128)S(1)}, u32[]{:S(2)}, u32[]{:S(2)}) collective-permute-start(f32[64,128]{1,0:T(8,128)S(1)} %get-tuple-element.43), channel_id=1, source_target_pairs={{4,0},{8,4},{12,8},{16,12},{20,16},{24,20},{28,24},{32,28},{36,32}... | collective-permute-start | bytes 98312 | tf_op jit(solution)/shard_map/ppermute | solution.py:616
  237.1 3.0 %gram2.1 = (f32[2,8,128]{2,1,0:T(8,128)S(1)}, f32[128,128]{1,0:T(8,128)S(1)}) custom-call(f32[32,280,256]{2,1,0:T(8,128)S(1)} %all_to_all.10.y_ref), custom_call_target="tpu_custom_call" | custom-call | flops 2147483648 | bytes 10485760 | tf_op jit(solution)/shard_map/gram2/pallas_call | solution.py:471
  241.9 3.5 %collective-permute-done.15 = f32[2,8,128]{2,1,0:T(8,128)S(1)} collective-permute-done((f32[2,8,128]{2,1,0:T(8,128)S(1)}, f32[2,8,128]{2,1,0:T(8,128)S(1)}, u32[]{:S(2)}, u32[]{:S(2)}) %collective-permute-start.15) | collective-permute-done | bytes 8224 | tf_op jit(solution)/shard_map/ppermute | solution.py:36
  245.7 3.8 %step2.1 = f32[256,8192]{1,0:T(8,128)} custom-call(f32[2,8,128]{2,1,0:T(8,128)S(1)} %add.87.norm_ref.norm2_ref, f32[2,128,128]{2,1,0:T(8,128)S(1)} %get-tuple-element.41.rot_ref.rot2_ref, f32[32,280,256]{2,1,0:T(8,128)S(1)} %all_to_all.10.y_ref), custom_call_target="tpu_custom_call" | custom-call | flops 2147483648 | bytes 18874368 | tf_op jit(solution)/shard_map/step2/pallas_call | solution.py:500
  249.5 2.6 collective-permute-done.19
  252.1 2.3 grams.1
  (62 shorter events, 13.4 us)
Async XLA Ops:
  7.2 103.5 %all-gather.2.cloned.1.call-start = ((), (), s32[]{:S(2)}) async-start(), calls=%async_computation.2 | async-start | bytes 4227072 | tf_op jit(solution)/shard_map/all_gather | solution.py:596
  12.1 1.5 collective-permute-start
  16.7 46.8 %all-to-all-start = ((f32[32,160,128]{2,1,0:T(8,128)}), f32[32,160,128]{2,1,0:T(8,128)S(1)}, u32[]{:S(2)}, u32[]{:S(2)}) async-start(f32[32,160,128]{2,1,0:T(8,128)} %spread.1), calls=%async_computation | async-start | bytes 5242880 | tf_op jit(solution)/shard_map/all_to_all | solution.py:598
  37.7 30.9 %copy-start.1 = (s32[128]{0:T(128)S(1)}, s32[128]{0:T(128)}, u32[]{:S(2)}) copy-start(s32[128]{0:T(128)} %order_ref.1) | copy-start | bytes 1540
  63.6 5.1 %collective-permute-start.3 = (f32[32,160,128]{2,1,0:T(8,128)S(1)}, f32[32,160,128]{2,1,0:T(8,128)}, u32[]{:S(2)}, u32[]{:S(2)}) collective-permute-start(f32[32,160,128]{2,1,0:T(8,128)S(1)} %all-to-all-done.arrived_ref.mine_ref), channel_id=1, source_target_pairs={{0,1},{1,0},{2,3},{3,2},{4,5},{5,4},{6,7},{7,6},{8,9},{9,8},{10,11... | collective-permute-start | bytes 7864328 | tf_op jit(solution)/shard_map/ppermute | solution.py:36
  63.6 3.8 %collective-permute-start.1 = (f32[32,128]{1,0:T(8,128)S(1)}, f32[32,128]{1,0:T(8,128)S(1)}, u32[]{:S(2)}, u32[]{:S(2)}) collective-permute-start(f32[32,128]{1,0:T(8,128)S(1)} %collect.1), channel_id=1, source_target_pairs={{0,2},{1,3},{2,0},{3,1},{4,6},{5,7},{6,4},{7,5},{8,10},{9,11},{10,... | collective-permute-start | bytes 49160 | tf_op jit(solution)/shard_map/ppermute | solution.py:36
  67.4 1.2 collective-permute-start.2
  80.8 8.4 %collective-permute-start.11 = (f32[2,2,32,24,128]{4,3,2,1,0:T(8,128)S(1)}, f32[2,2,32,24,128]{4,3,2,1,0:T(8,128)S(1)}, u32[]{:S(2)}, u32[]{:S(2)}) collective-permute-start(f32[2,2,32,24,128]{4,3,2,1,0:T(8,128)S(1)} %slice.32), channel_id=1, source_target_pairs={{0,1},{1,0},{2,3},{3,2},{4,5},{5,4},{6,7},{7,6},{8,9},{9,8},{10,11... | collective-permute-start | bytes 4718600 | tf_op jit(solution)/shard_map/ppermute | solution.py:36
  81.1 3.9 %collective-permute-start.4 = (f32[64,128]{1,0:T(8,128)S(1)}, f32[64,128]{1,0:T(8,128)S(1)}, u32[]{:S(2)}, u32[]{:S(2)}) collective-permute-start(f32[64,128]{1,0:T(8,128)S(1)} %get-tuple-element.24), channel_id=1, source_target_pairs={{0,32},{1,33},{2,34},{3,35},{4,36},{5,37},{6,38},{7,39},{8,40},{9,... | collective-permute-start | bytes 98312 | tf_op jit(solution)/shard_map/ppermute | solution.py:36
  85.0 4.2 %collective-permute-start.5 = (f32[64,128]{1,0:T(8,128)S(1)}, f32[64,128]{1,0:T(8,128)S(1)}, u32[]{:S(2)}, u32[]{:S(2)}) collective-permute-start(f32[64,128]{1,0:T(8,128)S(1)} %add.76), channel_id=1, source_target_pairs={{0,2},{1,3},{2,0},{3,1},{4,6},{5,7},{6,4},{7,5},{8,10},{9,11},{10,... | collective-permute-start | bytes 98312 | tf_op jit(solution)/shard_map/ppermute | solution.py:36
  89.5 21.1 %collective-permute-start.12 = (f32[32,24,128]{2,1,0:T(8,128)S(1)}, f32[32,24,128]{2,1,0:T(8,128)S(1)}, u32[]{:S(2)}, u32[]{:S(2)}) collective-permute-start(f32[32,24,128]{2,1,0:T(8,128)S(1)} %get-tuple-element.39), channel_id=1, source_target_pairs={{0,2},{1,3},{2,0},{3,1},{4,6},{5,7},{6,4},{7,5},{8,10},{9,11},{10,... | collective-permute-start | bytes 1179656 | tf_op jit(solution)/shard_map/ppermute | solution.py:36
  90.1 20.5 %collective-permute-start.13 = (f32[32,24,128]{2,1,0:T(8,128)S(1)}, f32[32,24,128]{2,1,0:T(8,128)S(1)}, u32[]{:S(2)}, u32[]{:S(2)}) collective-permute-start(f32[32,24,128]{2,1,0:T(8,128)S(1)} %get-tuple-element.38), channel_id=1, source_target_pairs={{0,32},{1,33},{2,34},{3,35},{4,36},{5,37},{6,38},{7,39},{8,40},{9,... | collective-permute-start | bytes 1179656 | tf_op jit(solution)/shard_map/ppermute | solution.py:36
  90.1 1.2 collective-permute-start.6
  91.3 5.4 %collective-permute-start.7 = (f32[64,128]{1,0:T(8,128)S(1)}, f32[64,128]{1,0:T(8,128)S(1)}, u32[]{:S(2)}, u32[]{:S(2)}) collective-permute-start(f32[64,128]{1,0:T(8,128)S(1)} %add.78), channel_id=1, source_target_pairs={{0,96},{1,97},{2,98},{3,99},{4,100},{5,101},{6,102},{7,103},{8,104... | collective-permute-start | bytes 98312 | tf_op jit(solution)/shard_map/ppermute | solution.py:36
  96.7 5.1 %collective-permute-start.8 = (f32[64,128]{1,0:T(8,128)S(1)}, f32[64,128]{1,0:T(8,128)S(1)}, u32[]{:S(2)}, u32[]{:S(2)}) collective-permute-start(f32[64,128]{1,0:T(8,128)S(1)} %add.79), channel_id=1, source_target_pairs={{0,6},{1,7},{2,4},{3,5},{4,2},{5,3},{6,0},{7,1},{8,14},{9,15},{10,... | collective-permute-start | bytes 98312 | tf_op jit(solution)/shard_map/ppermute | solution.py:36
  101.9 4.8 %collective-permute-start.9 = (f32[64,128]{1,0:T(8,128)S(1)}, f32[64,128]{1,0:T(8,128)S(1)}, u32[]{:S(2)}, u32[]{:S(2)}) collective-permute-start(f32[64,128]{1,0:T(8,128)S(1)} %add.80), channel_id=1, source_target_pairs={{0,8},{1,9},{2,10},{3,11},{4,12},{5,13},{6,14},{7,15},{8,0},{9,1},... | collective-permute-start | bytes 98312 | tf_op jit(solution)/shard_map/ppermute | solution.py:36
  106.6 3.9 %collective-permute-start.10 = (f32[64,128]{1,0:T(8,128)S(1)}, f32[64,128]{1,0:T(8,128)S(1)}, u32[]{:S(2)}, u32[]{:S(2)}) collective-permute-start(f32[64,128]{1,0:T(8,128)S(1)} %add.81), channel_id=1, source_target_pairs={{0,24},{1,25},{2,26},{3,27},{4,28},{5,29},{6,30},{7,31},{8,16},{9,... | collective-permute-start | bytes 98312 | tf_op jit(solution)/shard_map/ppermute | solution.py:36
  228.6 11.6 %collective-permute-start.16 = (f32[64,128]{1,0:T(8,128)S(1)}, f32[64,128]{1,0:T(8,128)S(1)}, u32[]{:S(2)}, u32[]{:S(2)}) collective-permute-start(f32[64,128]{1,0:T(8,128)S(1)} %get-tuple-element.42), channel_id=1, source_target_pairs={{0,4},{4,8},{8,12},{12,16},{16,20},{20,24},{24,28},{28,32},{32,36}... | collective-permute-start | bytes 98312 | tf_op jit(solution)/shard_map/ppermute | solution.py:615
  230.5 15.2 %copy-start.2 = (f32[2,2,128,128]{3,2,1,0:T(8,128)S(1)}, f32[2,2,128,128]{3,2,1,0:T(8,128)}, u32[]{:S(2)}) copy-start(f32[2,2,128,128]{3,2,1,0:T(8,128)} %get-tuple-element.34) | copy-start | bytes 786436
  230.5 9.6 %collective-permute-start.17 = (f32[64,128]{1,0:T(8,128)S(1)}, f32[64,128]{1,0:T(8,128)S(1)}, u32[]{:S(2)}, u32[]{:S(2)}) collective-permute-start(f32[64,128]{1,0:T(8,128)S(1)} %get-tuple-element.43), channel_id=1, source_target_pairs={{4,0},{8,4},{12,8},{16,12},{20,16},{24,20},{28,24},{32,28},{36,32}... | collective-permute-start | bytes 98312 | tf_op jit(solution)/shard_map/ppermute | solution.py:616
  240.2 5.2 %collective-permute-start.18 = (f32[448,128]{1,0:T(8,128)S(1)}, f32[448,128]{1,0:T(8,128)S(1)}, u32[]{:S(2)}, u32[]{:S(2)}) collective-permute-start(f32[448,128]{1,0:T(8,128)S(1)} %pad_maximum_fusion), channel_id=1, source_target_pairs={{0,1},{1,0},{2,3},{3,2},{4,5},{5,4},{6,7},{7,6},{8,9},{9,8},{10,11... | collective-permute-start | bytes 688136 | tf_op jit(solution)/shard_map/ppermute | solution.py:36
  240.3 1.5 collective-permute-start.14
  241.8 3.7 %collective-permute-start.15 = (f32[2,8,128]{2,1,0:T(8,128)S(1)}, f32[2,8,128]{2,1,0:T(8,128)S(1)}, u32[]{:S(2)}, u32[]{:S(2)}) collective-permute-start(f32[2,8,128]{2,1,0:T(8,128)S(1)} %add.86), channel_id=1, source_target_pairs={{0,2},{1,3},{2,0},{3,1},{4,6},{5,7},{6,4},{7,5},{8,10},{9,11},{10,... | collective-permute-start | bytes 24584 | tf_op jit(solution)/shard_map/ppermute | solution.py:36
  245.4 6.6 %collective-permute-start.19 = (f32[448,128]{1,0:T(8,128)S(1)}, f32[448,128]{1,0:T(8,128)S(1)}, u32[]{:S(2)}, u32[]{:S(2)}) collective-permute-start(f32[448,128]{1,0:T(8,128)S(1)} %fusion.2), channel_id=1, source_target_pairs={{0,2},{1,3},{2,0},{3,1},{4,6},{5,7},{6,4},{7,5},{8,10},{9,11},{10,... | collective-permute-start | bytes 688136 | tf_op jit(solution)/shard_map/ppermute | solution.py:36
  (2 other events, 2.8 us)
Sparse Core Ops, SparseCore 0:
  12.2 90.1 all-gather.1

commit v6 on v5

--- a/solution.py
+++ b/solution.py
@@ -163,7 +163,7 @@
             pltpu.VMEM((SAMP, NPAIR * PAIRW), F32),
             pltpu.VMEM((3, 2, PAIRW, PAIRW), F32),
             pltpu.VMEM((2, TILES, PAIRW), F32),
-            pltpu.SemaphoreType.DMA((8,)),
+            pltpu.SemaphoreType.DMA((16,)),
             pltpu.SemaphoreType.DMA,
         ],
         compiler_params=pltpu.CompilerParams(vmem_limit_bytes=58 * MIB),

time: 262 us -> 263 us (level)
  no operation moved by 1% of the time
where the time goes in v6:
time: 263 us; the launch traced here: 262 us
  blocking collectives  111 us (42%)
  waiting for transfers between devices  60.3 us (23%)
  Pallas kernels  44.1 us (17%)
  starting transfers between devices  29 us (11%)
  between operations  14.3 us (5%)
  local copies, waits for them, and re-layouts  3.06 us (1%)
    all_to_all x1, blocking collectives, body(): arrived = lax.all_to_all(payload, 'pair', 0, 0)  111 us
    ppermute x18, waiting for transfers between devices, exchange(): return lax.ppermute(value, BOTH, pairs)  34.5 us
    all_to_all x1, waiting for transfers between devices, body(): mine = lax.all_to_all(copies, 'pair', 0, 0)  25.8 us
    pallas_call x1, Pallas kernels, step0(): pl.pallas_call(step0_kernel, in_specs=[smem] * 3 + [vmem] * 2 + [hbm] * 3...  12.1 us
    all_to_all x1, starting transfers between devices, body(): mine = lax.all_to_all(copies, 'pair', 0, 0)  11.1 us
    pallas_call x1, Pallas kernels, prepare(): pl.pallas_call(prepare_kernel, grid=(x.shape[1] // width,), in_specs=[pl....  9.91 us
    ppermute x18, starting transfers between devices, exchange(): return lax.ppermute(value, BOTH, pairs)  9.35 us
    ppermute x1, starting transfers between devices, body(): lax.ppermute(sums[0, :HALF], 'pair', [(k + 1, k) for k in range(NDEV - 1)])  6.64 us
  transfers between devices with their start and end apart: 22, of which 14 were waited for; matrix products, arithmetic and copies ran while one was open for 0% of the time, Pallas kernels for 12%

profile of v6, /device:TPU:2, one launch (start us, length us, event | category | flops | bytes accessed | tf_op | source)
XLA Modules:
  0.0 262.0 jit_solution(17868299514531384891)
XLA Ops:
  7.2 5.3 %norms.1 = (f32[32,128]{1,0:T(8,128)}, f32[32,128]{1,0:T(8,128)}, f32[128,128]{1,0:T(8,128)}, f32[64,128]{1,0:T(8,128)}, f32[2,2,128,128]{3,2,1,0:T(8,128)}) custom-call(f32[256,8192]{1,0:T(8,128)} %bitcast.28, f32[3,2,128,128]{3,2,1,0:T(8,128)} %rotations_ref.1), custom_call_target="tpu_custom_call" | custom-call | flops 8388608 | bytes 8388608 | tf_op jit(solution)/shard_map/norms/pallas_call | solution.py:151
  14.7 2.5 spread.1
  17.2 11.1 %all-to-all-start = ((f32[32,160,128]{2,1,0:T(8,128)}), f32[32,160,128]{2,1,0:T(8,128)S(1)}, u32[]{:S(2)}, u32[]{:S(2)}) async-start(f32[32,160,128]{2,1,0:T(8,128)} %spread.1), calls=%async_computation | async-start | bytes 5242880 | tf_op jit(solution)/shard_map/all_to_all | solution.py:598
  28.3 9.9 %prepare.1.halves_ref = bf16[128,2,64,256]{3,2,1,0:T(8,128)(2,1)} custom-call(f32[256,8192]{1,0:T(8,128)} %bitcast.29), custom_call_target="tpu_custom_call" | custom-call | flops 1048576 | bytes 131072 | tf_op jit(solution)/shard_map/prepare/pallas_call | solution.py:188
  38.2 25.8 %all-to-all-done.arrived_ref.mine_ref = f32[32,160,128]{2,1,0:T(8,128)S(1)} async-done(((f32[32,160,128]{2,1,0:T(8,128)}), f32[32,160,128]{2,1,0:T(8,128)S(1)}, u32[]{:S(2)}, u32[]{:S(2)}) %all-to-all-start) | async-done | bytes 2621472 | tf_op jit(solution)/shard_map/all_to_all | solution.py:598
  64.7 3.2 %collective-permute-done.1 = f32[32,128]{1,0:T(8,128)S(1)} collective-permute-done((f32[32,128]{1,0:T(8,128)S(1)}, f32[32,128]{1,0:T(8,128)S(1)}, u32[]{:S(2)}, u32[]{:S(2)}) %collective-permute-start.1) | collective-permute-done | bytes 16416 | tf_op jit(solution)/shard_map/ppermute | solution.py:36
  69.1 12.1 %step0.1 = (bf16[256,2,2,64,256]{4,3,2,1,0:T(8,128)(2,1)}, f32[4,2,32,24,128]{4,3,2,1,0:T(8,128)S(1)}, f32[64,128]{1,0:T(8,128)S(1)}) custom-call(s32[64]{0:T(128)S(1)} %pad_add_fusion.tab_ref, s32[128]{0:T(128)S(1)} %copy-done.1, s32[6]{0:T(128)S(1)} %stack.35.place_ref, f32[32,128]{1,0:T(8,128)S(1)} %add.75.normc_ref, ...), custom_call_target="tpu_custom_call" | custom-call | flops 1048576 | bytes 131072 | tf_op jit(solution)/shard_map/step0/pallas_call | solution.py:345
  81.5 3.9 %collective-permute-done.4 = f32[64,128]{1,0:T(8,128)S(1)} collective-permute-done((f32[64,128]{1,0:T(8,128)S(1)}, f32[64,128]{1,0:T(8,128)S(1)}, u32[]{:S(2)}, u32[]{:S(2)}) %collective-permute-start.4) | collective-permute-done | bytes 32800 | tf_op jit(solution)/shard_map/ppermute | solution.py:36
  86.0 3.6 %collective-permute-done.5 = f32[64,128]{1,0:T(8,128)S(1)} collective-permute-done((f32[64,128]{1,0:T(8,128)S(1)}, f32[64,128]{1,0:T(8,128)S(1)}, u32[]{:S(2)}, u32[]{:S(2)}) %collective-permute-start.5) | collective-permute-done | bytes 32800 | tf_op jit(solution)/shard_map/ppermute | solution.py:36
  92.9 4.3 %collective-permute-done.7 = f32[64,128]{1,0:T(8,128)S(1)} collective-permute-done((f32[64,128]{1,0:T(8,128)S(1)}, f32[64,128]{1,0:T(8,128)S(1)}, u32[]{:S(2)}, u32[]{:S(2)}) %collective-permute-start.7) | collective-permute-done | bytes 32800 | tf_op jit(solution)/shard_map/ppermute | solution.py:36
  97.2 1.9 collective-permute-start.8
  99.1 3.2 %collective-permute-done.8 = f32[64,128]{1,0:T(8,128)S(1)} collective-permute-done((f32[64,128]{1,0:T(8,128)S(1)}, f32[64,128]{1,0:T(8,128)S(1)}, u32[]{:S(2)}, u32[]{:S(2)}) %collective-permute-start.8) | collective-permute-done | bytes 32800 | tf_op jit(solution)/shard_map/ppermute | solution.py:36
  102.3 2.9 %collective-permute-start.9 = (f32[64,128]{1,0:T(8,128)S(1)}, f32[64,128]{1,0:T(8,128)S(1)}, u32[]{:S(2)}, u32[]{:S(2)}) collective-permute-start(f32[64,128]{1,0:T(8,128)S(1)} %add.80), channel_id=1, source_target_pairs={{0,8},{1,9},{2,10},{3,11},{4,12},{5,13},{6,14},{7,15},{8,0},{9,1},... | collective-permute-start | bytes 98312 | tf_op jit(solution)/shard_map/ppermute | solution.py:36
  107.7 3.3 %collective-permute-done.10 = f32[64,128]{1,0:T(8,128)S(1)} collective-permute-done((f32[64,128]{1,0:T(8,128)S(1)}, f32[64,128]{1,0:T(8,128)S(1)}, u32[]{:S(2)}, u32[]{:S(2)}) %collective-permute-start.10) | collective-permute-done | bytes 32800 | tf_op jit(solution)/shard_map/ppermute | solution.py:36
  111.2 2.2 copy-done
  113.3 4.6 %step1.1 = f32[32,280,256]{2,1,0:T(8,128)S(1)} custom-call(f32[64,128]{1,0:T(8,128)S(1)} %add.82.norm_ref, bf16[256,2,2,64,256]{4,3,2,1,0:T(8,128)(2,1)} %get-tuple-element.25.operand_ref, f32[64,128,128]{2,1,0:T(8,128)S(1)} %bitcast.25, f32[32,24,128]{2,1,0:T(8,128)S(1)} %get-tuple-element.37.parta_ref, f32[32,24,128]{2,1,0:T(8,128)S(1)} %get-tuple-element.36.partb_ref), custom_call_target="tpu_custom_call" | custom-call | flops 3221225472 | bytes 25165824 | tf_op jit(solution)/shard_map/step1/pallas_call | solution.py:404
  117.9 110.8 %all_to_all.10.y_ref = f32[32,280,256]{2,1,0:T(8,128)S(1)} all-to-all(f32[32,280,256]{2,1,0:T(8,128)S(1)} %step1.1), channel_id=1, replica_groups=mesh['pair'=32,'row'=4] {'pair'}, dimensions={0} | all-to-all | bytes 18350080 | tf_op jit(solution)/shard_map/all_to_all | solution.py:612
  229.4 1.9 collective-permute-start.16
  231.3 6.6 %collective-permute-start.17 = (f32[64,128]{1,0:T(8,128)S(1)}, f32[64,128]{1,0:T(8,128)S(1)}, u32[]{:S(2)}, u32[]{:S(2)}) collective-permute-start(f32[64,128]{1,0:T(8,128)S(1)} %get-tuple-element.43), channel_id=1, source_target_pairs={{4,0},{8,4},{12,8},{16,12},{20,16},{24,20},{28,24},{32,28},{36,32}... | collective-permute-start | bytes 98312 | tf_op jit(solution)/shard_map/ppermute | solution.py:616
  238.0 3.0 %gram2.1 = (f32[2,8,128]{2,1,0:T(8,128)S(1)}, f32[128,128]{1,0:T(8,128)S(1)}) custom-call(f32[32,280,256]{2,1,0:T(8,128)S(1)} %all_to_all.10.y_ref), custom_call_target="tpu_custom_call" | custom-call | flops 2147483648 | bytes 10485760 | tf_op jit(solution)/shard_map/gram2/pallas_call | solution.py:471
  242.6 3.6 %collective-permute-done.15 = f32[2,8,128]{2,1,0:T(8,128)S(1)} collective-permute-done((f32[2,8,128]{2,1,0:T(8,128)S(1)}, f32[2,8,128]{2,1,0:T(8,128)S(1)}, u32[]{:S(2)}, u32[]{:S(2)}) %collective-permute-start.15) | collective-permute-done | bytes 8224 | tf_op jit(solution)/shard_map/ppermute | solution.py:36
  246.4 3.8 %step2.1 = f32[256,8192]{1,0:T(8,128)} custom-call(f32[2,8,128]{2,1,0:T(8,128)S(1)} %add.87.norm_ref.norm2_ref, f32[2,128,128]{2,1,0:T(8,128)S(1)} %get-tuple-element.41.rot_ref.rot2_ref, f32[32,280,256]{2,1,0:T(8,128)S(1)} %all_to_all.10.y_ref), custom_call_target="tpu_custom_call" | custom-call | flops 2147483648 | bytes 18874368 | tf_op jit(solution)/shard_map/step2/pallas_call | solution.py:500
  250.2 2.7 %collective-permute-done.19 = f32[448,128]{1,0:T(8,128)S(1)} collective-permute-done((f32[448,128]{1,0:T(8,128)S(1)}, f32[448,128]{1,0:T(8,128)S(1)}, u32[]{:S(2)}, u32[]{:S(2)}) %collective-permute-start.19) | collective-permute-done | bytes 229408 | tf_op jit(solution)/shard_map/ppermute | solution.py:36
  252.9 2.3 grams.1
  (62 shorter events, 13.1 us)
Async XLA Ops:
  7.2 104.0 %all-gather.2.cloned.1.call-start = ((), (), s32[]{:S(2)}) async-start(), calls=%async_computation.2 | async-start | bytes 4227072 | tf_op jit(solution)/shard_map/all_gather | solution.py:596
  12.6 1.5 collective-permute-start
  17.2 46.8 %all-to-all-start = ((f32[32,160,128]{2,1,0:T(8,128)}), f32[32,160,128]{2,1,0:T(8,128)S(1)}, u32[]{:S(2)}, u32[]{:S(2)}) async-start(f32[32,160,128]{2,1,0:T(8,128)} %spread.1), calls=%async_computation | async-start | bytes 5242880 | tf_op jit(solution)/shard_map/all_to_all | solution.py:598
  38.2 30.9 %copy-start.1 = (s32[128]{0:T(128)S(1)}, s32[128]{0:T(128)}, u32[]{:S(2)}) copy-start(s32[128]{0:T(128)} %order_ref.1) | copy-start | bytes 1540
  64.0 5.1 %collective-permute-start.3 = (f32[32,160,128]{2,1,0:T(8,128)S(1)}, f32[32,160,128]{2,1,0:T(8,128)}, u32[]{:S(2)}, u32[]{:S(2)}) collective-permute-start(f32[32,160,128]{2,1,0:T(8,128)S(1)} %all-to-all-done.arrived_ref.mine_ref), channel_id=1, source_target_pairs={{0,1},{1,0},{2,3},{3,2},{4,5},{5,4},{6,7},{7,6},{8,9},{9,8},{10,11... | collective-permute-start | bytes 7864328 | tf_op jit(solution)/shard_map/ppermute | solution.py:36
  64.1 3.8 %collective-permute-start.1 = (f32[32,128]{1,0:T(8,128)S(1)}, f32[32,128]{1,0:T(8,128)S(1)}, u32[]{:S(2)}, u32[]{:S(2)}) collective-permute-start(f32[32,128]{1,0:T(8,128)S(1)} %collect.1), channel_id=1, source_target_pairs={{0,2},{1,3},{2,0},{3,1},{4,6},{5,7},{6,4},{7,5},{8,10},{9,11},{10,... | collective-permute-start | bytes 49160 | tf_op jit(solution)/shard_map/ppermute | solution.py:36
  67.9 1.2 collective-permute-start.2
  81.3 8.4 %collective-permute-start.11 = (f32[2,2,32,24,128]{4,3,2,1,0:T(8,128)S(1)}, f32[2,2,32,24,128]{4,3,2,1,0:T(8,128)S(1)}, u32[]{:S(2)}, u32[]{:S(2)}) collective-permute-start(f32[2,2,32,24,128]{4,3,2,1,0:T(8,128)S(1)} %slice.32), channel_id=1, source_target_pairs={{0,1},{1,0},{2,3},{3,2},{4,5},{5,4},{6,7},{7,6},{8,9},{9,8},{10,11... | collective-permute-start | bytes 4718600 | tf_op jit(solution)/shard_map/ppermute | solution.py:36
  81.5 3.9 %collective-permute-start.4 = (f32[64,128]{1,0:T(8,128)S(1)}, f32[64,128]{1,0:T(8,128)S(1)}, u32[]{:S(2)}, u32[]{:S(2)}) collective-permute-start(f32[64,128]{1,0:T(8,128)S(1)} %get-tuple-element.24), channel_id=1, source_target_pairs={{0,32},{1,33},{2,34},{3,35},{4,36},{5,37},{6,38},{7,39},{8,40},{9,... | collective-permute-start | bytes 98312 | tf_op jit(solution)/shard_map/ppermute | solution.py:36
  85.5 4.2 %collective-permute-start.5 = (f32[64,128]{1,0:T(8,128)S(1)}, f32[64,128]{1,0:T(8,128)S(1)}, u32[]{:S(2)}, u32[]{:S(2)}) collective-permute-start(f32[64,128]{1,0:T(8,128)S(1)} %add.76), channel_id=1, source_target_pairs={{0,2},{1,3},{2,0},{3,1},{4,6},{5,7},{6,4},{7,5},{8,10},{9,11},{10,... | collective-permute-start | bytes 98312 | tf_op jit(solution)/shard_map/ppermute | solution.py:36
  89.9 21.1 %collective-permute-start.12 = (f32[32,24,128]{2,1,0:T(8,128)S(1)}, f32[32,24,128]{2,1,0:T(8,128)S(1)}, u32[]{:S(2)}, u32[]{:S(2)}) collective-permute-start(f32[32,24,128]{2,1,0:T(8,128)S(1)} %get-tuple-element.39), channel_id=1, source_target_pairs={{0,2},{1,3},{2,0},{3,1},{4,6},{5,7},{6,4},{7,5},{8,10},{9,11},{10,... | collective-permute-start | bytes 1179656 | tf_op jit(solution)/shard_map/ppermute | solution.py:36
  90.6 20.5 %collective-permute-start.13 = (f32[32,24,128]{2,1,0:T(8,128)S(1)}, f32[32,24,128]{2,1,0:T(8,128)S(1)}, u32[]{:S(2)}, u32[]{:S(2)}) collective-permute-start(f32[32,24,128]{2,1,0:T(8,128)S(1)} %get-tuple-element.38), channel_id=1, source_target_pairs={{0,32},{1,33},{2,34},{3,35},{4,36},{5,37},{6,38},{7,39},{8,40},{9,... | collective-permute-start | bytes 1179656 | tf_op jit(solution)/shard_map/ppermute | solution.py:36
  90.6 1.2 collective-permute-start.6
  91.8 5.4 %collective-permute-start.7 = (f32[64,128]{1,0:T(8,128)S(1)}, f32[64,128]{1,0:T(8,128)S(1)}, u32[]{:S(2)}, u32[]{:S(2)}) collective-permute-start(f32[64,128]{1,0:T(8,128)S(1)} %add.78), channel_id=1, source_target_pairs={{0,96},{1,97},{2,98},{3,99},{4,100},{5,101},{6,102},{7,103},{8,104... | collective-permute-start | bytes 98312 | tf_op jit(solution)/shard_map/ppermute | solution.py:36
  97.2 5.1 %collective-permute-start.8 = (f32[64,128]{1,0:T(8,128)S(1)}, f32[64,128]{1,0:T(8,128)S(1)}, u32[]{:S(2)}, u32[]{:S(2)}) collective-permute-start(f32[64,128]{1,0:T(8,128)S(1)} %add.79), channel_id=1, source_target_pairs={{0,6},{1,7},{2,4},{3,5},{4,2},{5,3},{6,0},{7,1},{8,14},{9,15},{10,... | collective-permute-start | bytes 98312 | tf_op jit(solution)/shard_map/ppermute | solution.py:36
  102.3 4.8 %collective-permute-start.9 = (f32[64,128]{1,0:T(8,128)S(1)}, f32[64,128]{1,0:T(8,128)S(1)}, u32[]{:S(2)}, u32[]{:S(2)}) collective-permute-start(f32[64,128]{1,0:T(8,128)S(1)} %add.80), channel_id=1, source_target_pairs={{0,8},{1,9},{2,10},{3,11},{4,12},{5,13},{6,14},{7,15},{8,0},{9,1},... | collective-permute-start | bytes 98312 | tf_op jit(solution)/shard_map/ppermute | solution.py:36
  107.1 3.9 %collective-permute-start.10 = (f32[64,128]{1,0:T(8,128)S(1)}, f32[64,128]{1,0:T(8,128)S(1)}, u32[]{:S(2)}, u32[]{:S(2)}) collective-permute-start(f32[64,128]{1,0:T(8,128)S(1)} %add.81), channel_id=1, source_target_pairs={{0,24},{1,25},{2,26},{3,27},{4,28},{5,29},{6,30},{7,31},{8,16},{9,... | collective-permute-start | bytes 98312 | tf_op jit(solution)/shard_map/ppermute | solution.py:36
  229.4 11.6 %collective-permute-start.16 = (f32[64,128]{1,0:T(8,128)S(1)}, f32[64,128]{1,0:T(8,128)S(1)}, u32[]{:S(2)}, u32[]{:S(2)}) collective-permute-start(f32[64,128]{1,0:T(8,128)S(1)} %get-tuple-element.42), channel_id=1, source_target_pairs={{0,4},{4,8},{8,12},{12,16},{16,20},{20,24},{24,28},{28,32},{32,36}... | collective-permute-start | bytes 98312 | tf_op jit(solution)/shard_map/ppermute | solution.py:615
  231.3 15.1 %copy-start.2 = (f32[2,2,128,128]{3,2,1,0:T(8,128)S(1)}, f32[2,2,128,128]{3,2,1,0:T(8,128)}, u32[]{:S(2)}) copy-start(f32[2,2,128,128]{3,2,1,0:T(8,128)} %get-tuple-element.34) | copy-start | bytes 786436
  231.3 9.6 %collective-permute-start.17 = (f32[64,128]{1,0:T(8,128)S(1)}, f32[64,128]{1,0:T(8,128)S(1)}, u32[]{:S(2)}, u32[]{:S(2)}) collective-permute-start(f32[64,128]{1,0:T(8,128)S(1)} %get-tuple-element.43), channel_id=1, source_target_pairs={{4,0},{8,4},{12,8},{16,12},{20,16},{24,20},{28,24},{32,28},{36,32}... | collective-permute-start | bytes 98312 | tf_op jit(solution)/shard_map/ppermute | solution.py:616
  241.0 5.2 %collective-permute-start.18 = (f32[448,128]{1,0:T(8,128)S(1)}, f32[448,128]{1,0:T(8,128)S(1)}, u32[]{:S(2)}, u32[]{:S(2)}) collective-permute-start(f32[448,128]{1,0:T(8,128)S(1)} %pad_maximum_fusion), channel_id=1, source_target_pairs={{0,1},{1,0},{2,3},{3,2},{4,5},{5,4},{6,7},{7,6},{8,9},{9,8},{10,11... | collective-permute-start | bytes 688136 | tf_op jit(solution)/shard_map/ppermute | solution.py:36
  241.1 1.5 collective-permute-start.14
  242.6 3.7 %collective-permute-start.15 = (f32[2,8,128]{2,1,0:T(8,128)S(1)}, f32[2,8,128]{2,1,0:T(8,128)S(1)}, u32[]{:S(2)}, u32[]{:S(2)}) collective-permute-start(f32[2,8,128]{2,1,0:T(8,128)S(1)} %add.86), channel_id=1, source_target_pairs={{0,2},{1,3},{2,0},{3,1},{4,6},{5,7},{6,4},{7,5},{8,10},{9,11},{10,... | collective-permute-start | bytes 24584 | tf_op jit(solution)/shard_map/ppermute | solution.py:36
  246.3 6.6 %collective-permute-start.19 = (f32[448,128]{1,0:T(8,128)S(1)}, f32[448,128]{1,0:T(8,128)S(1)}, u32[]{:S(2)}, u32[]{:S(2)}) collective-permute-start(f32[448,128]{1,0:T(8,128)S(1)} %fusion.2), channel_id=1, source_target_pairs={{0,2},{1,3},{2,0},{3,1},{4,6},{5,7},{6,4},{7,5},{8,10},{9,11},{10,... | collective-permute-start | bytes 688136 | tf_op jit(solution)/shard_map/ppermute | solution.py:36
  (2 other events, 2.8 us)
Sparse Core Ops, SparseCore 0:
  12.7 90.1 all-gather.1
